TPU v7x, 32 devices: a whole 2x2x4 slice. The times are simulated.
32 devices in a mesh: expert: 16 (over z, y, core), tensor: 2 (over x).
Axes of the slice: x: 2, y: 2, z: 4, core: 2. Of those that a mesh axis runs over, the one named last changes fastest.
Arguments:
- tokens: bfloat16 [25216, 512], P('expert'), may hold values from -6 to 6
- routes: int32 [25216, 2], P('expert'), may hold values from 0 to 15, all different within a row
- gain_attn: float32 [512], replicated, may hold values from 0.5 to 1.5
- w_qkv: bfloat16 [3, 512, 512], P(None, None, 'tensor'), may hold values from -0.25 to 0.25
- w_attn_out: bfloat16 [512, 512], P('tensor'), may hold values from -1.5 to 1.5
- gain_moe: float32 [512], replicated, may hold values from 0.5 to 1.5
- w_router: bfloat16 [512, 16], replicated, may hold values from -0.25 to 0.25
- w_expert_in: bfloat16 [16, 512, 2048], P('expert', None, 'tensor'), may hold values from -0.25 to 0.25
- w_expert_out: bfloat16 [16, 2048, 512], P('expert', 'tensor'), may hold values from -1.75 to 1.75
- cotangent: bfloat16 [25216, 512], P('expert'), may hold values from -6 to 6
Outputs:
- result: bfloat16 [25216, 512], P('expert')
- grad_tokens: float32 [25216, 512], P('expert')
- grad_gain_attn: float32 [512], replicated
- grad_w_qkv: float32 [3, 512, 512], P(None, None, 'tensor')
- grad_w_attn_out: float32 [512, 512], P('tensor')
- grad_gain_moe: float32 [512], replicated
- grad_w_router: float32 [512, 16], replicated
- grad_w_expert_in: float32 [16, 512, 2048], P('expert', None, 'tensor')
- grad_w_expert_out: float32 [16, 2048, 512], P('expert', 'tensor')
Inputs may be any that keep to these rules, and one draw needn't show every extreme that they name: `routes`: each token names two different experts.
All inputs are finite; a program needn't handle non-finite values.
Results may differ from a plain program's by a relative error of at most 0.025.
Values may be sent and summed in bfloat16 or wider, within the bound.
No kernel may reach another device: no remote copies, remote signals or barrier semaphores. Data moves between devices by JAX's collectives and lax.ppermute only.
A program may use at most 192 MiB of HBM per device.

v0:
```python
import functools

import jax
import jax.numpy as jnp
from jax import lax
from jax.experimental import pallas as pl
from jax.experimental.pallas import tpu as pltpu
from jax.sharding import PartitionSpec as P

HEAD_DIM = 64
SEQ = 197
PAD = 208
EPS = 1e-06
F32 = jnp.float32
BF16 = jnp.bfloat16
VMEM = pl.BlockSpec(memory_space=pltpu.VMEM)


def nn(a, b):
    return lax.dot_general(a, b, (((1,), (0,)), ((), ())), preferred_element_type=F32)


def nt(a, b):
    return lax.dot_general(a, b, (((1,), (1,)), ((), ())), preferred_element_type=F32)


def tn(a, b):
    return lax.dot_general(a, b, (((0,), (0,)), ((), ())), preferred_element_type=F32)


def params(mib=56):
    return pltpu.CompilerParams(vmem_limit_bytes=mib << 20)


def cost(us):
    return pl.CostEstimate(flops=0, bytes_accessed=int(us * 3.69e6), transcendentals=0)


def full(shape):
    return pl.BlockSpec(shape, lambda *_: (0,) * len(shape))


def pad_images(source, wide, target):
    wide[0 : source.shape[0], :] = source[...].astype(F32)

    def one_image(i, _):
        off = lax.rem(i * SEQ, 8)
        window = wide[pl.ds(pl.multiple_of(i * SEQ - off, 8), PAD + 8), :]
        window = pltpu.roll(window, lax.rem(PAD + 8 - off, PAD + 8), 0)[:PAD]
        target[i] = jnp.where(iota(window.shape, 0) < SEQ, window, 0.0).astype(BF16)
        return 0

    lax.fori_loop(0, target.shape[0], one_image, 0)


def pad_kernel(source, target, wide):
    pad_images(source, wide, target)


def wide_scratch(images, width):
    return pltpu.VMEM((-(-((images - 1) * SEQ + PAD + 8) // 16) * 16, width), F32)


def pad(rows):
    images, width = rows.shape[0] // SEQ, rows.shape[1]
    return pl.pallas_call(
        pad_kernel,
        out_shape=jax.ShapeDtypeStruct((images, PAD, width), BF16),
        in_specs=[VMEM],
        out_specs=VMEM,
        scratch_shapes=[wide_scratch(images, width)],
        compiler_params=params(),
        cost_estimate=cost(2),
        name="pad",
    )(rows)


def iota(shape, axis):
    return lax.broadcasted_iota(jnp.int32, shape, axis)


def slot_match(code_ref, start, step):
    slot = iota((step, code_ref.shape[1]), 0) + start
    return ((slot == code_ref[0:1, :]) | (slot == code_ref[1:2, :])).astype(BF16)


def front_kernel(rank_ref, cot_ref, col_ref, row_ref, cot_out, slots_out, col_out, row_out, wide, *, cap, half):
    experts, chunks, block, _ = slots_out.shape
    first_slot = rank_ref[0] * (half * chunks)

    def code(expert, position):
        place = position.astype(jnp.int32) - first_slot
        good = (expert >= 0) & (position < cap) & (place >= 0) & (place < half * chunks)
        slot = expert * block + place
        for c in range(1, chunks):
            slot = jnp.where(place >= c * half, slot + (experts * block - half), slot)
        return jnp.where(good, slot, -1)

    lanes = col_ref.shape[1]
    span = lanes * experts
    routes = col_ref[...]
    spread_lanes = (iota((lanes, span), 1) // experts == iota((lanes, span), 0)).astype(BF16)
    gather_lanes = (iota((span, lanes), 0) // experts == iota((span, lanes), 1)).astype(BF16)
    chosen = nn(routes.astype(F32).astype(BF16), spread_lanes) == (iota((PAD, span), 1) % experts).astype(F32)
    ones = chosen.astype(F32)
    lower = (iota((PAD, PAD), 0) > iota((PAD, PAD), 1)).astype(BF16)
    before = nn(lower, ones.astype(BF16))
    totals = jnp.broadcast_to(jnp.sum(ones, axis=0, keepdims=True), (16, span)).astype(BF16)
    source, target = iota((span, span), 0), iota((span, span), 1)
    order_s = (source // experts % 2) * lanes + source // (2 * experts)
    order_t = (target // experts % 2) * lanes + target // (2 * experts)
    earlier = (source % experts == target % experts) & (order_s < order_t)
    before = before + nn(totals, earlier.astype(BF16))[0:1]
    place = nn((jnp.minimum(before, float(cap)) * ones).astype(BF16), gather_lanes)
    col_out[...] = code(routes, place)

    step = 128
    blocks = row_ref.shape[1] // step
    upper = (iota((step, step), 0) < iota((step, step), 1)).astype(BF16)
    order = [(choice, b) for choice in range(2) for b in range(blocks)]
    picked = [row_ref[choice : choice + 1, b * step : (b + 1) * step] for choice, b in order]
    ones = [(p == iota((experts, step), 0)).astype(F32) for p in picked]
    before = nn(jnp.concatenate(ones, axis=0).astype(BF16), upper)
    base = jnp.zeros((experts, 1), F32)
    for k, (choice, b) in enumerate(order):
        position = jnp.sum((before[k * experts : (k + 1) * experts] + base) * ones[k], axis=0, keepdims=True)
        row_out[choice : choice + 1, b * step : (b + 1) * step] = code(picked[k], position)
        base = base + jnp.sum(ones[k], axis=1, keepdims=True)

    pad_images(cot_ref, wide, cot_out)
    rows = cot_out[...].reshape(-1, cot_out.shape[2])
    step = min(512, experts * block)
    per = step // block
    blocks = experts // per

    def some_slots(k, _):
        value = nn(slot_match(row_out, k * step, step), rows).astype(BF16)
        slots_out[pl.ds(lax.rem(k, blocks) * per, per), lax.div(k, blocks)] = value.reshape(per, block, -1)
        return 0

    lax.fori_loop(0, chunks * blocks, some_slots, 0)


def front(rank, cotangent, routes, experts, cap, half, block, chunks):
    rows, width = cotangent.shape
    images = rows // SEQ
    padded = jnp.pad(
        routes.reshape(images, SEQ, 2), ((0, 0), (0, PAD - SEQ), (0, 0)), constant_values=-1
    )
    down = padded.transpose(1, 0, 2).reshape(PAD, images * 2)
    across = padded.reshape(images * PAD, 2).T
    return pl.pallas_call(
        functools.partial(front_kernel, cap=cap, half=half),
        out_shape=(
            jax.ShapeDtypeStruct((images, PAD, width), BF16),
            jax.ShapeDtypeStruct((experts, chunks, block, width), BF16),
            jax.ShapeDtypeStruct(down.shape, jnp.int32),
            jax.ShapeDtypeStruct(across.shape, jnp.int32),
        ),
        in_specs=[pl.BlockSpec(memory_space=pltpu.SMEM)] + [VMEM] * 3,
        out_specs=(VMEM,) * 4,
        scratch_shapes=[wide_scratch(images, width)],
        compiler_params=params(),
        cost_estimate=cost(10),
        name="front",
    )(rank, cotangent, down, across)


def spread_kernel(code_ref, rows_ref, *outs, step, steps):
    number = pl.program_id(0)
    value = nn(slot_match(code_ref, number * step, step), rows_ref[...]).astype(BF16)
    for c, out_ref in enumerate(outs):

        @pl.when(lax.div(number, steps) == c)
        def _():
            out_ref[...] = value.reshape(out_ref.shape)


def spread(code_row, rows, experts, block, chunks, step=512):
    count, width = rows.shape
    step = min(step, experts * block)
    per, steps = step // block, experts * block // step

    def place(c):
        return lambda i: (jnp.clip(i - c * steps, 0, steps - 1), 0, 0)

    return pl.pallas_call(
        functools.partial(spread_kernel, step=step, steps=steps),
        out_shape=(jax.ShapeDtypeStruct((experts, block, width), BF16),) * chunks,
        grid=(chunks * steps,),
        in_specs=[full((2, count)), full((count, width))],
        out_specs=tuple(pl.BlockSpec((per, block, width), place(c)) for c in range(chunks)),
        compiler_params=params(),
        cost_estimate=cost(9),
        name="spread",
    )(code_row, rows)


def row_mean(v):
    return jnp.mean(v, axis=-1, keepdims=True)


def key_softmax(scores):
    cut = SEQ // 16 * 16
    head, tail = scores[:cut], scores[cut:]
    valid = lax.broadcasted_iota(jnp.int32, tail.shape, 0) < SEQ - cut
    tail = jnp.where(valid, tail, -jnp.inf)
    top = jnp.maximum(jnp.max(head, axis=0, keepdims=True), jnp.max(tail, axis=0, keepdims=True))
    head, tail = jnp.exp(head - top), jnp.exp(tail - top)
    total = jnp.sum(head, axis=0, keepdims=True) + jnp.sum(tail, axis=0, keepdims=True)
    scale = 1.0 / total
    return jnp.concatenate([head * scale, tail * scale], axis=0)


QUAD = 4 * HEAD_DIM


def quad_masks():
    lane = iota((PAD, QUAD), 1)
    return [(lane >= h * HEAD_DIM) & (lane < (h + 1) * HEAD_DIM) for h in range(4)]


def stacked(value, masks):
    return jnp.concatenate([jnp.where(m, value, jnp.zeros_like(value)) for m in masks], axis=0)


def unstacked(value, masks):
    return sum(jnp.where(m, value[h * PAD : (h + 1) * PAD], 0.0) for h, m in enumerate(masks))


def attend_kernel(place_ref, tok_ref, ga_ref, gm_ref, *rest, pieces, own):
    wq, wo, rest = rest[:pieces], rest[pieces : 2 * pieces], rest[2 * pieces :]
    routed_ref, res_ref, qkv_ref, prob_ref, att_ref, wq_all, wo_all, qkv_all, att_all = rest
    batch, _, model = tok_ref.shape
    keep = pl.program_id(0) * batch < own

    @pl.when(pl.program_id(0) == 0)
    def _():
        at = 0
        size = wo[0].shape[0]
        if pieces == 1:
            places = [0]
        else:
            core, small = place_ref[1], wo[1].shape[0]
            places = [0, size + core * small, size + (1 - core) * small]
        for k, start in enumerate(places):
            cols = wo[k].shape[0]
            for j in range(3):
                to = start + j * model
                if k:
                    to = pl.multiple_of(to, 128)
                wq_all[:, pl.ds(to, cols)] = wq[k][j]
            if k:
                start = pl.multiple_of(start, 128)
            wo_all[pl.ds(start, cols), :] = wo[k][...]

    tok = tok_ref[...].reshape(batch * PAD, model).astype(F32)
    center = tok - row_mean(tok)
    normed = (center * lax.rsqrt(row_mean(center * center) + EPS) * ga_ref[...]).astype(BF16)
    value = nn(normed, wq_all[...])
    qkv_all[:, :model] = (value[:, :model] * HEAD_DIM**-0.5).astype(BF16)
    qkv_all[:, model:] = value[:, model:].astype(BF16)
    masks = quad_masks()
    key_ok = iota((4 * PAD, PAD), 1) < SEQ
    for g in range(batch):
        rows = slice(g * PAD, (g + 1) * PAD)
        for quad in range(model // QUAD):
            q, k, v = (qkv_all[rows, j * model + quad * QUAD : j * model + (quad + 1) * QUAD] for j in range(3))
            scores = jnp.where(key_ok, nt(stacked(q, masks), k), -jnp.inf)
            ex = jnp.exp(scores - jnp.max(scores, axis=1, keepdims=True))
            probs = (ex * (1.0 / jnp.sum(ex, axis=1, keepdims=True))).astype(BF16)

            @pl.when(keep)
            def _():
                prob_ref[g, quad] = probs

            mixed = unstacked(nn(probs, v), masks)
            att_all[rows, quad * QUAD : (quad + 1) * QUAD] = mixed.astype(BF16)

    residual = tok + nn(att_all[...], wo_all[...])

    @pl.when(keep)
    def _():
        res_ref[...] = residual.reshape(batch, PAD, model)
        qkv_ref[...] = qkv_all[...].reshape(batch, PAD, 3 * model)
        att_ref[...] = att_all[...].reshape(batch, PAD, model)

    center = residual - row_mean(residual)
    normed = center * lax.rsqrt(row_mean(center * center) + EPS) * gm_ref[...]
    routed_ref[...] = normed.astype(BF16).reshape(batch, PAD, model)


def attend(place, tok_pad, gain_attn, gain_moe, wq, wo, own, batch=2):
    images, _, width = tok_pad.shape
    batch = batch if own % batch == 0 else 1
    pieces = len(wq)
    steps = images // batch

    def image(i, place_ref):
        return (lax.rem(i + place_ref[0] // batch, steps), 0, 0)

    def kept(*shape):
        return pl.BlockSpec(
            (batch,) + shape, lambda i, place_ref: (jnp.minimum(i, own // batch - 1),) + (0,) * len(shape)
        )

    rows = pl.BlockSpec((batch, PAD, width), image)
    probs = (width // QUAD, 4 * PAD, PAD)
    return pl.pallas_call(
        functools.partial(attend_kernel, pieces=pieces, own=own),
        out_shape=(
            jax.ShapeDtypeStruct((images, PAD, width), BF16),
            jax.ShapeDtypeStruct((own, PAD, width), F32),
            jax.ShapeDtypeStruct((own, PAD, 3 * width), BF16),
            jax.ShapeDtypeStruct((own,) + probs, BF16),
            jax.ShapeDtypeStruct((own, PAD, width), BF16),
            jax.ShapeDtypeStruct((width, 3 * width), BF16),
            jax.ShapeDtypeStruct((width, width), BF16),
        ),
        grid_spec=pltpu.PrefetchScalarGridSpec(
            num_scalar_prefetch=1,
            grid=(steps,),
            in_specs=[rows, full((1, width)), full((1, width))] + [full(v.shape) for v in (*wq, *wo)],
            out_specs=(
                rows,
                kept(PAD, width),
                kept(PAD, 3 * width),
                kept(*probs),
                kept(PAD, width),
                full((width, 3 * width)),
                full((width, width)),
            ),
            scratch_shapes=[
                pltpu.VMEM((batch * PAD, 3 * width), BF16),
                pltpu.VMEM((batch * PAD, width), BF16),
            ],
        ),
        compiler_params=params(),
        cost_estimate=cost(25),
        name="attend",
    )(place, tok_pad, gain_attn.reshape(1, -1), gain_moe.reshape(1, -1), *wq, *wo)


def expert_kernel(expert_ref, x_ref, cot_ref, wr_ref, *rest, parts, half, block, chunk, begins, ends):
    weights, rest = rest[: len(parts)], rest[len(parts) :]
    w1, w2, dw1, dw2, out_sum, gin_sum, low1, low2, load_sems, store_sems = rest[-10:]
    shards, _, hidden = w1.shape
    before, rest = ((), rest) if begins else (rest[: 2 * shards], rest[2 * shards + 1 :])
    gin_ref, out_ref = rest[:2]
    given = rest[2 : 2 + 2 * shards]
    expert = expert_ref[0]
    size = min(chunk, hidden)
    blocks = hidden // size

    loads = [(s, ref, (w1, w2)[k].at[s, pl.ds(at, ref.shape[0])]) for (k, s, at), ref in zip(parts, weights)]
    loads += [(k % shards, ref, (dw1, dw2)[k // shards].at[k % shards]) for k, ref in enumerate(before)]
    loads = [(s, pltpu.make_async_copy(a, b, load_sems.at[k])) for k, (s, a, b) in enumerate(loads)]
    for s in range(shards):
        for where, copy in loads:
            if where == s:
                copy.start()

    def stores(s, c):
        cols = pl.ds(pl.multiple_of(c * size, size), size)
        if ends and s:
            sources = low1.at[:, cols], low2.at[cols, :]
        else:
            sources = dw1.at[s, :, cols], dw2.at[s, cols, :]
        targets = given[s].at[:, cols], given[shards + s].at[cols, :]
        return [
            pltpu.make_async_copy(a, b, store_sems.at[(s * blocks + c) * 2 + k])
            for k, (a, b) in enumerate(zip(sources, targets))
        ]

    x = x_ref[...]
    rows, width = x.shape
    cot = cot_ref[...].reshape(rows, width).astype(F32)
    logits = nn(x, wr_ref[...])
    ex = jnp.exp(logits - jnp.max(logits, axis=1, keepdims=True))
    mine = iota(ex.shape, 1) == expert
    gate = jnp.sum(jnp.where(mine, ex, 0.0), axis=1, keepdims=True) / jnp.sum(
        ex, axis=1, keepdims=True
    )
    grad_out = (gate * cot).astype(BF16)
    x_t = x.T
    out_sum[...] = jnp.zeros_like(out_sum)
    gin_sum[...] = jnp.zeros_like(gin_sum)
    c0 = (2.0 / jnp.pi) ** 0.5

    def some_hidden(k, _):
        for s in range(shards):

            @pl.when(k == s * blocks)
            def _():
                for where, copy in loads:
                    if where == s:
                        copy.wait()

        shard, at = lax.div(k, blocks), lax.rem(k, blocks)
        cols = pl.ds(pl.multiple_of(at * size, size), size)
        u = nn(x, w1[shard, :, cols])
        square = u * u
        t = jnp.tanh(u * (c0 + (c0 * 0.044715) * square))
        h = 0.5 + 0.5 * t
        slope = h + (0.5 * u) * (1.0 - t * t) * (c0 + (3 * c0 * 0.044715) * square)
        active = (u * h).astype(BF16)
        out_sum[...] += nn(active, w2[shard, cols, :])
        grad_pre = (nt(grad_out, w2[shard, cols, :]) * slope).astype(BF16)
        gin_sum[...] += nt(grad_pre, w1[shard, :, cols])
        first, second = nn(x_t, grad_pre), tn(active, grad_out)
        dw1[shard, :, cols] = first if begins else dw1[shard, :, cols] + first
        dw2[shard, cols, :] = second if begins else dw2[shard, cols, :] + second
        for s in range(shards):

            @pl.when(shard == s)
            def _():
                if ends and s:
                    low1[:, cols] = dw1[shard, :, cols].astype(BF16)
                    low2[cols, :] = dw2[shard, cols, :].astype(BF16)
                for copy in stores(s, at):
                    copy.start()

        return 0

    lax.fori_loop(0, shards * blocks, some_hidden, 0)
    out, gin = out_sum[...], gin_sum[...]
    out_ref[...] = (gate * out).astype(BF16).reshape(out_ref.shape)
    gate_grad = jnp.sum(cot * out, axis=1, keepdims=True)
    down, across = iota((block, width), 0), iota((block, width), 1)
    for g in range(rows // block):
        span = slice(g * block, (g + 1) * block)
        line = jnp.sum(jnp.where(down == across, gate_grad[span], 0.0), axis=0, keepdims=True)
        high = line.astype(BF16).astype(F32)
        value = jnp.where(down == half, high, jnp.where(down == half + 1, line - high, gin[span]))
        gin_ref[span, :] = value.astype(BF16)
    for s in range(shards):
        for c in range(blocks):
            for copy in stores(s, c):
                copy.wait()


def experts_step(expert, x, cot, before, number, ends, w_router, w1, w2, half, block, chunk=512):
    rows, width = x.shape
    shards = len(w1)
    hidden = w1[0][0].shape[1]
    row_spec = full((rows, width))
    chunk_spec = pl.BlockSpec((rows // block, 1, block, width), lambda i, _: (0, number, 0, 0))
    anywhere = pl.BlockSpec(memory_space=pl.ANY)
    old = [] if before is None else [*before[1:], before[0]]
    parts, weights = [], []
    for k, shards_of_one in enumerate((w1, w2)):
        for s, pieces in enumerate(shards_of_one):
            at = 0
            for piece in pieces:
                parts.append((k, s, at))
                weights.append(piece)
                at += piece.shape[0]
    shapes = [(width, hidden)] * shards + [(hidden, width)] * shards
    low = (8, 128) if shards == 1 or not ends else None
    at = 4 + len(weights)
    alias = {at + 2 * shards: 1} if old else {}
    return pl.pallas_call(
        functools.partial(
            expert_kernel,
            parts=parts,
            half=half,
            block=block,
            chunk=chunk,
            begins=before is None,
            ends=ends,
        ),
        out_shape=(jax.ShapeDtypeStruct((rows, width), BF16), jax.ShapeDtypeStruct(cot.shape, BF16))
        + tuple(
            jax.ShapeDtypeStruct(v, BF16 if ends and k % shards else F32) for k, v in enumerate(shapes)
        ),
        grid_spec=pltpu.PrefetchScalarGridSpec(
            num_scalar_prefetch=1,
            grid=(1,),
            in_specs=[row_spec, chunk_spec, full(w_router.shape)] + [anywhere] * (len(weights) + len(old)),
            out_specs=(row_spec, chunk_spec) + (anywhere,) * len(shapes),
            scratch_shapes=[
                pltpu.VMEM((shards, width, hidden), BF16),
                pltpu.VMEM((shards, hidden, width), BF16),
                pltpu.VMEM((shards, width, hidden), F32),
                pltpu.VMEM((shards, hidden, width), F32),
                pltpu.VMEM((rows, width), F32),
                pltpu.VMEM((rows, width), F32),
                pltpu.VMEM(low or (width, hidden), BF16),
                pltpu.VMEM(low or (hidden, width), BF16),
                pltpu.SemaphoreType.DMA((len(weights) + 2 * shards,)),
                pltpu.SemaphoreType.DMA((2 * shards * hidden // min(chunk, hidden),)),
            ],
        ),
        input_output_aliases=alias,
        compiler_params=params(62),
        cost_estimate=cost(20),
        name="experts",
    )(expert, x, cot, w_router, *weights, *old)


def collect_kernel(first_ref, code_ref, *rest, numbers, half, block, probs, before):
    chunks = len(numbers)
    parts, rest = rest[:chunks], rest[chunks:]
    old, rest = rest[:before], rest[before:]
    out_ref, rest = rest[0], rest[1:]
    count, width = parts[0].shape
    experts = count // block
    rows = PAD
    codes = code_ref[...]
    across = iota(codes.shape, 1)
    at = (first_ref[0] + pl.program_id(0)) * 2
    columns = [jnp.sum(jnp.where(across == at + c, codes, 0), axis=1, keepdims=True) for c in range(2)]
    lane = iota((rows, count), 1)
    total = old[0][0] if old else None
    grads = None
    for c in range(chunks):
        shift = numbers[c] * count
        match = ((lane + shift == columns[0]) | (lane + shift == columns[1])).astype(BF16)
        value = nn(match, parts[c][...])
        total = value if total is None else total + value
        if probs:
            slot_grads = rest[1 + c]

            @pl.when(pl.program_id(0) == 0)
            def _():
                lines = jnp.zeros((experts, 128), F32)
                for e in range(experts):
                    tail = parts[c][e * block + block - 16 : (e + 1) * block, 0:128].astype(F32)
                    here = half - (block - 16)
                    line = tail[here : here + 1] + tail[here + 1 : here + 2]
                    lines = jnp.where(iota(lines.shape, 0) == e, line, lines)
                turned = lines.T[:block]
                high = turned.astype(BF16).astype(F32)
                both = jnp.concatenate([high, turned - high], axis=1)
                for e in range(experts):
                    own_lane = iota(both.shape, 1) % experts == e
                    slot_grads[e * block : (e + 1) * block, :] = jnp.where(own_lane, both, 0.0).astype(BF16)

            value = nn(match, slot_grads[...])
            grads = value if grads is None else grads + value
    out_ref[0] = total.astype(out_ref.dtype)
    if probs:
        turned = grads.T
        value = turned[:experts] + turned[experts:]
        rest[0][0] = value + old[1][0] if old else value


def collect(first, code_col, parts, own, dtype, half, block, probs=False, numbers=None, before=()):
    numbers = tuple(range(len(parts))) if numbers is None else numbers
    count, width = parts[0].shape
    outs = [jax.ShapeDtypeStruct((own, PAD, width), dtype)]
    if probs:
        outs.append(jax.ShapeDtypeStruct((own, count // block, PAD), F32))
    return pl.pallas_call(
        functools.partial(
            collect_kernel, numbers=numbers, half=half, block=block, probs=probs, before=len(before)
        ),
        out_shape=tuple(outs),
        grid_spec=pltpu.PrefetchScalarGridSpec(
            num_scalar_prefetch=1,
            grid=(own,),
            in_specs=[full(code_col.shape)]
            + [full((count, width))] * len(parts)
            + [pl.BlockSpec((1,) + v.shape[1:], lambda i, f: (i + f[0], 0, 0)) for v in before],
            out_specs=tuple(pl.BlockSpec((1,) + v.shape[1:], lambda i, f: (i, 0, 0)) for v in outs),
            scratch_shapes=[pltpu.VMEM((count, 2 * (count // block)), BF16)] * (len(parts) if probs else 0),
        ),
        compiler_params=params(),
        cost_estimate=cost(7),
        name="collect",
    )(first, code_col, *parts, *before)


def back_kernel(first_ref, *rest, steps, received):
    (sum_ref, gp_ref), rest = rest[:2], rest[2:]
    more, rest = rest[: 2 * received], rest[2 * received :]
    (res_ref, cot_ref, tok_ref, ga_ref, gm_ref, wrt_ref, wq, wo, qkv_ref, prob_ref, att_ref), rest = rest[:11], rest[11:]
    gtok_ref, pack_ref, dwq, dwo, small, gatt_all, dqkv_all = rest
    experts = wrt_ref.shape[0]
    batch, _, model = res_ref.shape
    rows = batch * PAD
    step = pl.program_id(0)

    @pl.when(step == 0)
    def _():
        for ref in (dwq, dwo, small):
            ref[...] = jnp.zeros_like(ref)

    def flat(ref):
        return ref[...].reshape(rows, -1).astype(F32)

    residual = flat(res_ref)
    center = residual - row_mean(residual)
    scale = lax.rsqrt(row_mean(center * center) + EPS)
    xhat = center * scale
    gm = gm_ref[...]
    routed = (xhat * gm).astype(BF16)
    logits = nt(wrt_ref[...], routed)
    ex = jnp.exp(logits - jnp.max(logits, axis=0, keepdims=True))
    probs = ex / jnp.sum(ex, axis=0, keepdims=True)
    grad_probs = gp_ref[...]
    grad_routed = flat(sum_ref)
    if received:
        grad_routed = grad_routed + flat(more[0])
        grad_probs = grad_probs + more[1][...]
    grad_probs = jnp.concatenate([grad_probs[g] for g in range(batch)], axis=1)
    grad_logits = probs * (grad_probs - jnp.sum(probs * grad_probs, axis=0, keepdims=True))
    high = grad_logits.astype(BF16)
    low = (grad_logits - high.astype(F32)).astype(BF16)
    both = jnp.concatenate([high, low], axis=0)
    new = nn(both, routed)
    small[0:experts, :] += new[:experts] + new[experts:]
    grad_routed = grad_routed + tn(both, jnp.concatenate([wrt_ref[...]] * 2, axis=0))
    small[experts + 1 : experts + 2, :] += jnp.sum(grad_routed * xhat, axis=0, keepdims=True)
    g = grad_routed * gm
    grad_res = flat(cot_ref) + scale * (g - row_mean(g) - xhat * row_mean(g * xhat))
    grad_mixed = grad_res.astype(BF16)
    dwo[...] += tn(att_ref[...].reshape(rows, model), grad_mixed)
    gatt_all[...] = nt(grad_mixed, wo[...]).astype(BF16)

    masks = quad_masks()

    def one_image(b, _):
        span = pl.ds(pl.multiple_of(b * PAD, PAD), PAD)
        for quad in range(model // QUAD):
            q, k, v = (
                qkv_ref[b, :, j * model + quad * QUAD : j * model + (quad + 1) * QUAD] for j in range(3)
            )
            grad_heads = stacked(gatt_all[span, quad * QUAD : (quad + 1) * QUAD], masks)
            low_probs = prob_ref[b, quad]
            p = low_probs.astype(F32)
            gw = nt(grad_heads, v)
            ds = (p * (gw - jnp.sum(p * gw, axis=1, keepdims=True))).astype(BF16)
            grad_q = unstacked(nn(ds, k), masks) * HEAD_DIM**-0.5
            grad_k = tn(ds, stacked(q, masks))
            grad_v = tn(low_probs, grad_heads)
            for j, value in enumerate((grad_q, grad_k, grad_v)):
                dqkv_all[span, j * model + quad * QUAD : j * model + (quad + 1) * QUAD] = value.astype(BF16)
        return 0

    lax.fori_loop(0, batch, one_image, 0)
    tok = flat(tok_ref)
    center = tok - row_mean(tok)
    tok_scale = lax.rsqrt(row_mean(center * center) + EPS)
    xin = center * tok_scale
    ga = ga_ref[...]
    normed = (xin * ga).astype(BF16)
    dwq[...] += tn(normed, dqkv_all[...])
    grad_normed = nt(dqkv_all[...], wq[...])
    small[experts : experts + 1, :] += jnp.sum(grad_normed * xin, axis=0, keepdims=True)
    h = grad_normed * ga
    grad_tok = grad_res + tok_scale * (h - row_mean(h) - xin * row_mean(h * xin))
    gtok_ref[...] = grad_tok.astype(BF16).reshape(gtok_ref.shape)

    @pl.when(step == steps - 1)
    def _():
        shards = pack_ref.shape[0]
        part = model // shards
        for s in range(shards):
            at = 0
            blocks = [dwq[:, j * model + s * part : j * model + (s + 1) * part] for j in range(3)]
            for value in blocks + [dwo[s * part : (s + 1) * part, :], small[...]]:
                for c in range(value.shape[1] // 256):
                    pack_ref[s, at : at + value.shape[0], :] = value[:, c * 256 : (c + 1) * 256].astype(BF16)
                    at += value.shape[0]
            if at < pack_ref.shape[1]:
                pack_ref[s, at:, :] = jnp.zeros((pack_ref.shape[1] - at, 256), BF16)


def small_rows(experts):
    return -(-(experts + 2) // 16) * 16


def pack_rows(width, part, experts, align):
    rows = 3 * width * (part // 256) + part * (width // 256) + small_rows(experts) * (width // 256)
    return -(-rows // align) * align


def back(first, sums, residual, cot_pad, tok_pad, qkv, probs, att, gain_attn, gain_moe, w_router, wq, wo, shards, align, batch=2):
    own, _, width = residual.shape
    batch = batch if own % batch == 0 else 1
    experts = w_router.shape[1]
    rows = pack_rows(width, width // shards, experts, align)

    def mine(*shape):
        return pl.BlockSpec((batch,) + shape, lambda i, f: (i,) + (0,) * len(shape))

    image = pl.BlockSpec((batch, PAD, width), lambda i, f: (i + f[0] // batch, 0, 0))
    flat = [v for pair in sums for v in pair]
    return pl.pallas_call(
        functools.partial(back_kernel, steps=own // batch, received=len(sums) - 1),
        out_shape=(
            jax.ShapeDtypeStruct((own, PAD, width), BF16),
            jax.ShapeDtypeStruct((shards, rows, 256), BF16),
        ),
        grid_spec=pltpu.PrefetchScalarGridSpec(
            num_scalar_prefetch=1,
            grid=(own // batch,),
            in_specs=[mine(PAD, width), mine(experts, PAD)] * len(sums)
            + [
                mine(PAD, width),
                image,
                image,
                full((1, width)),
                full((1, width)),
                full((experts, width)),
                full(wq.shape),
                full(wo.shape),
                mine(*qkv.shape[1:]),
                mine(*probs.shape[1:]),
                mine(*att.shape[1:]),
            ],
            out_specs=(mine(PAD, width), full((shards, rows, 256))),
            scratch_shapes=[
                pltpu.VMEM((width, 3 * width), F32),
                pltpu.VMEM((width, width), F32),
                pltpu.VMEM((small_rows(experts), width), F32),
                pltpu.VMEM((batch * PAD, width), BF16),
                pltpu.VMEM((batch * PAD, 3 * width), BF16),
            ],
        ),
        compiler_params=params(),
        cost_estimate=cost(16),
        name="back",
    )(
        first,
        *flat,
        residual,
        cot_pad,
        tok_pad,
        gain_attn.reshape(1, -1),
        gain_moe.reshape(1, -1),
        w_router.T,
        wq,
        wo,
        qkv,
        probs,
        att,
    )


def unpad_kernel(first_ref, own_ref, peer_ref, out_ref, wide, *, images):
    own = own_ref.shape[0]

    def one_image(i, _):
        inner = lax.rem(i, own)
        mine = first_ref[0] == i - inner
        value = jnp.where(mine, own_ref[inner].astype(F32), peer_ref[inner].astype(F32))
        off = lax.rem(i * SEQ, 8)
        span = pl.ds(pl.multiple_of(i * SEQ - off, 8), PAD + 8)
        value = pltpu.roll(jnp.concatenate([value, jnp.zeros((8, value.shape[1]), F32)], axis=0), off, 0)
        wide[span, :] = jnp.where(iota(value.shape, 0) < off, wide[span, :], value)
        return 0

    lax.fori_loop(0, images, one_image, 0)
    out_ref[...] = wide[0 : images * SEQ, :].astype(out_ref.dtype)


def unpad(first, own, peer, dtype):
    images, width = 2 * own.shape[0], own.shape[2]
    return pl.pallas_call(
        functools.partial(unpad_kernel, images=images),
        out_shape=jax.ShapeDtypeStruct((images * SEQ, width), dtype),
        in_specs=[pl.BlockSpec(memory_space=pltpu.SMEM), VMEM, VMEM],
        out_specs=VMEM,
        scratch_shapes=[wide_scratch(images, width)],
        compiler_params=params(),
        cost_estimate=cost(2),
        name="unpad",
    )(first, own, peer)


def body(tokens, routes, gain_attn, w_qkv, w_attn_out, gain_moe, w_router, w_expert_in, w_expert_out, cotangent, *, ways, groups):
    tok_rows, width = tokens.shape
    experts = w_router.shape[1]
    cap = max(4, (5 * tok_rows // (2 * experts) + 7) // 8 * 8)
    chunks = 2
    half = -(-cap // (ways * chunks))
    block = -(-(half + 2) // 16) * 16
    slots = experts * block
    images = tok_rows // SEQ
    own = images // ways
    rank = lax.axis_index("tensor")
    expert = lax.axis_index("expert")
    first = (rank * own).astype(jnp.int32).reshape(1)
    swap = [(0, 1), (1, 0)]

    def other(v):
        return lax.ppermute(v, "tensor", swap)

    def shards_of(v, axis):
        if ways == 2:
            return [v, other(v)]
        return [lax.all_gather(v, "tensor", axis=axis, tiled=True)]

    def exchange(rows):
        return lax.all_to_all(rows, "expert", split_axis=0, concat_axis=0, tiled=True)

    def after(v, *others):
        return lax.optimization_barrier((v,) + others)[0]

    def rows_of(v):
        return v.reshape(-1, width)

    def collected(number, parts, dtype, probs=False, numbers=None, before=()):
        return collect(number, code_col, parts, own, dtype, half, block, probs, numbers, before)

    if ways == 2:
        core = expert % 2
        near = [(i, i ^ 1) for i in range(groups)]

        def part_of(v, axis):
            size = v.shape[axis] // 2
            return other(lax.dynamic_slice_in_dim(v, core * size, size, axis))

    else:
        core = 0 * expert
        wq, wo = shards_of(w_qkv, 2), shards_of(w_attn_out, 0)
    cot_pad, cot_slots, code_col, code_row = front(
        rank.astype(jnp.int32).reshape(1), cotangent, routes, experts, cap, half, block, chunks
    )
    tok_pad = pad(after(tokens, cot_pad))
    if ways == 2:
        got_q, got_o = part_of(after(w_qkv, cot_slots), 2), part_of(after(w_attn_out, cot_slots), 0)
        got_q, got_o, tok_pad = lax.optimization_barrier((got_q, got_o, tok_pad))
        wq = [w_qkv, got_q, lax.ppermute(got_q, "expert", near)]
        wo = [w_attn_out, got_o, lax.ppermute(got_o, "expert", near)]
    cot_slots = exchange(cot_slots)
    w1 = shards_of(after(w_expert_in[0], wq[-1], wo[-1]), 1)
    if ways == 2:
        cut = w_expert_out.shape[1] // 4
        w2_first = other(after(w_expert_out[0, :cut], wq[-1], wo[-1]))
        w2_rest = other(after(w_expert_out[0, cut:], wq[-1], wo[-1]))
    place = jnp.stack([rank * own, core]).astype(jnp.int32)
    routed, residual, qkv, probs, att, wq, wo = attend(place, tok_pad, gain_attn, gain_moe, wq, wo, own)
    sent, x_slots = spread(code_row, rows_of(routed), experts, block, chunks), []
    for c in range(chunks):
        rows = sent[c]
        if c == 0:
            rows, cot_slots = lax.optimization_barrier((rows, cot_slots))
            if ways == 2:
                rows = after(rows, w1[-1], w2_first)
        elif ways == 2:
            rows = after(rows, w2_rest)
        x_slots.append(exchange(rows))
    if ways == 2:
        w1 = [[v] for v in w1]
        w2 = [[w_expert_out[0]], [w2_first, w2_rest]]
    else:
        w1 = [w1]
        w2 = [shards_of(w_expert_out[0], 0)]
    gin, more = [], None
    expert_number = expert.astype(jnp.int32).reshape(1)
    for c in range(chunks):
        new, *more = experts_step(
            expert_number, rows_of(x_slots[c]), cot_slots, more, c, c == chunks - 1, w_router, w1, w2, half, block
        )
        gin.append(exchange(new.reshape(experts, block, width)))
    gated, *dw = more
    gin = [rows_of(v) for v in gin]
    if ways == 2:
        there = ((1 - rank) * own).astype(jnp.int32).reshape(1)
        dw1_peer = other(dw[1])
        cut = dw[3].shape[0] // 4
        dw2_peer = [other(dw[3][:cut])]
        zero = jnp.zeros((1,), jnp.int32)
        start = collect(zero, code_col, gin[:1], images, F32, half, block, True, (0,))
        gin[1], *start = lax.optimization_barrier((gin[1], *start))
        sent = collected(there, gin[1:], BF16, True, (1,), start)
        received = tuple(other(v) for v in sent)
        mine = collected(first, gin[1:], F32, True, (1,), start)
        gated = exchange(after(gated, *sent, dw1_peer, dw2_peer[0]))
        grad_w1 = dw[0] + dw1_peer.astype(F32)
        *received, grad_w1 = lax.optimization_barrier((*received, grad_w1, *mine))[:3]
        sums = [mine, received]
        dw2_peer.append(other(after(dw[3][cut:], *received)))
    else:
        gated = exchange(gated)
        every = [collected(jnp.full((1,), r * own, jnp.int32), gin, F32, True) for r in range(ways)]
        sums = [
            tuple(
                lax.psum_scatter(jnp.stack([v[k] for v in every]).astype(t), "tensor", scatter_dimension=0).astype(F32)
                for k, t in ((0, BF16), (1, F32))
            )
        ]
        grad_w1 = lax.psum_scatter(dw[0].astype(BF16), "tensor", scatter_dimension=1, tiled=True).astype(F32)
        grad_w2 = lax.psum_scatter(dw[1].astype(BF16), "tensor", scatter_dimension=0, tiled=True).astype(F32)
    grad_tok, pack = back(
        first, sums, residual, cot_pad, tok_pad, qkv, probs, att, gain_attn, gain_moe, w_router, wq, wo,
        2 if ways == 2 else 1, groups * 8,
    )

    bits = [1 << b for b in range(groups.bit_length() - 1)]
    if ways == 2:

        def swap_bit(v, bit):
            return lax.ppermute(v, "expert", [(i, i ^ bit) for i in range(groups)])

        def add(a, b):
            return (a.astype(F32) + b.astype(F32)).astype(BF16)

        def halves(v, bit):
            size = v.shape[-2] // 2
            upper = (expert // bit) % 2
            keep = lax.dynamic_slice_in_dim(v, upper * size, size, v.ndim - 2)
            give = lax.dynamic_slice_in_dim(v, (1 - upper) * size, size, v.ndim - 2)
            return keep, give

        pack, grad_tok, gated, dw2_peer[1] = lax.optimization_barrier((pack, grad_tok, gated, dw2_peer[1]))
        grad_peer = other(grad_tok)
        gated = [rows_of(gated[:, c]) for c in range(chunks)]
        (mix,) = collect(zero, code_col, gated, images, BF16, half, block)
        mix_there = lax.dynamic_slice_in_dim(mix, (1 - rank) * own, own, 0)
        mix_here = lax.dynamic_slice_in_dim(mix, rank * own, own, 0)
        for bit in bits[:2]:
            keep, give = halves(pack, bit)
            pack = add(keep, swap_bit(give, bit))
        pack, grad_peer, mix_there, mix_here, grad_w2 = lax.optimization_barrier(
            (pack, grad_peer, mix_there, mix_here, dw[2] + jnp.concatenate(dw2_peer).astype(F32))
        )
        swapped = other(pack[1])
        mix_peer = other(after(mix_there, pack))
        total = add(pack[0], swapped)

        def gathered(v, bit):
            got = swap_bit(v, bit)
            upper = (expert // bit) % 2 == 1
            return jnp.where(upper, jnp.concatenate([got, v]), jnp.concatenate([v, got]))

        grad_tokens = unpad(first, grad_tok, grad_peer, F32)
        keep, give = halves(total, bits[2])
        total = add(keep, swap_bit(give, bits[2]))
        total = add(total, swap_bit(total, bits[3]))
        total, grad_tokens = lax.optimization_barrier((total, grad_tokens))
        total, mix_peer = lax.optimization_barrier((total, mix_peer))
        result = (residual + (mix_here.astype(F32) + mix_peer.astype(F32))).astype(BF16)
        result_peer = other(result)
        total, result = lax.optimization_barrier((total, result))
        for bit in bits[2:0:-1]:
            total = gathered(total, bit)
        total, result_peer = lax.optimization_barrier((total, result_peer))
        total = gathered(total, bits[0])
        result = unpad(first, result, result_peer, BF16)
        total = total.astype(F32)
        part = w_qkv.shape[2]
    else:
        gated = [rows_of(gated[:, c]) for c in range(chunks)]
        every = [collected(jnp.full((1,), r * own, jnp.int32), gated, BF16)[0] for r in range(ways)]
        mixture = lax.psum_scatter(jnp.stack(every), "tensor", scatter_dimension=0).astype(F32)

        def whole(v):
            v = lax.all_gather(v, "tensor", axis=0, tiled=True)
            return v[:, :SEQ].reshape(tok_rows, width)

        result = whole((residual + mixture).astype(BF16))
        grad_tokens = whole(grad_tok).astype(F32)
        total = lax.psum(pack[0], ("expert", "tensor")).astype(F32)
        part = width

    def take(at, rows, cols):
        blocks = [total[at + b * rows : at + (b + 1) * rows] for b in range(cols // 256)]
        return jnp.concatenate(blocks, axis=1) if len(blocks) > 1 else blocks[0]

    step = width * (part // 256)
    grad_w_qkv = jnp.stack([take(j * step, width, part) for j in range(3)])
    grad_w_attn_out = take(3 * step, part, width)
    small = take(3 * step + part * (width // 256), small_rows(experts), width)
    if ways != 2:
        grad_w_qkv = lax.dynamic_slice_in_dim(grad_w_qkv, rank * w_qkv.shape[2], w_qkv.shape[2], 2)
        grad_w_attn_out = lax.dynamic_slice_in_dim(grad_w_attn_out, rank * w_qkv.shape[2], w_qkv.shape[2], 0)
    return (
        result,
        grad_tokens,
        small[experts],
        grad_w_qkv,
        grad_w_attn_out,
        small[experts + 1],
        small[:experts].T,
        grad_w1[None],
        grad_w2[None],
    )


def solution(mesh):
    placed = (
        P("expert", None),
        P("expert", None),
        P(),
        P(None, None, "tensor"),
        P("tensor", None),
        P(),
        P(),
        P("expert", None, "tensor"),
        P("expert", "tensor", None),
        P("expert", None),
    )
    return jax.shard_map(
        functools.partial(body, ways=mesh.shape["tensor"], groups=mesh.shape["expert"]),
        mesh=mesh,
        in_specs=placed,
        out_specs=(
            P("expert", None),
            P("expert", None),
            P(),
            P(None, None, "tensor"),
            P("tensor", None),
            P(),
            P(),
            P("expert", None, "tensor"),
            P("expert", "tensor", None),
        ),
        check_vma=False,
    )
```

profile of v0, /device:TPU:0, one launch (start us, length us, event | category | flops | bytes accessed | tf_op | source)
XLA Modules:
  0.0 326.9 jit_solution(804640573569351956)
XLA Ops:
  3.0 9.6 %front.1 = (bf16[8,208,512]{2,1,0:T(8,128)(2,1)}, bf16[16,2,64,512]{3,2,1,0:T(8,128)(2,1)}, s32[208,16]{1,0:T(8,128)}, s32[2,1664]{1,0:T(2,128)}) custom-call(s32[1]{0:T(128)} %bitcast.1.rank_ref, bf16[1576,512]{1,0:T(8,128)(2,1)} %cot_ref.1, s32[208,16]{1,0:T(8,128)} %copy.25.col_ref, s32[2,1664]{1,0:T(2,128)} %bitcast.63), custom_call_target="tpu_custom_call" | custom-call | bytes 36900000 | tf_op jit(solution)/shard_map/front/pallas_call | solution.py:152
  12.6 7.5 %all-to-all-start.1 = ((bf16[16,2,64,512]{3,2,1,0:T(8,128)(2,1)}), bf16[16,2,64,512]{3,2,1,0:T(8,128)(2,1)S(1)}, u32[]{:S(2)}, u32[]{:S(2)}) async-start(bf16[16,2,64,512]{3,2,1,0:T(8,128)(2,1)} %get-tuple-element.83), calls=%async_computation.1 | async-start | bytes 4194304 | tf_op jit(solution)/shard_map/all_to_all | solution.py:797
  20.2 1.6 collective-permute-start
  22.4 4.2 %pad.65.tok_ref.rest_6_ = bf16[8,208,512]{2,1,0:T(8,128)(2,1)} custom-call(bf16[1576,512]{1,0:T(8,128)(2,1)} %source), custom_call_target="tpu_custom_call" | custom-call | bytes 7380000 | tf_op jit(solution)/shard_map/pad/pallas_call | solution.py:66
  26.6 7.9 %collective-permute-done.1.rest_4_ = bf16[128,512]{1,0:T(8,128)(2,1)S(1)} collective-permute-done((bf16[128,512]{1,0:T(8,128)(2,1)S(1)}, bf16[128,512]{1,0:T(8,128)(2,1)S(1)}, u32[]{:S(2)}, u32[]{:S(2)}) %collective-permute-start.1) | collective-permute-done | bytes 131104 | tf_op jit(solution)/shard_map/ppermute | solution.py:789
  36.5 1.5 collective-permute-start.5
  39.9 22.2 %attend.1 = (bf16[8,208,512]{2,1,0:T(8,128)(2,1)}, f32[4,208,512]{2,1,0:T(8,128)}, bf16[4,208,1536]{2,1,0:T(8,128)(2,1)}, bf16[4,2,832,208]{3,2,1,0:T(8,128)(2,1...) custom-call(s32[2]{0:T(128)} %pad_add_fusion.place_ref, ...), custom_call_target="tpu_custom_call" | custom-call | bytes 92250000 | tf_op jit(solution)/shard_map/attend/pallas_call | solution.py:309
  62.2 7.3 %spread.1 = (bf16[16,64,512]{2,1,0:T(8,128)(2,1)}, bf16[16,64,512]{2,1,0:T(8,128)(2,1)}) custom-call(s32[2,1664]{1,0:T(2,128)} %get-tuple-element.82.code_ref, bf16[1664,512]{1,0:T(8,128)(2,1)} %bitcast.59), custom_call_target="tpu_custom_call" | custom-call | bytes 33210000 | tf_op jit(solution)/shard_map/spread/pallas_call | solution.py:187
  69.5 5.8 %all-to-all-start.2 = ((bf16[16,64,512]{2,1,0:T(8,128)(2,1)}), bf16[16,64,512]{2,1,0:T(8,128)(2,1)}, u32[]{:S(2)}, u32[]{:S(2)}) async-start(bf16[16,64,512]{2,1,0:T(8,128)(2,1)} %get-tuple-element.100), calls=%async_computation.2 | async-start | bytes 2097152 | tf_op jit(solution)/shard_map/all_to_all | solution.py:797
  75.4 1.5 collective-permute-start.4
  76.9 18.4 %collective-permute-done.4.rest_4_ = bf16[768,512]{1,0:T(8,128)(2,1)S(1)} collective-permute-done((bf16[768,512]{1,0:T(8,128)(2,1)S(1)}, bf16[768,512]{1,0:T(8,128)(2,1)S(1)}, u32[]{:S(2)}, u32[]{:S(2)}) %collective-permute-start.4) | collective-permute-done | bytes 786464 | tf_op jit(solution)/shard_map/ppermute | solution.py:789
  95.2 3.0 all-to-all-done.2
  98.3 6.9 %all-to-all-start = ((bf16[16,64,512]{2,1,0:T(8,128)(2,1)}), bf16[16,64,512]{2,1,0:T(8,128)(2,1)S(1)}, u32[]{:S(2)}, u32[]{:S(2)}) async-start(bf16[16,64,512]{2,1,0:T(8,128)(2,1)} %get-tuple-element.94), calls=%async_computation | async-start | bytes 2097152 | tf_op jit(solution)/shard_map/all_to_all | solution.py:797
  105.9 22.0 %experts.2 = (bf16[1024,512]{1,0:T(8,128)(2,1)}, bf16[16,2,64,512]{3,2,1,0:T(8,128)(2,1)}, f32[512,1024]{1,0:T(8,128)}, f32[512,1024]{1,0:T(8,128)}, f32[1024,512]{1,0:T(8,128)}, /*index=5*/f32[1024,512]{1,0:T(8,128)}) custom-call(s32[1]{0:T(128)} %bitcast.4.expert_ref, bf16[1024,512]{1,0:T(8,128)(2,1)} %bitcast.14.x_ref, bf16[16,2,64,512]{3,2,1,0:T(8,128)(2,1)} %copy-done, ...), custom_call_target="tpu_custom_call" | custom-call | bytes 73800000 | tf_op jit(solution)/shard_map/experts/pallas_call | solution.py:462
  129.1 6.9 %all-to-all-start.4 = ((bf16[16,64,512]{2,1,0:T(8,128)(2,1)}), bf16[16,64,512]{2,1,0:T(8,128)(2,1)S(1)}, u32[]{:S(2)}, u32[]{:S(2)}) async-start(bf16[16,64,512]{2,1,0:T(8,128)(2,1)} %bitcast.61), calls=%async_computation.4 | async-start | bytes 2097152 | tf_op jit(solution)/shard_map/all_to_all | solution.py:797
  135.9 22.8 %experts.3 = (bf16[1024,512]{1,0:T(8,128)(2,1)}, bf16[16,2,64,512]{3,2,1,0:T(8,128)(2,1)}, f32[512,1024]{1,0:T(8,128)}, bf16[512,1024]{1,0:T(8,128)(2,1)}, f32[1...) custom-call(s32[1]{0:T(128)} %bitcast.4.expert_ref, bf16[1024,512]{1,0:T(8,128)(2,1)} %bitcast.56, ...), custom_call_target="tpu_custom_call", output_to_operand_aliasing={{1}: (13, {})} | custom-call | bytes 73800000 | tf_op jit(solution)/shard_map/experts/pallas_call | solution.py:462
  158.9 6.9 %all-to-all-start.3 = ((bf16[16,64,512]{2,1,0:T(8,128)(2,1)}), bf16[16,64,512]{2,1,0:T(8,128)(2,1)S(1)}, u32[]{:S(2)}, u32[]{:S(2)}) async-start(bf16[16,64,512]{2,1,0:T(8,128)(2,1)} %bitcast.60), calls=%async_computation.3 | async-start | bytes 2097152 | tf_op jit(solution)/shard_map/all_to_all | solution.py:797
  165.8 1.5 collective-permute-start.9
  168.9 8.9 %collect.4 = (f32[8,208,512]{2,1,0:T(8,128)}, f32[8,16,208]{2,1,0:T(8,128)}) custom-call(s32[1]{0:T(128)} %constant.87.clone.1.first_ref, s32[208,16]{1,0:T(8,128)} %get-tuple-element.81.code_ref, bf16[1024,512]{1,0:T(8,128)(2,1)} %bitcast.53), custom_call_target="tpu_custom_call" | custom-call | bytes 25830000 | tf_op jit(solution)/shard_map/collect/pallas_call | solution.py:554
  177.8 10.9 %all-to-all-done.3 = bf16[16,64,512]{2,1,0:T(8,128)(2,1)S(1)} async-done(((bf16[16,64,512]{2,1,0:T(8,128)(2,1)}), bf16[16,64,512]{2,1,0:T(8,128)(2,1)S(1)}, u32[]{:S(2)}, u32[]{:S(2)}) %all-to-all-start.3) | async-done | bytes 1048608 | tf_op jit(solution)/shard_map/all_to_all | solution.py:797
  189.7 5.9 %collect.6 = (bf16[4,208,512]{2,1,0:T(8,128)(2,1)}, f32[4,16,208]{2,1,0:T(8,128)}) custom-call(s32[1]{0:T(128)} %bitcast.19.first_ref, s32[208,16]{1,0:T(8,128)} %get-tuple-element.81.code_ref, bf16[1024,512]{1,0:T(8,128)(2,1)} %bitcast.49, f32[8,208,512]{2,1,0:T(8,128)} %get-tuple-element.111.rest_1_, f32[8,16,208]{2,1,0:T(8,128)} %get-tuple-element.112.rest_2_), custom_call_target="tpu_custom_call" | custom-call | bytes 25830000 | tf_op jit(solution)/shard_map/collect/pallas_call | solution.py:554
  195.5 1.5 collective-permute-done.10
  197.1 5.9 %all-to-all-start.5 = ((bf16[16,2,64,512]{3,2,1,0:T(8,128)(2,1)}), bf16[16,2,64,512]{3,2,1,0:T(8,128)(2,1)S(1)}, u32[]{:S(2)}, u32[]{:S(2)}) async-start(bf16[16,2,64,512]{3,2,1,0:T(8,128)(2,1)} %get-tuple-element.131), calls=%async_computation.5 | async-start | bytes 4194304 | tf_op jit(solution)/shard_map/all_to_all | solution.py:797
  203.0 1.5 collective-permute-start.7
  206.0 3.6 %convert_add_fusion.1 = f32[512,1024]{1,0:T(8,128)} fusion(f32[512,1024]{1,0:T(8,128)} %get-tuple-element.117, bf16[512,1024]{1,0:T(8,128)(2,1)} %collective-permute-done.9), kind=kLoop, calls=%fused_computation.2 | loop fusion | flops 1048576 | bytes 5242880 | tf_op jit(solution)/shard_map/add | solution.py:873
  209.6 5.9 %collect.5 = (f32[4,208,512]{2,1,0:T(8,128)}, f32[4,16,208]{2,1,0:T(8,128)}) custom-call(s32[1]{0:T(128)} %bitcast.first_ref, s32[208,16]{1,0:T(8,128)} %get-tuple-element.81.code_ref, bf16[1024,512]{1,0:T(8,128)(2,1)} %bitcast.50, f32[8,208,512]{2,1,0:T(8,128)} %get-tuple-element.111.rest_1_, f32[8,16,208]{2,1,0:T(8,128)} %get-tuple-element.112.rest_2_), custom_call_target="tpu_custom_call" | custom-call | bytes 25830000 | tf_op jit(solution)/shard_map/collect/pallas_call | solution.py:554
  215.5 10.5 %collective-permute-done.8.rest_3_ = f32[4,16,208]{2,1,0:T(8,128)S(1)} collective-permute-done((f32[4,16,208]{2,1,0:T(8,128)S(1)}, f32[4,16,208]{2,1,0:T(8,128)S(1)}, u32[]{:S(2)}, u32[]{:S(2)}) %collective-permute-start.8) | collective-permute-done | bytes 53280 | tf_op jit(solution)/shard_map/ppermute | solution.py:789
  225.9 1.4 collective-permute-start.11
  227.4 20.0 %back.1 = (bf16[4,208,512]{2,1,0:T(8,128)(2,1)}, bf16[2,2176,256]{2,1,0:T(8,128)(2,1)}) custom-call(s32[1]{0:T(128)} %bitcast.first_ref, f32[4,208,512]{2,1,0:T(8,128)} %get-tuple-element.113.rest_0_, f32[4,16,208]{2,1,0:T(8,128)} %get-tuple-element.114.rest_1_, bf16[4,208,512]{2,1,0:T(8,128)(2,1)} %collective-permute-done.7.rest_2_, ...), custom_call_target="tpu_custom_call" | custom-call | bytes 59040000 | tf_op jit(solution)/shard_map/back/pallas_call | solution.py:690
  250.4 2.1 collective-permute-done.12
  252.5 1.9 add_convert_fusion
  254.4 1.7 collective-permute-start.13
  256.1 1.5 fusion.5
  257.6 8.2 %collect.7 = bf16[8,208,512]{2,1,0:T(8,128)(2,1)} custom-call(s32[1]{0:T(128)} %constant.87.clone.1.first_ref, s32[208,16]{1,0:T(8,128)} %get-tuple-element.81.code_ref, bf16[1024,512]{1,0:T(8,128)(2,1)} %bitcast.55, bf16[1024,512]{1,0:T(8,128)(2,1)} %bitcast.54), custom_call_target="tpu_custom_call" | custom-call | bytes 25830000 | tf_op jit(solution)/shard_map/collect/pallas_call | solution.py:554
  265.8 1.7 constant_dynamic-slice_fusion.1
  268.1 1.6 convert_add_fusion
  273.4 7.7 %collective-permute-done.15 = bf16[544,256]{1,0:T(8,128)(2,1)} collective-permute-done((bf16[544,256]{1,0:T(8,128)(2,1)S(1)}, bf16[544,256]{1,0:T(8,128)(2,1)}, u32[]{:S(2)}, u32[]{:S(2)}) %collective-permute-start.15) | collective-permute-done | bytes 278560 | tf_op jit(solution)/shard_map/ppermute | solution.py:789
  282.1 2.6 collective-permute-start.16
  284.7 3.0 collective-permute-done.16
  287.8 5.7 %collective-permute-start.17 = (bf16[272,256]{1,0:T(8,128)(2,1)S(1)}, bf16[272,256]{1,0:T(8,128)(2,1)S(1)}, u32[]{:S(2)}, u32[]{:S(2)}) collective-permute-start(bf16[272,256]{1,0:T(8,128)(2,1)S(1)} %add_convert_fusion.4), channel_id=1, source_target_pairs={{0,16},{2,18},{4,20},{6,22},{8,24},{10,26},{12,28},{14,30},{16,0},... | collective-permute-start | bytes 417800 | tf_op jit(solution)/shard_map/ppermute | solution.py:897
  293.4 5.1 %unpad.2 = f32[1576,512]{1,0:T(8,128)} custom-call(s32[1]{0:T(128)} %bitcast.first_ref, bf16[4,208,512]{2,1,0:T(8,128)(2,1)} %get-tuple-element.134.own_ref, bf16[4,208,512]{2,1,0:T(8,128)(2,1)} %collective-permute-done.14.peer_ref), custom_call_target="tpu_custom_call" | custom-call | bytes 7380000 | tf_op jit(solution)/shard_map/unpad/pallas_call | solution.py:761
  299.0 1.5 collective-permute-start.21
  300.5 2.0 collective-permute-start.19
  302.5 3.1 collective-permute-done.19
  305.6 2.4 collective-permute-start.20
  308.1 4.5 %collective-permute-done.20 = bf16[544,256]{1,0:T(8,128)(2,1)S(1)} collective-permute-done((bf16[544,256]{1,0:T(8,128)(2,1)S(1)}, bf16[544,256]{1,0:T(8,128)(2,1)S(1)}, u32[]{:S(2)}, u32[]{:S(2)}) %collective-permute-start.20) | collective-permute-done | bytes 278560 | tf_op jit(solution)/shard_map/ppermute | solution.py:897
  312.9 4.9 %collective-permute-done.21.peer_ref = bf16[4,208,512]{2,1,0:T(8,128)(2,1)S(1)} collective-permute-done((bf16[4,208,512]{2,1,0:T(8,128)(2,1)S(1)}, bf16[4,208,512]{2,1,0:T(8,128)(2,1)S(1)}, u32[]{:S(2)}, u32[]{:S(2)}) %collective-permute-start.21) | collective-permute-done | bytes 852000 | tf_op jit(solution)/shard_map/ppermute | solution.py:789
  318.7 4.5 %unpad.3 = bf16[1576,512]{1,0:T(8,128)(2,1)} custom-call(s32[1]{0:T(128)} %bitcast.first_ref, bf16[4,208,512]{2,1,0:T(8,128)(2,1)} %copy-done.6, bf16[4,208,512]{2,1,0:T(8,128)(2,1)} %copy-done.12), custom_call_target="tpu_custom_call" | custom-call | bytes 7380000 | tf_op jit(solution)/shard_map/unpad/pallas_call | solution.py:761
  (109 shorter events, 26.8 us)
Async XLA Ops:
  12.5 7.6 %copy-start.9 = (bf16[3,512,256]{2,1,0:T(8,128)(2,1)S(1)}, bf16[3,512,256]{2,1,0:T(8,128)(2,1)}, u32[]{:S(2)}) copy-start(bf16[3,512,256]{2,1,0:T(8,128)(2,1)} %rest_0_.1) | copy-start | bytes 2359300
  12.5 9.2 %copy-start.15 = (bf16[256,512]{1,0:T(8,128)(2,1)S(1)}, bf16[256,512]{1,0:T(8,128)(2,1)}, u32[]{:S(2)}) copy-start(bf16[256,512]{1,0:T(8,128)(2,1)} %rest_3_.1) | copy-start | bytes 786436
  12.6 56.9 %all-to-all-start.1 = ((bf16[16,2,64,512]{3,2,1,0:T(8,128)(2,1)}), bf16[16,2,64,512]{3,2,1,0:T(8,128)(2,1)S(1)}, u32[]{:S(2)}, u32[]{:S(2)}) async-start(bf16[16,2,64,512]{3,2,1,0:T(8,128)(2,1)} %get-tuple-element.83), calls=%async_computation.1 | async-start | bytes 4194304 | tf_op jit(solution)/shard_map/all_to_all | solution.py:797
  20.2 14.3 %collective-permute-start = (bf16[3,512,128]{2,1,0:T(8,128)(2,1)S(1)}, bf16[3,512,128]{2,1,0:T(8,128)(2,1)S(1)}, u32[]{:S(2)}, u32[]{:S(2)}) collective-permute-start(bf16[3,512,128]{2,1,0:T(8,128)(2,1)S(1)} %constant_dynamic-slice_fusion.6), channel_id=1, source_target_pairs={{0,1},{1,0},{2,3},{3,2},{4,5},{5,4},{6,7},{7,6},{8,9},{9,8},{10,11... | collective-permute-start | bytes 1179656 | tf_op jit(solution)/shard_map/ppermute | solution.py:789
  21.8 16.2 %copy-start.2 = (bf16[1,1024,512]{2,1,0:T(8,128)(2,1)S(1)}, bf16[1,1024,512]{2,1,0:T(8,128)(2,1)}, u32[]{:S(2)}) copy-start(bf16[1,1024,512]{2,1,0:T(8,128)(2,1)} %param.18) | copy-start | bytes 3145732
  21.8 12.7 %collective-permute-start.1 = (bf16[128,512]{1,0:T(8,128)(2,1)S(1)}, bf16[128,512]{1,0:T(8,128)(2,1)S(1)}, u32[]{:S(2)}, u32[]{:S(2)}) collective-permute-start(bf16[128,512]{1,0:T(8,128)(2,1)S(1)} %constant_dynamic-slice_fusion.5), channel_id=1, source_target_pairs={{0,1},{1,0},{2,3},{3,2},{4,5},{5,4},{6,7},{7,6},{8,9},{9,8},{10,11... | collective-permute-start | bytes 393224 | tf_op jit(solution)/shard_map/ppermute | solution.py:789
  34.5 5.5 %copy-start.18 = (bf16[128,512]{1,0:T(8,128)(2,1)}, bf16[128,512]{1,0:T(8,128)(2,1)S(1)}, u32[]{:S(2)}) copy-start(bf16[128,512]{1,0:T(8,128)(2,1)S(1)} %collective-permute-done.1.rest_4_) | copy-start | bytes 393220
  34.5 3.5 %copy-start.16 = (bf16[3,512,128]{2,1,0:T(8,128)(2,1)}, bf16[3,512,128]{2,1,0:T(8,128)(2,1)S(1)}, u32[]{:S(2)}) copy-start(bf16[3,512,128]{2,1,0:T(8,128)(2,1)S(1)} %collective-permute-done.rest_1_) | copy-start | bytes 1179652
  34.5 2.0 collective-permute-start.2
  34.6 1.9 collective-permute-start.3
  36.5 1.6 copy-start.19
  36.5 2.3 copy-start.17
  36.5 33.0 %collective-permute-start.5 = (bf16[512,1024]{1,0:T(8,128)(2,1)}, bf16[512,1024]{1,0:T(8,128)(2,1)}, u32[]{:S(2)}, u32[]{:S(2)}) collective-permute-start(bf16[512,1024]{1,0:T(8,128)(2,1)} %bitcast.11.rest_0_), channel_id=1, source_target_pairs={{0,1},{1,0},{2,3},{3,2},{4,5},{5,4},{6,7},{7,6},{8,9},{9,8},{10,11... | collective-permute-start | bytes 3145736 | tf_op jit(solution)/shard_map/ppermute | solution.py:789
  38.8 30.7 %collective-permute-start.6 = (bf16[256,512]{1,0:T(8,128)(2,1)}, bf16[256,512]{1,0:T(8,128)(2,1)S(1)}, u32[]{:S(2)}, u32[]{:S(2)}) collective-permute-start(bf16[256,512]{1,0:T(8,128)(2,1)} %slice_bitcast_fusion.5), channel_id=1, source_target_pairs={{0,1},{1,0},{2,3},{3,2},{4,5},{5,4},{6,7},{7,6},{8,9},{9,8},{10,11... | collective-permute-start | bytes 786440 | tf_op jit(solution)/shard_map/ppermute | solution.py:789
  69.4 5.9 %copy-start = (bf16[16,2,64,512]{3,2,1,0:T(8,128)(2,1)}, bf16[16,2,64,512]{3,2,1,0:T(8,128)(2,1)S(1)}, u32[]{:S(2)}) copy-start(bf16[16,2,64,512]{3,2,1,0:T(8,128)(2,1)S(1)} %all-to-all-done.1.cot_ref) | copy-start | bytes 6291460
  69.4 5.8 %copy-start.11 = (bf16[256,512]{1,0:T(8,128)(2,1)}, bf16[256,512]{1,0:T(8,128)(2,1)S(1)}, u32[]{:S(2)}) copy-start(bf16[256,512]{1,0:T(8,128)(2,1)S(1)} %collective-permute-done.6.rest_3_) | copy-start | bytes 786436
  69.5 28.8 %all-to-all-start.2 = ((bf16[16,64,512]{2,1,0:T(8,128)(2,1)}), bf16[16,64,512]{2,1,0:T(8,128)(2,1)}, u32[]{:S(2)}, u32[]{:S(2)}) async-start(bf16[16,64,512]{2,1,0:T(8,128)(2,1)} %get-tuple-element.100), calls=%async_computation.2 | async-start | bytes 2097152 | tf_op jit(solution)/shard_map/all_to_all | solution.py:797
  75.3 29.9 %copy-start.21 = (bf16[512,16]{0,1:T(8,128)(2,1)S(1)}, bf16[512,16]{0,1:T(8,128)(2,1)}, u32[]{:S(2)}) copy-start(bf16[512,16]{0,1:T(8,128)(2,1)} %param.16) | copy-start | bytes 49156
  75.4 19.9 %collective-permute-start.4 = (bf16[768,512]{1,0:T(8,128)(2,1)S(1)}, bf16[768,512]{1,0:T(8,128)(2,1)S(1)}, u32[]{:S(2)}, u32[]{:S(2)}) collective-permute-start(bf16[768,512]{1,0:T(8,128)(2,1)S(1)} %slice_bitcast_fusion), channel_id=1, source_target_pairs={{0,1},{1,0},{2,3},{3,2},{4,5},{5,4},{6,7},{7,6},{8,9},{9,8},{10,11... | collective-permute-start | bytes 2359304 | tf_op jit(solution)/shard_map/ppermute | solution.py:789
  95.2 10.7 %copy-start.7 = (bf16[768,512]{1,0:T(8,128)(2,1)}, bf16[768,512]{1,0:T(8,128)(2,1)S(1)}, u32[]{:S(2)}) copy-start(bf16[768,512]{1,0:T(8,128)(2,1)S(1)} %collective-permute-done.4.rest_4_) | copy-start | bytes 2359300
  98.3 29.8 %all-to-all-start = ((bf16[16,64,512]{2,1,0:T(8,128)(2,1)}), bf16[16,64,512]{2,1,0:T(8,128)(2,1)S(1)}, u32[]{:S(2)}, u32[]{:S(2)}) async-start(bf16[16,64,512]{2,1,0:T(8,128)(2,1)} %get-tuple-element.94), calls=%async_computation | async-start | bytes 2097152 | tf_op jit(solution)/shard_map/all_to_all | solution.py:797
  129.1 29.8 %all-to-all-start.4 = ((bf16[16,64,512]{2,1,0:T(8,128)(2,1)}), bf16[16,64,512]{2,1,0:T(8,128)(2,1)S(1)}, u32[]{:S(2)}, u32[]{:S(2)}) async-start(bf16[16,64,512]{2,1,0:T(8,128)(2,1)} %bitcast.61), calls=%async_computation.4 | async-start | bytes 2097152 | tf_op jit(solution)/shard_map/all_to_all | solution.py:797
  158.9 10.0 %copy-start.4 = (bf16[16,64,512]{2,1,0:T(8,128)(2,1)}, bf16[16,64,512]{2,1,0:T(8,128)(2,1)S(1)}, u32[]{:S(2)}) copy-start(bf16[16,64,512]{2,1,0:T(8,128)(2,1)S(1)} %all-to-all-done.4) | copy-start | bytes 3145732
  158.9 29.8 %all-to-all-start.3 = ((bf16[16,64,512]{2,1,0:T(8,128)(2,1)}), bf16[16,64,512]{2,1,0:T(8,128)(2,1)S(1)}, u32[]{:S(2)}, u32[]{:S(2)}) async-start(bf16[16,64,512]{2,1,0:T(8,128)(2,1)} %bitcast.60), calls=%async_computation.3 | async-start | bytes 2097152 | tf_op jit(solution)/shard_map/all_to_all | solution.py:797
  165.8 31.3 %collective-permute-start.9 = (bf16[512,1024]{1,0:T(8,128)(2,1)}, bf16[512,1024]{1,0:T(8,128)(2,1)}, u32[]{:S(2)}, u32[]{:S(2)}) collective-permute-start(bf16[512,1024]{1,0:T(8,128)(2,1)} %get-tuple-element.118), channel_id=1, source_target_pairs={{0,1},{1,0},{2,3},{3,2},{4,5},{5,4},{6,7},{7,6},{8,9},{9,8},{10,11... | collective-permute-start | bytes 3145736 | tf_op jit(solution)/shard_map/ppermute | solution.py:789
  168.2 28.8 %collective-permute-start.10 = (bf16[256,512]{1,0:T(8,128)(2,1)S(1)}, bf16[256,512]{1,0:T(8,128)(2,1)S(1)}, u32[]{:S(2)}, u32[]{:S(2)}) collective-permute-start(bf16[256,512]{1,0:T(8,128)(2,1)S(1)} %slice.56), channel_id=1, source_target_pairs={{0,1},{1,0},{2,3},{3,2},{4,5},{5,4},{6,7},{7,6},{8,9},{9,8},{10,11... | collective-permute-start | bytes 786440 | tf_op jit(solution)/shard_map/ppermute | solution.py:789
  197.1 7.4 %copy-start.10 = (bf16[1024,512]{1,0:T(8,128)(2,1)S(1)}, bf16[1024,512]{1,0:T(8,128)(2,1)}, u32[]{:S(2)}) copy-start(bf16[1024,512]{1,0:T(8,128)(2,1)} %get-tuple-element.130) | copy-start | bytes 3145732
  197.1 8.3 %copy-start.22 = (f32[4,16,208]{2,1,0:T(8,128)S(1)}, f32[4,16,208]{2,1,0:T(8,128)}, u32[]{:S(2)}) copy-start(f32[4,16,208]{2,1,0:T(8,128)} %get-tuple-element.116) | copy-start | bytes 159748
  197.1 50.3 %all-to-all-start.5 = ((bf16[16,2,64,512]{3,2,1,0:T(8,128)(2,1)}), bf16[16,2,64,512]{3,2,1,0:T(8,128)(2,1)S(1)}, u32[]{:S(2)}, u32[]{:S(2)}) async-start(bf16[16,2,64,512]{3,2,1,0:T(8,128)(2,1)} %get-tuple-element.131), calls=%async_computation.5 | async-start | bytes 4194304 | tf_op jit(solution)/shard_map/all_to_all | solution.py:797
  203.0 23.0 %collective-permute-start.7 = (bf16[4,208,512]{2,1,0:T(8,128)(2,1)}, bf16[4,208,512]{2,1,0:T(8,128)(2,1)}, u32[]{:S(2)}, u32[]{:S(2)}) collective-permute-start(bf16[4,208,512]{2,1,0:T(8,128)(2,1)} %get-tuple-element.115), channel_id=1, source_target_pairs={{0,1},{1,0},{2,3},{3,2},{4,5},{5,4},{6,7},{7,6},{8,9},{9,8},{10,11... | collective-permute-start | bytes 2555912 | tf_op jit(solution)/shard_map/ppermute | solution.py:789
  205.4 20.5 %collective-permute-start.8 = (f32[4,16,208]{2,1,0:T(8,128)S(1)}, f32[4,16,208]{2,1,0:T(8,128)S(1)}, u32[]{:S(2)}, u32[]{:S(2)}) collective-permute-start(f32[4,16,208]{2,1,0:T(8,128)S(1)} %copy-done.22), channel_id=1, source_target_pairs={{0,1},{1,0},{2,3},{3,2},{4,5},{5,4},{6,7},{7,6},{8,9},{9,8},{10,11... | collective-permute-start | bytes 159752 | tf_op jit(solution)/shard_map/ppermute | solution.py:789
  225.9 1.4 copy-start.20
  225.9 21.4 %collective-permute-start.11 = (bf16[768,512]{1,0:T(8,128)(2,1)}, bf16[768,512]{1,0:T(8,128)(2,1)S(1)}, u32[]{:S(2)}, u32[]{:S(2)}) collective-permute-start(bf16[768,512]{1,0:T(8,128)(2,1)} %slice.57), channel_id=1, source_target_pairs={{0,1},{1,0},{2,3},{3,2},{4,5},{5,4},{6,7},{7,6},{8,9},{9,8},{10,11... | collective-permute-start | bytes 2359304 | tf_op jit(solution)/shard_map/ppermute | solution.py:789
  249.6 3.0 collective-permute-start.12
  249.7 21.6 %collective-permute-start.14 = (bf16[4,208,512]{2,1,0:T(8,128)(2,1)}, bf16[4,208,512]{2,1,0:T(8,128)(2,1)}, u32[]{:S(2)}, u32[]{:S(2)}) collective-permute-start(bf16[4,208,512]{2,1,0:T(8,128)(2,1)} %get-tuple-element.134.own_ref), channel_id=1, source_target_pairs={{0,1},{1,0},{2,3},{3,2},{4,5},{5,4},{6,7},{7,6},{8,9},{9,8},{10,11... | collective-permute-start | bytes 2555912 | tf_op jit(solution)/shard_map/ppermute | solution.py:789
  254.4 15.3 %collective-permute-start.13 = (bf16[2,544,256]{2,1,0:T(8,128)(2,1)S(1)}, bf16[2,544,256]{2,1,0:T(8,128)(2,1)S(1)}, u32[]{:S(2)}, u32[]{:S(2)}) collective-permute-start(bf16[2,544,256]{2,1,0:T(8,128)(2,1)S(1)} %constant_dynamic-slice_fusion.3), channel_id=1, source_target_pairs={{0,4},{2,6},{4,0},{6,2},{8,12},{10,14},{12,8},{14,10},{16,20},{18,... | collective-permute-start | bytes 1671176 | tf_op jit(solution)/shard_map/ppermute | solution.py:897
  265.8 2.1 copy-start.8
  265.8 2.3 copy-start.14
  271.3 9.8 %collective-permute-start.15 = (bf16[544,256]{1,0:T(8,128)(2,1)S(1)}, bf16[544,256]{1,0:T(8,128)(2,1)}, u32[]{:S(2)}, u32[]{:S(2)}) collective-permute-start(bf16[544,256]{1,0:T(8,128)(2,1)S(1)} %slice_bitcast_fusion.4), channel_id=1, source_target_pairs={{0,1},{1,0},{2,3},{3,2},{4,5},{5,4},{6,7},{7,6},{8,9},{9,8},{10,11... | collective-permute-start | bytes 835592 | tf_op jit(solution)/shard_map/ppermute | solution.py:789
  272.0 26.5 %collective-permute-start.18 = (bf16[4,208,512]{2,1,0:T(8,128)(2,1)S(1)}, bf16[4,208,512]{2,1,0:T(8,128)(2,1)S(1)}, u32[]{:S(2)}, u32[]{:S(2)}) collective-permute-start(bf16[4,208,512]{2,1,0:T(8,128)(2,1)S(1)} %get-tuple-element.142), channel_id=1, source_target_pairs={{0,1},{1,0},{2,3},{3,2},{4,5},{5,4},{6,7},{7,6},{8,9},{9,8},{10,11... | collective-permute-start | bytes 2555912 | tf_op jit(solution)/shard_map/ppermute | solution.py:789
  282.1 5.6 %collective-permute-start.16 = (bf16[272,256]{1,0:T(8,128)(2,1)S(1)}, bf16[272,256]{1,0:T(8,128)(2,1)S(1)}, u32[]{:S(2)}, u32[]{:S(2)}) collective-permute-start(bf16[272,256]{1,0:T(8,128)(2,1)S(1)} %constant_dynamic-slice_fusion), channel_id=1, source_target_pairs={{0,8},{2,10},{4,12},{6,14},{8,0},{10,2},{12,4},{14,6},{16,24},{18,... | collective-permute-start | bytes 417800 | tf_op jit(solution)/shard_map/ppermute | solution.py:897
  287.8 10.8 %copy-start.3 = (f32[4,208,512]{2,1,0:T(8,128)S(1)}, f32[4,208,512]{2,1,0:T(8,128)}, u32[]{:S(2)}) copy-start(f32[4,208,512]{2,1,0:T(8,128)} %get-tuple-element.121.rest_4_) | copy-start | bytes 5111812
  287.8 10.7 %collective-permute-start.17 = (bf16[272,256]{1,0:T(8,128)(2,1)S(1)}, bf16[272,256]{1,0:T(8,128)(2,1)S(1)}, u32[]{:S(2)}, u32[]{:S(2)}) collective-permute-start(bf16[272,256]{1,0:T(8,128)(2,1)S(1)} %add_convert_fusion.4), channel_id=1, source_target_pairs={{0,16},{2,18},{4,20},{6,22},{8,24},{10,26},{12,28},{14,30},{16,0},... | collective-permute-start | bytes 417800 | tf_op jit(solution)/shard_map/ppermute | solution.py:897
  298.9 18.8 %copy-start.6 = (bf16[4,208,512]{2,1,0:T(8,128)(2,1)}, bf16[4,208,512]{2,1,0:T(8,128)(2,1)S(1)}, u32[]{:S(2)}) copy-start(bf16[4,208,512]{2,1,0:T(8,128)(2,1)S(1)} %add_convert_fusion.1.own_ref) | copy-start | bytes 2555908
  299.0 18.8 %collective-permute-start.21 = (bf16[4,208,512]{2,1,0:T(8,128)(2,1)S(1)}, bf16[4,208,512]{2,1,0:T(8,128)(2,1)S(1)}, u32[]{:S(2)}, u32[]{:S(2)}) collective-permute-start(bf16[4,208,512]{2,1,0:T(8,128)(2,1)S(1)} %add_convert_fusion.1.own_ref), channel_id=1, source_target_pairs={{0,1},{1,0},{2,3},{3,2},{4,5},{5,4},{6,7},{7,6},{8,9},{9,8},{10,11... | collective-permute-start | bytes 2555912 | tf_op jit(solution)/shard_map/ppermute | solution.py:789
  300.5 5.1 %collective-permute-start.19 = (bf16[272,256]{1,0:T(8,128)(2,1)S(1)}, bf16[272,256]{1,0:T(8,128)(2,1)S(1)}, u32[]{:S(2)}, u32[]{:S(2)}) collective-permute-start(bf16[272,256]{1,0:T(8,128)(2,1)S(1)} %add_convert_fusion.3), channel_id=1, source_target_pairs={{0,8},{2,10},{4,12},{6,14},{8,0},{10,2},{12,4},{14,6},{16,24},{18,... | collective-permute-start | bytes 417800 | tf_op jit(solution)/shard_map/ppermute | solution.py:897
  305.6 7.0 %collective-permute-start.20 = (bf16[544,256]{1,0:T(8,128)(2,1)S(1)}, bf16[544,256]{1,0:T(8,128)(2,1)S(1)}, u32[]{:S(2)}, u32[]{:S(2)}) collective-permute-start(bf16[544,256]{1,0:T(8,128)(2,1)S(1)} %maximum_select_fusion.2), channel_id=1, source_target_pairs={{0,4},{2,6},{4,0},{6,2},{8,12},{10,14},{12,8},{14,10},{16,20},{18,... | collective-permute-start | bytes 835592 | tf_op jit(solution)/shard_map/ppermute | solution.py:897
  317.7 5.4 %collective-permute-start.22 = (bf16[1088,256]{1,0:T(8,128)(2,1)S(1)}, bf16[1088,256]{1,0:T(8,128)(2,1)S(1)}, u32[]{:S(2)}, u32[]{:S(2)}) collective-permute-start(bf16[1088,256]{1,0:T(8,128)(2,1)S(1)} %maximum_select_fusion.1), channel_id=1, source_target_pairs={{0,2},{2,0},{4,6},{6,4},{8,10},{10,8},{12,14},{14,12},{16,18},{18,... | collective-permute-start | bytes 1671176 | tf_op jit(solution)/shard_map/ppermute | solution.py:897
  (4 other events, 3.8 us)
where the time goes:
time: 329 us; the launch traced here: 327 us
  Pallas kernels  146 us (44%)
  waiting for transfers between devices  80.5 us (24%)
  starting transfers between devices  70.6 us (21%)
  local copies, waits for them, and re-layouts  14.9 us (5%)
  other arithmetic  13.2 us (4%)
    ppermute x14, waiting for transfers between devices, other(): return lax.ppermute(v, 'tensor', swap)  52.2 us
    pallas_call x2, Pallas kernels, experts_step(): pl.pallas_call(functools.partial(expert_kernel, parts=parts, half=half, b...  44.9 us
    all_to_all x6, starting transfers between devices, exchange(): lax.all_to_all(rows, 'expert', split_axis=0, concat_axis=0, tiled=True)  39.8 us
    pallas_call x4, Pallas kernels, collect(): pl.pallas_call(functools.partial(collect_kernel, numbers=numbers, half=ha...  28.9 us
    pallas_call x1, Pallas kernels, attend(): pl.pallas_call(functools.partial(attend_kernel, pieces=pieces, own=own),...  22.2 us
    pallas_call x1, Pallas kernels, back(): pl.pallas_call(functools.partial(back_kernel, steps=own // batch, receive...  20 us
    ppermute x14, starting transfers between devices, other(): return lax.ppermute(v, 'tensor', swap)  15.8 us
    ppermute x7, starting transfers between devices, swap_bit(): return lax.ppermute(v, 'expert', [(i, i ^ bit) for i in range(groups)])  14.4 us
  transfers between devices with their start and end apart: 29, of which 16 were waited for; matrix products, arithmetic and copies ran while one was open for 5% of the time, Pallas kernels for 42%

commit v1 on v0

--- a/solution.py
+++ b/solution.py
@@ -166,32 +166,24 @@
     )(rank, cotangent, down, across)
 
 
-def spread_kernel(code_ref, rows_ref, *outs, step, steps):
-    number = pl.program_id(0)
-    value = nn(slot_match(code_ref, number * step, step), rows_ref[...]).astype(BF16)
-    for c, out_ref in enumerate(outs):
-
-        @pl.when(lax.div(number, steps) == c)
-        def _():
-            out_ref[...] = value.reshape(out_ref.shape)
-
-
-def spread(code_row, rows, experts, block, chunks, step=512):
+def spread_kernel(code_ref, rows_ref, out_ref, *, start):
+    step = out_ref.shape[0] * out_ref.shape[1]
+    value = nn(slot_match(code_ref, pl.program_id(0) * step + start, step), rows_ref[...])
+    out_ref[...] = value.astype(BF16).reshape(out_ref.shape)
+
+
+def spread(code_row, rows, experts, block, chunk, step=256):
     count, width = rows.shape
-    step = min(step, experts * block)
-    per, steps = step // block, experts * block // step
-
-    def place(c):
-        return lambda i: (jnp.clip(i - c * steps, 0, steps - 1), 0, 0)
-
+    slots = experts * block
+    per = step // block
     return pl.pallas_call(
-        functools.partial(spread_kernel, step=step, steps=steps),
-        out_shape=(jax.ShapeDtypeStruct((experts, block, width), BF16),) * chunks,
-        grid=(chunks * steps,),
+        functools.partial(spread_kernel, start=chunk * slots),
+        out_shape=jax.ShapeDtypeStruct((experts, block, width), BF16),
+        grid=(slots // step,),
         in_specs=[full((2, count)), full((count, width))],
-        out_specs=tuple(pl.BlockSpec((per, block, width), place(c)) for c in range(chunks)),
+        out_specs=pl.BlockSpec((per, block, width), lambda i: (i, 0, 0)),
         compiler_params=params(),
-        cost_estimate=cost(9),
+        cost_estimate=cost(5),
         name="spread",
     )(code_row, rows)
 
@@ -343,7 +335,7 @@
 
 def expert_kernel(expert_ref, x_ref, cot_ref, wr_ref, *rest, parts, half, block, chunk, begins, ends):
     weights, rest = rest[: len(parts)], rest[len(parts) :]
-    w1, w2, dw1, dw2, out_sum, gin_sum, low1, low2, load_sems, store_sems = rest[-10:]
+    w1, w2, dw1, dw2, out_sum, gin_sum, low1, low2, gates, load_sems, store_sems = rest[-11:]
     shards, _, hidden = w1.shape
     before, rest = ((), rest) if begins else (rest[: 2 * shards], rest[2 * shards + 1 :])
     gin_ref, out_ref = rest[:2]
@@ -423,16 +415,27 @@
         return 0
 
     lax.fori_loop(0, shards * blocks, some_hidden, 0)
-    out, gin = out_sum[...], gin_sum[...]
-    out_ref[...] = (gate * out).astype(BF16).reshape(out_ref.shape)
-    gate_grad = jnp.sum(cot * out, axis=1, keepdims=True)
     down, across = iota((block, width), 0), iota((block, width), 1)
-    for g in range(rows // block):
-        span = slice(g * block, (g + 1) * block)
-        line = jnp.sum(jnp.where(down == across, gate_grad[span], 0.0), axis=0, keepdims=True)
-        high = line.astype(BF16).astype(F32)
-        value = jnp.where(down == half, high, jnp.where(down == half + 1, line - high, gin[span]))
-        gin_ref[span, :] = value.astype(BF16)
+    gates[...] = jnp.broadcast_to(gate, gates.shape)
+    group = min(2, rows // block)
+
+    def some_groups(i, _):
+        at = pl.multiple_of(i * group * block, group * block)
+        span = pl.ds(at, group * block)
+        out = out_sum[span, :]
+        out_ref[pl.ds(i * group, group), 0] = (gates[span, 0:1] * out).astype(BF16).reshape(group, block, width)
+        cot = cot_ref[pl.ds(i * group, group), 0].reshape(group * block, width).astype(F32)
+        gate_grad = jnp.sum(cot * out, axis=1, keepdims=True)
+        for g in range(group):
+            rows_of_one = pl.ds(at + g * block, block)
+            line = jnp.where(down == across, gate_grad[g * block : (g + 1) * block], 0.0)
+            line = jnp.sum(line, axis=0, keepdims=True)
+            high = line.astype(BF16).astype(F32)
+            value = jnp.where(down == half + 1, line - high, gin_sum[rows_of_one, :])
+            gin_ref[rows_of_one, :] = jnp.where(down == half, high, value).astype(BF16)
+        return 0
+
+    lax.fori_loop(0, rows // (group * block), some_groups, 0)
     for s in range(shards):
         for c in range(blocks):
             for copy in stores(s, c):
@@ -487,6 +490,7 @@
                 pltpu.VMEM((rows, width), F32),
                 pltpu.VMEM(low or (width, hidden), BF16),
                 pltpu.VMEM(low or (hidden, width), BF16),
+                pltpu.VMEM((rows, 128), F32),
                 pltpu.SemaphoreType.DMA((len(weights) + 2 * shards,)),
                 pltpu.SemaphoreType.DMA((2 * shards * hidden // min(chunk, hidden),)),
             ],
@@ -575,14 +579,26 @@
     (sum_ref, gp_ref), rest = rest[:2], rest[2:]
     more, rest = rest[: 2 * received], rest[2 * received :]
     (res_ref, cot_ref, tok_ref, ga_ref, gm_ref, wrt_ref, wq, wo, qkv_ref, prob_ref, att_ref), rest = rest[:11], rest[11:]
-    gtok_ref, pack_ref, dwq, dwo, small, gatt_all, dqkv_all = rest
+    gtok_ref, pack_ref, dwq, dwo, small, gatt_all, dqkv_all, wq_here, qkv_here, prob_here, sems = rest
     experts = wrt_ref.shape[0]
     batch, _, model = res_ref.shape
     rows = batch * PAD
     step = pl.program_id(0)
 
+    def loads(number):
+        span = pl.ds(number * batch, batch)
+        pairs = [(v.at[span], w.at[span]) for v, w in ((qkv_ref, qkv_here), (prob_ref, prob_here))]
+        return [pltpu.make_async_copy(a, b, sems.at[number, k]) for k, (a, b) in enumerate(pairs)]
+
+    weights = pltpu.make_async_copy(wq, wq_here, sems.at[0, 2])
+
     @pl.when(step == 0)
     def _():
+        for copy in loads(0) + [weights]:
+            copy.start()
+        for number in range(1, steps):
+            for copy in loads(number):
+                copy.start()
         for ref in (dwq, dwo, small):
             ref[...] = jnp.zeros_like(ref)
 
@@ -619,15 +635,22 @@
     gatt_all[...] = nt(grad_mixed, wo[...]).astype(BF16)
 
     masks = quad_masks()
-
-    def one_image(b, _):
-        span = pl.ds(pl.multiple_of(b * PAD, PAD), PAD)
+    for number in range(steps):
+
+        @pl.when(step == number)
+        def _():
+            for copy in loads(number):
+                copy.wait()
+
+    for b in range(batch):
+        span = slice(b * PAD, (b + 1) * PAD)
+        image = step * batch + b
         for quad in range(model // QUAD):
             q, k, v = (
-                qkv_ref[b, :, j * model + quad * QUAD : j * model + (quad + 1) * QUAD] for j in range(3)
+                qkv_here[image, :, j * model + quad * QUAD : j * model + (quad + 1) * QUAD] for j in range(3)
             )
             grad_heads = stacked(gatt_all[span, quad * QUAD : (quad + 1) * QUAD], masks)
-            low_probs = prob_ref[b, quad]
+            low_probs = prob_here[image, quad]
             p = low_probs.astype(F32)
             gw = nt(grad_heads, v)
             ds = (p * (gw - jnp.sum(p * gw, axis=1, keepdims=True))).astype(BF16)
@@ -636,9 +659,7 @@
             grad_v = tn(low_probs, grad_heads)
             for j, value in enumerate((grad_q, grad_k, grad_v)):
                 dqkv_all[span, j * model + quad * QUAD : j * model + (quad + 1) * QUAD] = value.astype(BF16)
-        return 0
-
-    lax.fori_loop(0, batch, one_image, 0)
+
     tok = flat(tok_ref)
     center = tok - row_mean(tok)
     tok_scale = lax.rsqrt(row_mean(center * center) + EPS)
@@ -646,7 +667,12 @@
     ga = ga_ref[...]
     normed = (xin * ga).astype(BF16)
     dwq[...] += tn(normed, dqkv_all[...])
-    grad_normed = nt(dqkv_all[...], wq[...])
+
+    @pl.when(step == 0)
+    def _():
+        weights.wait()
+
+    grad_normed = nt(dqkv_all[...], wq_here[...])
     small[experts : experts + 1, :] += jnp.sum(grad_normed * xin, axis=0, keepdims=True)
     h = grad_normed * ga
     grad_tok = grad_res + tok_scale * (h - row_mean(h) - xin * row_mean(h * xin))
@@ -704,10 +730,10 @@
                 full((1, width)),
                 full((1, width)),
                 full((experts, width)),
-                full(wq.shape),
+                pl.BlockSpec(memory_space=pl.ANY),
                 full(wo.shape),
-                mine(*qkv.shape[1:]),
-                mine(*probs.shape[1:]),
+                pl.BlockSpec(memory_space=pl.ANY),
+                pl.BlockSpec(memory_space=pl.ANY),
                 mine(*att.shape[1:]),
             ],
             out_specs=(mine(PAD, width), full((shards, rows, 256))),
@@ -717,6 +743,10 @@
                 pltpu.VMEM((small_rows(experts), width), F32),
                 pltpu.VMEM((batch * PAD, width), BF16),
                 pltpu.VMEM((batch * PAD, 3 * width), BF16),
+                pltpu.VMEM(wq.shape, BF16),
+                pltpu.VMEM(qkv.shape, BF16),
+                pltpu.VMEM(probs.shape, BF16),
+                pltpu.SemaphoreType.DMA((own // batch, 3)),
             ],
         ),
         compiler_params=params(),
@@ -739,35 +769,32 @@
     )
 
 
-def unpad_kernel(first_ref, own_ref, peer_ref, out_ref, wide, *, images):
-    own = own_ref.shape[0]
-
-    def one_image(i, _):
-        inner = lax.rem(i, own)
+def unpad_kernel(first_ref, *refs, images):
+    out_ref, wide = refs[-2:]
+    pieces = len(refs) // 2 - 1
+    parts = refs[:pieces], refs[pieces:-2]
+    own, peer = ([(ref, i) for ref in part for i in range(ref.shape[0])] for part in parts)
+    for i in range(images):
+        inner = i % len(own)
         mine = first_ref[0] == i - inner
-        value = jnp.where(mine, own_ref[inner].astype(F32), peer_ref[inner].astype(F32))
-        off = lax.rem(i * SEQ, 8)
-        span = pl.ds(pl.multiple_of(i * SEQ - off, 8), PAD + 8)
-        value = pltpu.roll(jnp.concatenate([value, jnp.zeros((8, value.shape[1]), F32)], axis=0), off, 0)
-        wide[span, :] = jnp.where(iota(value.shape, 0) < off, wide[span, :], value)
-        return 0
-
-    lax.fori_loop(0, images, one_image, 0)
+        (own_ref, k), (peer_ref, _) = own[inner], peer[inner]
+        value = jnp.where(mine, own_ref[k], peer_ref[k]).astype(F32)
+        wide[i * SEQ : (i + 1) * SEQ, :] = value[:SEQ]
     out_ref[...] = wide[0 : images * SEQ, :].astype(out_ref.dtype)
 
 
 def unpad(first, own, peer, dtype):
-    images, width = 2 * own.shape[0], own.shape[2]
+    images, width = 2 * sum(v.shape[0] for v in own), own[0].shape[2]
     return pl.pallas_call(
         functools.partial(unpad_kernel, images=images),
         out_shape=jax.ShapeDtypeStruct((images * SEQ, width), dtype),
-        in_specs=[pl.BlockSpec(memory_space=pltpu.SMEM), VMEM, VMEM],
+        in_specs=[pl.BlockSpec(memory_space=pltpu.SMEM)] + [VMEM] * (2 * len(own)),
         out_specs=VMEM,
         scratch_shapes=[wide_scratch(images, width)],
         compiler_params=params(),
         cost_estimate=cost(2),
         name="unpad",
-    )(first, own, peer)
+    )(first, *own, *peer)
 
 
 def body(tokens, routes, gain_attn, w_qkv, w_attn_out, gain_moe, w_router, w_expert_in, w_expert_out, cotangent, *, ways, groups):
@@ -833,9 +860,9 @@
         w2_rest = other(after(w_expert_out[0, cut:], wq[-1], wo[-1]))
     place = jnp.stack([rank * own, core]).astype(jnp.int32)
     routed, residual, qkv, probs, att, wq, wo = attend(place, tok_pad, gain_attn, gain_moe, wq, wo, own)
-    sent, x_slots = spread(code_row, rows_of(routed), experts, block, chunks), []
+    x_slots = []
     for c in range(chunks):
-        rows = sent[c]
+        rows = spread(code_row, rows_of(routed), experts, block, c)
         if c == 0:
             rows, cot_slots = lax.optimization_barrier((rows, cot_slots))
             if ways == 2:
@@ -861,7 +888,7 @@
     if ways == 2:
         there = ((1 - rank) * own).astype(jnp.int32).reshape(1)
         dw1_peer = other(dw[1])
-        cut = dw[3].shape[0] // 4
+        cut = 3 * dw[3].shape[0] // 16
         dw2_peer = [other(dw[3][:cut])]
         zero = jnp.zeros((1,), jnp.int32)
         start = collect(zero, code_col, gin[:1], images, F32, half, block, True, (0,))
@@ -915,11 +942,20 @@
         for bit in bits[:2]:
             keep, give = halves(pack, bit)
             pack = add(keep, swap_bit(give, bit))
-        pack, grad_peer, mix_there, mix_here, grad_w2 = lax.optimization_barrier(
-            (pack, grad_peer, mix_there, mix_here, dw[2] + jnp.concatenate(dw2_peer).astype(F32))
+        pack, mix_there, grad_peer = lax.optimization_barrier((pack, mix_there, grad_peer))
+        mix_peer = other(mix_there)
+        keep, give = halves(pack, bits[2])
+        pack = add(keep, swap_bit(give, bits[2]))
+        grad_tokens = unpad(first, [grad_tok], [grad_peer], F32)
+        keep, give = halves(pack, bits[3])
+        pack, grad_w2, mix_here = lax.optimization_barrier(
+            (add(keep, swap_bit(give, bits[3])), dw[2] + jnp.concatenate(dw2_peer).astype(F32), mix_here)
         )
+        pack, mix_peer, grad_tokens = lax.optimization_barrier((pack, mix_peer, grad_tokens))
         swapped = other(pack[1])
-        mix_peer = other(after(mix_there, pack))
+        result = (residual + (mix_here.astype(F32) + mix_peer.astype(F32))).astype(BF16)
+        swapped, result = lax.optimization_barrier((swapped, result))
+        result_peer = other(result)
         total = add(pack[0], swapped)
 
         def gathered(v, bit):
@@ -927,20 +963,11 @@
             upper = (expert // bit) % 2 == 1
             return jnp.where(upper, jnp.concatenate([got, v]), jnp.concatenate([v, got]))
 
-        grad_tokens = unpad(first, grad_tok, grad_peer, F32)
-        keep, give = halves(total, bits[2])
-        total = add(keep, swap_bit(give, bits[2]))
-        total = add(total, swap_bit(total, bits[3]))
-        total, grad_tokens = lax.optimization_barrier((total, grad_tokens))
-        total, mix_peer = lax.optimization_barrier((total, mix_peer))
-        result = (residual + (mix_here.astype(F32) + mix_peer.astype(F32))).astype(BF16)
-        result_peer = other(result)
-        total, result = lax.optimization_barrier((total, result))
-        for bit in bits[2:0:-1]:
+        for bit in bits[3:1:-1]:
             total = gathered(total, bit)
+        total = gathered(total, bits[1])
         total, result_peer = lax.optimization_barrier((total, result_peer))
         total = gathered(total, bits[0])
-        result = unpad(first, result, result_peer, BF16)
         total = total.astype(F32)
         part = w_qkv.shape[2]
     else:
@@ -968,17 +995,10 @@
     if ways != 2:
         grad_w_qkv = lax.dynamic_slice_in_dim(grad_w_qkv, rank * w_qkv.shape[2], w_qkv.shape[2], 2)
         grad_w_attn_out = lax.dynamic_slice_in_dim(grad_w_attn_out, rank * w_qkv.shape[2], w_qkv.shape[2], 0)
-    return (
-        result,
-        grad_tokens,
-        small[experts],
-        grad_w_qkv,
-        grad_w_attn_out,
-        small[experts + 1],
-        small[:experts].T,
-        grad_w1[None],
-        grad_w2[None],
-    )
+    sums = (small[experts], grad_w_qkv, grad_w_attn_out, small[experts + 1], small[:experts].T)
+    if ways == 2:
+        result = unpad(first, [result], [result_peer], BF16)
+    return (result, grad_tokens, *sums, grad_w1[None], grad_w2[None])
 
 
 def solution(mesh):

time: 329 us -> 326 us (level)
  waiting for transfers between devices: 80.5 us -> 77.2 us
    ppermute x14, waiting for transfers between devices: 52.2 us -> 40.5 us  [other(): return lax.ppermute(v, 'tensor', swap)]
    ppermute x7 -> x8, waiting for transfers between devices: 12.7 us -> 21.1 us  [swap_bit(): return lax.ppermute(v, 'expert', [(i, i ^ bit) for i in range(groups)])]
    ppermute x7 -> x8, starting transfers between devices: 14.4 us -> 10.9 us  [swap_bit(): return lax.ppermute(v, 'expert', [(i, i ^ bit) for i in range(groups)])]
    pallas_call x1 -> x2, Pallas kernels: 7.26 us -> 9.73 us  [spread(): pl.pallas_call(functools.partial(spread_kernel, start=chunk * slots), out...]
  transfers between devices with their start and end apart: 29 -> 30, of which waited for: 16 -> 19; matrix products, arithmetic and copies ran while one was open for 5% -> 6% of each run, Pallas kernels for 42% -> 42%
where the time goes in v1:
time: 326 us; the launch traced here: 325 us
  Pallas kernels  145 us (44%)
  waiting for transfers between devices  77.2 us (24%)
  starting transfers between devices  69.8 us (21%)
  local copies, waits for them, and re-layouts  16.9 us (5%)
  other arithmetic  15.1 us (5%)
    pallas_call x2, Pallas kernels, experts_step(): pl.pallas_call(functools.partial(expert_kernel, parts=parts, half=half, b...  45 us
    all_to_all x6, starting transfers between devices, exchange(): lax.all_to_all(rows, 'expert', split_axis=0, concat_axis=0, tiled=True)  40.8 us
    ppermute x14, waiting for transfers between devices, other(): return lax.ppermute(v, 'tensor', swap)  40.5 us
    pallas_call x4, Pallas kernels, collect(): pl.pallas_call(functools.partial(collect_kernel, numbers=numbers, half=ha...  28.9 us
    pallas_call x1, Pallas kernels, attend(): pl.pallas_call(functools.partial(attend_kernel, pieces=pieces, own=own),...  22.2 us
    ppermute x8, waiting for transfers between devices, swap_bit(): return lax.ppermute(v, 'expert', [(i, i ^ bit) for i in range(groups)])  21.1 us
    pallas_call x1, Pallas kernels, back(): pl.pallas_call(functools.partial(back_kernel, steps=own // batch, receive...  18.5 us
    ppermute x14, starting transfers between devices, other(): return lax.ppermute(v, 'tensor', swap)  17.6 us
  transfers between devices with their start and end apart: 30, of which 19 were waited for; matrix products, arithmetic and copies ran while one was open for 6% of the time, Pallas kernels for 42%

profile of v1, /device:TPU:0, one launch (start us, length us, event | category | flops | bytes accessed | tf_op | source)
XLA Modules:
  0.0 325.1 jit_solution(1140357144414601600)
XLA Ops:
  3.0 9.6 %front.1 = (bf16[8,208,512]{2,1,0:T(8,128)(2,1)}, bf16[16,2,64,512]{3,2,1,0:T(8,128)(2,1)}, s32[208,16]{1,0:T(8,128)}, s32[2,1664]{1,0:T(2,128)}) custom-call(s32[1]{0:T(128)} %bitcast.1.rank_ref, bf16[1576,512]{1,0:T(8,128)(2,1)} %cot_ref.1, s32[208,16]{1,0:T(8,128)} %copy.25.col_ref, s32[2,1664]{1,0:T(2,128)} %bitcast.64), custom_call_target="tpu_custom_call" | custom-call | bytes 36900000 | tf_op jit(solution)/shard_map/front/pallas_call | solution.py:152
  12.5 7.5 %all-to-all-start.1 = ((bf16[16,2,64,512]{3,2,1,0:T(8,128)(2,1)}), bf16[16,2,64,512]{3,2,1,0:T(8,128)(2,1)S(1)}, u32[]{:S(2)}, u32[]{:S(2)}) async-start(bf16[16,2,64,512]{3,2,1,0:T(8,128)(2,1)} %get-tuple-element.80), calls=%async_computation.1 | async-start | bytes 4194304 | tf_op jit(solution)/shard_map/all_to_all | solution.py:824
  20.2 1.6 collective-permute-start
  22.4 4.2 %pad.73.tok_ref.rest_6_ = bf16[8,208,512]{2,1,0:T(8,128)(2,1)} custom-call(bf16[1576,512]{1,0:T(8,128)(2,1)} %source), custom_call_target="tpu_custom_call" | custom-call | bytes 7380000 | tf_op jit(solution)/shard_map/pad/pallas_call | solution.py:66
  26.6 7.9 %collective-permute-done.1.rest_4_ = bf16[128,512]{1,0:T(8,128)(2,1)S(1)} collective-permute-done((bf16[128,512]{1,0:T(8,128)(2,1)S(1)}, bf16[128,512]{1,0:T(8,128)(2,1)S(1)}, u32[]{:S(2)}, u32[]{:S(2)}) %collective-permute-start.1) | collective-permute-done | bytes 131104 | tf_op jit(solution)/shard_map/ppermute | solution.py:816
  36.4 1.5 collective-permute-start.5
  39.9 22.2 %attend.1 = (bf16[8,208,512]{2,1,0:T(8,128)(2,1)}, f32[4,208,512]{2,1,0:T(8,128)}, bf16[4,208,1536]{2,1,0:T(8,128)(2,1)}, bf16[4,2,832,208]{3,2,1,0:T(8,128)(2,1...) custom-call(s32[2]{0:T(128)} %pad_add_fusion.place_ref, ...), custom_call_target="tpu_custom_call" | custom-call | bytes 92250000 | tf_op jit(solution)/shard_map/attend/pallas_call | solution.py:301
  62.1 4.9 %spread.3 = bf16[16,64,512]{2,1,0:T(8,128)(2,1)} custom-call(s32[2,1664]{1,0:T(2,128)} %get-tuple-element.79.code_ref, bf16[1664,512]{1,0:T(8,128)(2,1)} %bitcast.53), custom_call_target="tpu_custom_call" | custom-call | bytes 18450000 | tf_op jit(solution)/shard_map/spread/pallas_call | solution.py:179
  67.5 5.8 %all-to-all-start.2 = ((bf16[16,64,512]{2,1,0:T(8,128)(2,1)}), bf16[16,64,512]{2,1,0:T(8,128)(2,1)}, u32[]{:S(2)}, u32[]{:S(2)}) async-start(bf16[16,64,512]{2,1,0:T(8,128)(2,1)} %spread.3), calls=%async_computation.2 | async-start | bytes 2097152 | tf_op jit(solution)/shard_map/all_to_all | solution.py:824
  73.4 1.6 collective-permute-start.4
  74.9 4.8 %spread.2 = bf16[16,64,512]{2,1,0:T(8,128)(2,1)} custom-call(s32[2,1664]{1,0:T(2,128)} %get-tuple-element.79.code_ref, bf16[1664,512]{1,0:T(8,128)(2,1)} %bitcast.54), custom_call_target="tpu_custom_call" | custom-call | bytes 18450000 | tf_op jit(solution)/shard_map/spread/pallas_call | solution.py:179
  79.8 13.5 %collective-permute-done.4.rest_4_ = bf16[768,512]{1,0:T(8,128)(2,1)S(1)} collective-permute-done((bf16[768,512]{1,0:T(8,128)(2,1)S(1)}, bf16[768,512]{1,0:T(8,128)(2,1)S(1)}, u32[]{:S(2)}, u32[]{:S(2)}) %collective-permute-start.4) | collective-permute-done | bytes 786464 | tf_op jit(solution)/shard_map/ppermute | solution.py:816
  93.2 3.0 all-to-all-done.2
  96.3 6.9 %all-to-all-start = ((bf16[16,64,512]{2,1,0:T(8,128)(2,1)}), bf16[16,64,512]{2,1,0:T(8,128)(2,1)S(1)}, u32[]{:S(2)}, u32[]{:S(2)}) async-start(bf16[16,64,512]{2,1,0:T(8,128)(2,1)} %spread.2), calls=%async_computation | async-start | bytes 2097152 | tf_op jit(solution)/shard_map/all_to_all | solution.py:824
  103.9 22.0 %experts.2 = (bf16[1024,512]{1,0:T(8,128)(2,1)}, bf16[16,2,64,512]{3,2,1,0:T(8,128)(2,1)}, f32[512,1024]{1,0:T(8,128)}, f32[512,1024]{1,0:T(8,128)}, f32[1024,512]{1,0:T(8,128)}, /*index=5*/f32[1024,512]{1,0:T(8,128)}) custom-call(s32[1]{0:T(128)} %bitcast.4.expert_ref, bf16[1024,512]{1,0:T(8,128)(2,1)} %bitcast.14.x_ref, bf16[16,2,64,512]{3,2,1,0:T(8,128)(2,1)} %copy-done, ...), custom_call_target="tpu_custom_call" | custom-call | bytes 73800000 | tf_op jit(solution)/shard_map/experts/pallas_call | solution.py:465
  127.1 6.9 %all-to-all-start.4 = ((bf16[16,64,512]{2,1,0:T(8,128)(2,1)}), bf16[16,64,512]{2,1,0:T(8,128)(2,1)S(1)}, u32[]{:S(2)}, u32[]{:S(2)}) async-start(bf16[16,64,512]{2,1,0:T(8,128)(2,1)} %bitcast.62), calls=%async_computation.4 | async-start | bytes 2097152 | tf_op jit(solution)/shard_map/all_to_all | solution.py:824
  133.9 23.0 %experts.3 = (bf16[1024,512]{1,0:T(8,128)(2,1)}, bf16[16,2,64,512]{3,2,1,0:T(8,128)(2,1)}, f32[512,1024]{1,0:T(8,128)}, bf16[512,1024]{1,0:T(8,128)(2,1)}, f32[1...) custom-call(s32[1]{0:T(128)} %bitcast.4.expert_ref, bf16[1024,512]{1,0:T(8,128)(2,1)} %bitcast.58, ...), custom_call_target="tpu_custom_call", output_to_operand_aliasing={{1}: (13, {})} | custom-call | bytes 73800000 | tf_op jit(solution)/shard_map/experts/pallas_call | solution.py:465
  156.9 6.8 %all-to-all-start.3 = ((bf16[16,64,512]{2,1,0:T(8,128)(2,1)}), bf16[16,64,512]{2,1,0:T(8,128)(2,1)S(1)}, u32[]{:S(2)}, u32[]{:S(2)}) async-start(bf16[16,64,512]{2,1,0:T(8,128)(2,1)} %bitcast.61), calls=%async_computation.3 | async-start | bytes 2097152 | tf_op jit(solution)/shard_map/all_to_all | solution.py:824
  163.8 1.6 collective-permute-start.9
  166.9 8.9 %collect.4 = (f32[8,208,512]{2,1,0:T(8,128)}, f32[8,16,208]{2,1,0:T(8,128)}) custom-call(s32[1]{0:T(128)} %constant.104.clone.1.first_ref, s32[208,16]{1,0:T(8,128)} %get-tuple-element.78.code_ref, bf16[1024,512]{1,0:T(8,128)(2,1)} %bitcast.55), custom_call_target="tpu_custom_call" | custom-call | bytes 25830000 | tf_op jit(solution)/shard_map/collect/pallas_call | solution.py:558
  175.8 10.9 %all-to-all-done.3 = bf16[16,64,512]{2,1,0:T(8,128)(2,1)S(1)} async-done(((bf16[16,64,512]{2,1,0:T(8,128)(2,1)}), bf16[16,64,512]{2,1,0:T(8,128)(2,1)S(1)}, u32[]{:S(2)}, u32[]{:S(2)}) %all-to-all-start.3) | async-done | bytes 1048608 | tf_op jit(solution)/shard_map/all_to_all | solution.py:824
  187.7 5.9 %collect.6 = (bf16[4,208,512]{2,1,0:T(8,128)(2,1)}, f32[4,16,208]{2,1,0:T(8,128)}) custom-call(s32[1]{0:T(128)} %bitcast.19.first_ref, s32[208,16]{1,0:T(8,128)} %get-tuple-element.78.code_ref, bf16[1024,512]{1,0:T(8,128)(2,1)} %bitcast.49, f32[8,208,512]{2,1,0:T(8,128)} %get-tuple-element.106.rest_1_, f32[8,16,208]{2,1,0:T(8,128)} %get-tuple-element.107.rest_2_), custom_call_target="tpu_custom_call" | custom-call | bytes 25830000 | tf_op jit(solution)/shard_map/collect/pallas_call | solution.py:558
  193.7 6.9 %all-to-all-start.5 = ((bf16[16,2,64,512]{3,2,1,0:T(8,128)(2,1)}), bf16[16,2,64,512]{3,2,1,0:T(8,128)(2,1)S(1)}, u32[]{:S(2)}, u32[]{:S(2)}) async-start(bf16[16,2,64,512]{3,2,1,0:T(8,128)(2,1)} %get-tuple-element.126), calls=%async_computation.5 | async-start | bytes 4194304 | tf_op jit(solution)/shard_map/all_to_all | solution.py:824
  200.6 1.6 collective-permute-start.7
  203.7 3.6 %convert_add_fusion.1 = f32[512,1024]{1,0:T(8,128)} fusion(f32[512,1024]{1,0:T(8,128)} %get-tuple-element.112, bf16[512,1024]{1,0:T(8,128)(2,1)} %collective-permute-done.9), kind=kLoop, calls=%fused_computation.2 | loop fusion | flops 1048576 | bytes 5242880 | tf_op jit(solution)/shard_map/add | solution.py:900
  207.3 5.9 %collect.5 = (f32[4,208,512]{2,1,0:T(8,128)}, f32[4,16,208]{2,1,0:T(8,128)}) custom-call(s32[1]{0:T(128)} %bitcast.first_ref, s32[208,16]{1,0:T(8,128)} %get-tuple-element.78.code_ref, bf16[1024,512]{1,0:T(8,128)(2,1)} %bitcast.50, f32[8,208,512]{2,1,0:T(8,128)} %get-tuple-element.106.rest_1_, f32[8,16,208]{2,1,0:T(8,128)} %get-tuple-element.107.rest_2_), custom_call_target="tpu_custom_call" | custom-call | bytes 25830000 | tf_op jit(solution)/shard_map/collect/pallas_call | solution.py:558
  213.2 10.4 %collective-permute-done.8.rest_3_ = f32[4,16,208]{2,1,0:T(8,128)S(1)} collective-permute-done((f32[4,16,208]{2,1,0:T(8,128)S(1)}, f32[4,16,208]{2,1,0:T(8,128)S(1)}, u32[]{:S(2)}, u32[]{:S(2)}) %collective-permute-start.8) | collective-permute-done | bytes 53280 | tf_op jit(solution)/shard_map/ppermute | solution.py:816
  224.5 1.5 collective-permute-start.11
  226.0 18.5 %back.1 = (bf16[4,208,512]{2,1,0:T(8,128)(2,1)}, bf16[2,2176,256]{2,1,0:T(8,128)(2,1)}) custom-call(s32[1]{0:T(128)} %bitcast.first_ref, f32[4,208,512]{2,1,0:T(8,128)} %get-tuple-element.108.rest_0_, f32[4,16,208]{2,1,0:T(8,128)} %get-tuple-element.109.rest_1_, bf16[4,208,512]{2,1,0:T(8,128)(2,1)} %copy-done.13, f32[4,16,208]{2,1,0:T(8,128)} %copy-done.19, ...), custom_call_target="tpu_custom_call" | custom-call | bytes 59040000 | tf_op jit(solution)/shard_map/back/pallas_call | solution.py:716
  247.5 1.6 collective-permute-start.14
  250.4 1.9 add_convert_fusion
  255.9 8.2 %collect.7 = bf16[8,208,512]{2,1,0:T(8,128)(2,1)} custom-call(s32[1]{0:T(128)} %constant.104.clone.1.first_ref, s32[208,16]{1,0:T(8,128)} %get-tuple-element.78.code_ref, bf16[1024,512]{1,0:T(8,128)(2,1)} %bitcast.57, bf16[1024,512]{1,0:T(8,128)(2,1)} %bitcast.56), custom_call_target="tpu_custom_call" | custom-call | bytes 25830000 | tf_op jit(solution)/shard_map/collect/pallas_call | solution.py:558
  264.1 2.5 constant_dynamic-slice_fusion
  266.5 1.5 collective-permute-done.13
  269.3 3.6 %collective-permute-start.15 = (bf16[2,272,256]{2,1,0:T(8,128)(2,1)S(1)}, bf16[2,272,256]{2,1,0:T(8,128)(2,1)S(1)}, u32[]{:S(2)}, u32[]{:S(2)}) collective-permute-start(bf16[2,272,256]{2,1,0:T(8,128)(2,1)S(1)} %constant_dynamic-slice_fusion.2), channel_id=1, source_target_pairs={{0,8},{2,10},{4,12},{6,14},{8,0},{10,2},{12,4},{14,6},{16,24},{18,... | collective-permute-start | bytes 835592 | tf_op jit(solution)/shard_map/ppermute | solution.py:924
  272.9 1.5 collective-permute-start.17
  274.4 5.1 %collective-permute-done.15 = bf16[2,272,256]{2,1,0:T(8,128)(2,1)S(1)} collective-permute-done((bf16[2,272,256]{2,1,0:T(8,128)(2,1)S(1)}, bf16[2,272,256]{2,1,0:T(8,128)(2,1)S(1)}, u32[]{:S(2)}, u32[]{:S(2)}) %collective-permute-start.15) | collective-permute-done | bytes 278560 | tf_op jit(solution)/shard_map/ppermute | solution.py:924
  279.7 2.8 collective-permute-start.16
  282.5 3.4 %convert_add_fusion = f32[1024,512]{1,0:T(8,128)} fusion(f32[1024,512]{1,0:T(8,128)} %get-tuple-element.132, bf16[832,512]{1,0:T(8,128)(2,1)} %copy-done.11, bf16[192,512]{1,0:T(8,128)(2,1)S(1)} %collective-permute-done.10), kind=kLoop, calls=%fused_computation.1 | loop fusion | flops 2621440 | bytes 5242880 | tf_op jit(solution)/shard_map/add | solution.py:952
  285.9 3.8 %unpad.2 = f32[1576,512]{1,0:T(8,128)} custom-call(s32[1]{0:T(128)} %bitcast.first_ref, bf16[4,208,512]{2,1,0:T(8,128)(2,1)} %get-tuple-element.130.refs_0_, bf16[4,208,512]{2,1,0:T(8,128)(2,1)} %collective-permute-done.14.refs_1_), custom_call_target="tpu_custom_call" | custom-call | bytes 7380000 | tf_op jit(solution)/shard_map/unpad/pallas_call | solution.py:788
  289.8 3.7 %collective-permute-done.17 = bf16[4,208,512]{2,1,0:T(8,128)(2,1)S(1)} collective-permute-done((bf16[4,208,512]{2,1,0:T(8,128)(2,1)}, bf16[4,208,512]{2,1,0:T(8,128)(2,1)S(1)}, u32[]{:S(2)}, u32[]{:S(2)}) %collective-permute-start.17) | collective-permute-done | bytes 852000 | tf_op jit(solution)/shard_map/ppermute | solution.py:816
  293.5 1.5 collective-permute-start.18
  295.4 2.4 collective-permute-done.18
  297.9 1.5 collective-permute-start.19
  300.9 3.0 collective-permute-done.19
  304.0 5.0 %collective-permute-done.20 = bf16[272,256]{1,0:T(8,128)(2,1)S(1)} collective-permute-done((bf16[272,256]{1,0:T(8,128)(2,1)S(1)}, bf16[272,256]{1,0:T(8,128)(2,1)S(1)}, u32[]{:S(2)}, u32[]{:S(2)}) %collective-permute-start.20) | collective-permute-done | bytes 139296 | tf_op jit(solution)/shard_map/ppermute | solution.py:924
  310.6 5.2 %collective-permute-done.21 = bf16[544,256]{1,0:T(8,128)(2,1)S(1)} collective-permute-done((bf16[544,256]{1,0:T(8,128)(2,1)S(1)}, bf16[544,256]{1,0:T(8,128)(2,1)S(1)}, u32[]{:S(2)}, u32[]{:S(2)}) %collective-permute-start.21) | collective-permute-done | bytes 278560 | tf_op jit(solution)/shard_map/ppermute | solution.py:924
  318.3 3.1 unpad.3
  (112 shorter events, 33.4 us)
Async XLA Ops:
  12.5 7.6 %copy-start.8 = (bf16[3,512,256]{2,1,0:T(8,128)(2,1)S(1)}, bf16[3,512,256]{2,1,0:T(8,128)(2,1)}, u32[]{:S(2)}) copy-start(bf16[3,512,256]{2,1,0:T(8,128)(2,1)} %rest_0_.1) | copy-start | bytes 2359300
  12.5 9.2 %copy-start.14 = (bf16[256,512]{1,0:T(8,128)(2,1)S(1)}, bf16[256,512]{1,0:T(8,128)(2,1)}, u32[]{:S(2)}) copy-start(bf16[256,512]{1,0:T(8,128)(2,1)} %rest_3_.1) | copy-start | bytes 786436
  12.5 54.5 %all-to-all-start.1 = ((bf16[16,2,64,512]{3,2,1,0:T(8,128)(2,1)}), bf16[16,2,64,512]{3,2,1,0:T(8,128)(2,1)S(1)}, u32[]{:S(2)}, u32[]{:S(2)}) async-start(bf16[16,2,64,512]{3,2,1,0:T(8,128)(2,1)} %get-tuple-element.80), calls=%async_computation.1 | async-start | bytes 4194304 | tf_op jit(solution)/shard_map/all_to_all | solution.py:824
  20.2 14.3 %collective-permute-start = (bf16[3,512,128]{2,1,0:T(8,128)(2,1)S(1)}, bf16[3,512,128]{2,1,0:T(8,128)(2,1)S(1)}, u32[]{:S(2)}, u32[]{:S(2)}) collective-permute-start(bf16[3,512,128]{2,1,0:T(8,128)(2,1)S(1)} %constant_dynamic-slice_fusion.7), channel_id=1, source_target_pairs={{0,1},{1,0},{2,3},{3,2},{4,5},{5,4},{6,7},{7,6},{8,9},{9,8},{10,11... | collective-permute-start | bytes 1179656 | tf_op jit(solution)/shard_map/ppermute | solution.py:816
  21.8 16.2 %copy-start.2 = (bf16[1,1024,512]{2,1,0:T(8,128)(2,1)S(1)}, bf16[1,1024,512]{2,1,0:T(8,128)(2,1)}, u32[]{:S(2)}) copy-start(bf16[1,1024,512]{2,1,0:T(8,128)(2,1)} %param.18) | copy-start | bytes 3145732
  21.8 12.7 %collective-permute-start.1 = (bf16[128,512]{1,0:T(8,128)(2,1)S(1)}, bf16[128,512]{1,0:T(8,128)(2,1)S(1)}, u32[]{:S(2)}, u32[]{:S(2)}) collective-permute-start(bf16[128,512]{1,0:T(8,128)(2,1)S(1)} %constant_dynamic-slice_fusion.6), channel_id=1, source_target_pairs={{0,1},{1,0},{2,3},{3,2},{4,5},{5,4},{6,7},{7,6},{8,9},{9,8},{10,11... | collective-permute-start | bytes 393224 | tf_op jit(solution)/shard_map/ppermute | solution.py:816
  34.5 5.5 %copy-start.17 = (bf16[128,512]{1,0:T(8,128)(2,1)}, bf16[128,512]{1,0:T(8,128)(2,1)S(1)}, u32[]{:S(2)}) copy-start(bf16[128,512]{1,0:T(8,128)(2,1)S(1)} %collective-permute-done.1.rest_4_) | copy-start | bytes 393220
  34.5 3.5 %copy-start.15 = (bf16[3,512,128]{2,1,0:T(8,128)(2,1)}, bf16[3,512,128]{2,1,0:T(8,128)(2,1)S(1)}, u32[]{:S(2)}) copy-start(bf16[3,512,128]{2,1,0:T(8,128)(2,1)S(1)} %collective-permute-done.rest_1_) | copy-start | bytes 1179652
  34.5 2.0 collective-permute-start.2
  34.5 1.9 collective-permute-start.3
  36.4 1.6 copy-start.18
  36.4 2.3 copy-start.16
  36.4 31.0 %collective-permute-start.5 = (bf16[512,1024]{1,0:T(8,128)(2,1)}, bf16[512,1024]{1,0:T(8,128)(2,1)}, u32[]{:S(2)}, u32[]{:S(2)}) collective-permute-start(bf16[512,1024]{1,0:T(8,128)(2,1)} %bitcast.11.rest_0_), channel_id=1, source_target_pairs={{0,1},{1,0},{2,3},{3,2},{4,5},{5,4},{6,7},{7,6},{8,9},{9,8},{10,11... | collective-permute-start | bytes 3145736 | tf_op jit(solution)/shard_map/ppermute | solution.py:816
  38.7 28.8 %collective-permute-start.6 = (bf16[256,512]{1,0:T(8,128)(2,1)}, bf16[256,512]{1,0:T(8,128)(2,1)S(1)}, u32[]{:S(2)}, u32[]{:S(2)}) collective-permute-start(bf16[256,512]{1,0:T(8,128)(2,1)} %slice_bitcast_fusion.4), channel_id=1, source_target_pairs={{0,1},{1,0},{2,3},{3,2},{4,5},{5,4},{6,7},{7,6},{8,9},{9,8},{10,11... | collective-permute-start | bytes 786440 | tf_op jit(solution)/shard_map/ppermute | solution.py:816
  67.0 6.3 %copy-start = (bf16[16,2,64,512]{3,2,1,0:T(8,128)(2,1)}, bf16[16,2,64,512]{3,2,1,0:T(8,128)(2,1)S(1)}, u32[]{:S(2)}) copy-start(bf16[16,2,64,512]{3,2,1,0:T(8,128)(2,1)S(1)} %all-to-all-done.1.cot_ref) | copy-start | bytes 6291460
  67.5 5.8 %copy-start.10 = (bf16[256,512]{1,0:T(8,128)(2,1)}, bf16[256,512]{1,0:T(8,128)(2,1)S(1)}, u32[]{:S(2)}) copy-start(bf16[256,512]{1,0:T(8,128)(2,1)S(1)} %collective-permute-done.6.rest_3_) | copy-start | bytes 786436
  67.5 28.8 %all-to-all-start.2 = ((bf16[16,64,512]{2,1,0:T(8,128)(2,1)}), bf16[16,64,512]{2,1,0:T(8,128)(2,1)}, u32[]{:S(2)}, u32[]{:S(2)}) async-start(bf16[16,64,512]{2,1,0:T(8,128)(2,1)} %spread.3), calls=%async_computation.2 | async-start | bytes 2097152 | tf_op jit(solution)/shard_map/all_to_all | solution.py:824
  73.4 19.9 %collective-permute-start.4 = (bf16[768,512]{1,0:T(8,128)(2,1)S(1)}, bf16[768,512]{1,0:T(8,128)(2,1)S(1)}, u32[]{:S(2)}, u32[]{:S(2)}) collective-permute-start(bf16[768,512]{1,0:T(8,128)(2,1)S(1)} %slice_bitcast_fusion), channel_id=1, source_target_pairs={{0,1},{1,0},{2,3},{3,2},{4,5},{5,4},{6,7},{7,6},{8,9},{9,8},{10,11... | collective-permute-start | bytes 2359304 | tf_op jit(solution)/shard_map/ppermute | solution.py:816
  79.8 23.4 %copy-start.20 = (bf16[512,16]{0,1:T(8,128)(2,1)S(1)}, bf16[512,16]{0,1:T(8,128)(2,1)}, u32[]{:S(2)}) copy-start(bf16[512,16]{0,1:T(8,128)(2,1)} %param.16) | copy-start | bytes 49156
  93.2 10.7 %copy-start.7 = (bf16[768,512]{1,0:T(8,128)(2,1)}, bf16[768,512]{1,0:T(8,128)(2,1)S(1)}, u32[]{:S(2)}) copy-start(bf16[768,512]{1,0:T(8,128)(2,1)S(1)} %collective-permute-done.4.rest_4_) | copy-start | bytes 2359300
  96.3 29.8 %all-to-all-start = ((bf16[16,64,512]{2,1,0:T(8,128)(2,1)}), bf16[16,64,512]{2,1,0:T(8,128)(2,1)S(1)}, u32[]{:S(2)}, u32[]{:S(2)}) async-start(bf16[16,64,512]{2,1,0:T(8,128)(2,1)} %spread.2), calls=%async_computation | async-start | bytes 2097152 | tf_op jit(solution)/shard_map/all_to_all | solution.py:824
  126.1 1.0 copy-start.5
  127.1 29.9 %all-to-all-start.4 = ((bf16[16,64,512]{2,1,0:T(8,128)(2,1)}), bf16[16,64,512]{2,1,0:T(8,128)(2,1)S(1)}, u32[]{:S(2)}, u32[]{:S(2)}) async-start(bf16[16,64,512]{2,1,0:T(8,128)(2,1)} %bitcast.62), calls=%async_computation.4 | async-start | bytes 2097152 | tf_op jit(solution)/shard_map/all_to_all | solution.py:824
  156.9 9.9 %copy-start.4 = (bf16[16,64,512]{2,1,0:T(8,128)(2,1)}, bf16[16,64,512]{2,1,0:T(8,128)(2,1)S(1)}, u32[]{:S(2)}) copy-start(bf16[16,64,512]{2,1,0:T(8,128)(2,1)S(1)} %all-to-all-done.4) | copy-start | bytes 3145732
  156.9 29.8 %all-to-all-start.3 = ((bf16[16,64,512]{2,1,0:T(8,128)(2,1)}), bf16[16,64,512]{2,1,0:T(8,128)(2,1)S(1)}, u32[]{:S(2)}, u32[]{:S(2)}) async-start(bf16[16,64,512]{2,1,0:T(8,128)(2,1)} %bitcast.61), calls=%async_computation.3 | async-start | bytes 2097152 | tf_op jit(solution)/shard_map/all_to_all | solution.py:824
  163.8 29.9 %collective-permute-start.9 = (bf16[512,1024]{1,0:T(8,128)(2,1)}, bf16[512,1024]{1,0:T(8,128)(2,1)}, u32[]{:S(2)}, u32[]{:S(2)}) collective-permute-start(bf16[512,1024]{1,0:T(8,128)(2,1)} %get-tuple-element.113), channel_id=1, source_target_pairs={{0,1},{1,0},{2,3},{3,2},{4,5},{5,4},{6,7},{7,6},{8,9},{9,8},{10,11... | collective-permute-start | bytes 3145736 | tf_op jit(solution)/shard_map/ppermute | solution.py:816
  166.3 27.4 %collective-permute-start.10 = (bf16[192,512]{1,0:T(8,128)(2,1)S(1)}, bf16[192,512]{1,0:T(8,128)(2,1)S(1)}, u32[]{:S(2)}, u32[]{:S(2)}) collective-permute-start(bf16[192,512]{1,0:T(8,128)(2,1)S(1)} %slice.56), channel_id=1, source_target_pairs={{0,1},{1,0},{2,3},{3,2},{4,5},{5,4},{6,7},{7,6},{8,9},{9,8},{10,11... | collective-permute-start | bytes 589832 | tf_op jit(solution)/shard_map/ppermute | solution.py:816
  193.7 8.5 %copy-start.9 = (bf16[1024,512]{1,0:T(8,128)(2,1)S(1)}, bf16[1024,512]{1,0:T(8,128)(2,1)}, u32[]{:S(2)}) copy-start(bf16[1024,512]{1,0:T(8,128)(2,1)} %get-tuple-element.125) | copy-start | bytes 3145732
  193.7 51.5 %all-to-all-start.5 = ((bf16[16,2,64,512]{3,2,1,0:T(8,128)(2,1)}), bf16[16,2,64,512]{3,2,1,0:T(8,128)(2,1)S(1)}, u32[]{:S(2)}, u32[]{:S(2)}) async-start(bf16[16,2,64,512]{3,2,1,0:T(8,128)(2,1)} %get-tuple-element.126), calls=%async_computation.5 | async-start | bytes 4194304 | tf_op jit(solution)/shard_map/all_to_all | solution.py:824
  200.6 2.6 copy-start.21
  200.6 23.0 %collective-permute-start.7 = (bf16[4,208,512]{2,1,0:T(8,128)(2,1)}, bf16[4,208,512]{2,1,0:T(8,128)(2,1)S(1)}, u32[]{:S(2)}, u32[]{:S(2)}) collective-permute-start(bf16[4,208,512]{2,1,0:T(8,128)(2,1)} %get-tuple-element.110), channel_id=1, source_target_pairs={{0,1},{1,0},{2,3},{3,2},{4,5},{5,4},{6,7},{7,6},{8,9},{9,8},{10,11... | collective-permute-start | bytes 2555912 | tf_op jit(solution)/shard_map/ppermute | solution.py:816
  203.1 20.4 %collective-permute-start.8 = (f32[4,16,208]{2,1,0:T(8,128)S(1)}, f32[4,16,208]{2,1,0:T(8,128)S(1)}, u32[]{:S(2)}, u32[]{:S(2)}) collective-permute-start(f32[4,16,208]{2,1,0:T(8,128)S(1)} %copy-done.21), channel_id=1, source_target_pairs={{0,1},{1,0},{2,3},{3,2},{4,5},{5,4},{6,7},{7,6},{8,9},{9,8},{10,11... | collective-permute-start | bytes 159752 | tf_op jit(solution)/shard_map/ppermute | solution.py:816
  223.6 2.4 copy-start.19
  224.5 20.7 %collective-permute-start.11 = (bf16[832,512]{1,0:T(8,128)(2,1)}, bf16[832,512]{1,0:T(8,128)(2,1)S(1)}, u32[]{:S(2)}, u32[]{:S(2)}) collective-permute-start(bf16[832,512]{1,0:T(8,128)(2,1)} %slice.57), channel_id=1, source_target_pairs={{0,1},{1,0},{2,3},{3,2},{4,5},{5,4},{6,7},{7,6},{8,9},{9,8},{10,11... | collective-permute-start | bytes 2555912 | tf_op jit(solution)/shard_map/ppermute | solution.py:816
  247.4 3.0 collective-permute-start.12
  247.5 21.7 %collective-permute-start.14 = (bf16[4,208,512]{2,1,0:T(8,128)(2,1)}, bf16[4,208,512]{2,1,0:T(8,128)(2,1)}, u32[]{:S(2)}, u32[]{:S(2)}) collective-permute-start(bf16[4,208,512]{2,1,0:T(8,128)(2,1)} %get-tuple-element.130.refs_0_), channel_id=1, source_target_pairs={{0,1},{1,0},{2,3},{3,2},{4,5},{5,4},{6,7},{7,6},{8,9},{9,8},{10,11... | collective-permute-start | bytes 2555912 | tf_op jit(solution)/shard_map/ppermute | solution.py:816
  253.1 15.0 %collective-permute-start.13 = (bf16[2,544,256]{2,1,0:T(8,128)(2,1)}, bf16[2,544,256]{2,1,0:T(8,128)(2,1)}, u32[]{:S(2)}, u32[]{:S(2)}) collective-permute-start(bf16[2,544,256]{2,1,0:T(8,128)(2,1)} %constant_dynamic-slice_fusion.4), channel_id=1, source_target_pairs={{0,4},{2,6},{4,0},{6,2},{8,12},{10,14},{12,8},{14,10},{16,20},{18,... | collective-permute-start | bytes 1671176 | tf_op jit(solution)/shard_map/ppermute | solution.py:924
  269.3 10.3 %collective-permute-start.15 = (bf16[2,272,256]{2,1,0:T(8,128)(2,1)S(1)}, bf16[2,272,256]{2,1,0:T(8,128)(2,1)S(1)}, u32[]{:S(2)}, u32[]{:S(2)}) collective-permute-start(bf16[2,272,256]{2,1,0:T(8,128)(2,1)S(1)} %constant_dynamic-slice_fusion.2), channel_id=1, source_target_pairs={{0,8},{2,10},{4,12},{6,14},{8,0},{10,2},{12,4},{14,6},{16,24},{18,... | collective-permute-start | bytes 835592 | tf_op jit(solution)/shard_map/ppermute | solution.py:924
  272.9 20.6 %collective-permute-start.17 = (bf16[4,208,512]{2,1,0:T(8,128)(2,1)}, bf16[4,208,512]{2,1,0:T(8,128)(2,1)S(1)}, u32[]{:S(2)}, u32[]{:S(2)}) collective-permute-start(bf16[4,208,512]{2,1,0:T(8,128)(2,1)} %get-tuple-element.135), channel_id=1, source_target_pairs={{0,1},{1,0},{2,3},{3,2},{4,5},{5,4},{6,7},{7,6},{8,9},{9,8},{10,11... | collective-permute-start | bytes 2555912 | tf_op jit(solution)/shard_map/ppermute | solution.py:816
  279.7 10.1 %collective-permute-start.16 = (bf16[2,136,256]{2,1,0:T(8,128)(2,1)S(1)}, bf16[2,136,256]{2,1,0:T(8,128)(2,1)S(1)}, u32[]{:S(2)}, u32[]{:S(2)}) collective-permute-start(bf16[2,136,256]{2,1,0:T(8,128)(2,1)S(1)} %constant_dynamic-slice_fusion.1), channel_id=1, source_target_pairs={{0,16},{2,18},{4,20},{6,22},{8,24},{10,26},{12,28},{14,30},{16,0},... | collective-permute-start | bytes 417800 | tf_op jit(solution)/shard_map/ppermute | solution.py:924
  285.9 9.1 %copy-start.3 = (f32[4,208,512]{2,1,0:T(8,128)S(1)}, f32[4,208,512]{2,1,0:T(8,128)}, u32[]{:S(2)}) copy-start(f32[4,208,512]{2,1,0:T(8,128)} %get-tuple-element.116.rest_4_) | copy-start | bytes 5111812
  293.5 4.3 %collective-permute-start.18 = (bf16[136,256]{1,0:T(8,128)(2,1)S(1)}, bf16[136,256]{1,0:T(8,128)(2,1)S(1)}, u32[]{:S(2)}, u32[]{:S(2)}) collective-permute-start(bf16[136,256]{1,0:T(8,128)(2,1)S(1)} %slice_bitcast_fusion.5), channel_id=1, source_target_pairs={{0,1},{1,0},{2,3},{3,2},{4,5},{5,4},{6,7},{7,6},{8,9},{9,8},{10,11... | collective-permute-start | bytes 208904 | tf_op jit(solution)/shard_map/ppermute | solution.py:816
  295.4 21.9 %copy-start.6 = (bf16[4,208,512]{2,1,0:T(8,128)(2,1)}, bf16[4,208,512]{2,1,0:T(8,128)(2,1)S(1)}, u32[]{:S(2)}) copy-start(bf16[4,208,512]{2,1,0:T(8,128)(2,1)S(1)} %add_convert_fusion.1.refs_0_) | copy-start | bytes 2555908
  297.9 6.0 %collective-permute-start.19 = (bf16[136,256]{1,0:T(8,128)(2,1)S(1)}, bf16[136,256]{1,0:T(8,128)(2,1)S(1)}, u32[]{:S(2)}, u32[]{:S(2)}) collective-permute-start(bf16[136,256]{1,0:T(8,128)(2,1)S(1)} %fusion.1), channel_id=1, source_target_pairs={{0,16},{2,18},{4,20},{6,22},{8,24},{10,26},{12,28},{14,30},{16,0},... | collective-permute-start | bytes 208904 | tf_op jit(solution)/shard_map/ppermute | solution.py:924
  299.4 17.9 %collective-permute-start.22 = (bf16[4,208,512]{2,1,0:T(8,128)(2,1)S(1)}, bf16[4,208,512]{2,1,0:T(8,128)(2,1)S(1)}, u32[]{:S(2)}, u32[]{:S(2)}) collective-permute-start(bf16[4,208,512]{2,1,0:T(8,128)(2,1)S(1)} %add_convert_fusion.1.refs_0_), channel_id=1, source_target_pairs={{0,1},{1,0},{2,3},{3,2},{4,5},{5,4},{6,7},{7,6},{8,9},{9,8},{10,11... | collective-permute-start | bytes 2555912 | tf_op jit(solution)/shard_map/ppermute | solution.py:816
  303.9 5.1 %collective-permute-start.20 = (bf16[272,256]{1,0:T(8,128)(2,1)S(1)}, bf16[272,256]{1,0:T(8,128)(2,1)S(1)}, u32[]{:S(2)}, u32[]{:S(2)}) collective-permute-start(bf16[272,256]{1,0:T(8,128)(2,1)S(1)} %maximum_select_fusion.3), channel_id=1, source_target_pairs={{0,8},{2,10},{4,12},{6,14},{8,0},{10,2},{12,4},{14,6},{16,24},{18,... | collective-permute-start | bytes 417800 | tf_op jit(solution)/shard_map/ppermute | solution.py:924
  309.1 6.6 %collective-permute-start.21 = (bf16[544,256]{1,0:T(8,128)(2,1)S(1)}, bf16[544,256]{1,0:T(8,128)(2,1)S(1)}, u32[]{:S(2)}, u32[]{:S(2)}) collective-permute-start(bf16[544,256]{1,0:T(8,128)(2,1)S(1)} %maximum_select_fusion.2), channel_id=1, source_target_pairs={{0,4},{2,6},{4,0},{6,2},{8,12},{10,14},{12,8},{14,10},{16,20},{18,... | collective-permute-start | bytes 835592 | tf_op jit(solution)/shard_map/ppermute | solution.py:924
  317.3 4.1 %collective-permute-start.23 = (bf16[1088,256]{1,0:T(8,128)(2,1)S(1)}, bf16[1088,256]{1,0:T(8,128)(2,1)S(1)}, u32[]{:S(2)}, u32[]{:S(2)}) collective-permute-start(bf16[1088,256]{1,0:T(8,128)(2,1)S(1)} %maximum_select_fusion.1), channel_id=1, source_target_pairs={{0,2},{2,0},{4,6},{6,4},{8,10},{10,8},{12,14},{14,12},{16,18},{18,... | collective-permute-start | bytes 1671176 | tf_op jit(solution)/shard_map/ppermute | solution.py:924
  (4 other events, 3.7 us)

commit v2 on v1

--- a/solution.py
+++ b/solution.py
@@ -96,9 +96,9 @@
             slot = jnp.where(place >= c * half, slot + (experts * block - half), slot)
         return jnp.where(good, slot, -1)
 
-    lanes = col_ref.shape[1]
+    lanes = col_ref.shape[0]
     span = lanes * experts
-    routes = col_ref[...]
+    routes = col_ref[...].astype(F32).T.astype(jnp.int32)
     spread_lanes = (iota((lanes, span), 1) // experts == iota((lanes, span), 0)).astype(BF16)
     gather_lanes = (iota((span, lanes), 0) // experts == iota((span, lanes), 1)).astype(BF16)
     chosen = nn(routes.astype(F32).astype(BF16), spread_lanes) == (iota((PAD, span), 1) % experts).astype(F32)
@@ -107,9 +107,7 @@
     before = nn(lower, ones.astype(BF16))
     totals = jnp.broadcast_to(jnp.sum(ones, axis=0, keepdims=True), (16, span)).astype(BF16)
     source, target = iota((span, span), 0), iota((span, span), 1)
-    order_s = (source // experts % 2) * lanes + source // (2 * experts)
-    order_t = (target // experts % 2) * lanes + target // (2 * experts)
-    earlier = (source % experts == target % experts) & (order_s < order_t)
+    earlier = (source % experts == target % experts) & (source // experts < target // experts)
     before = before + nn(totals, earlier.astype(BF16))[0:1]
     place = nn((jnp.minimum(before, float(cap)) * ones).astype(BF16), gather_lanes)
     col_out[...] = code(routes, place)
@@ -145,16 +143,16 @@
     rows, width = cotangent.shape
     images = rows // SEQ
     padded = jnp.pad(
-        routes.reshape(images, SEQ, 2), ((0, 0), (0, PAD - SEQ), (0, 0)), constant_values=-1
+        routes.T.reshape(2, images, SEQ), ((0, 0), (0, 0), (0, PAD - SEQ)), constant_values=-1
     )
-    down = padded.transpose(1, 0, 2).reshape(PAD, images * 2)
-    across = padded.reshape(images * PAD, 2).T
+    down = padded.reshape(2 * images, PAD)
+    across = padded.reshape(2, images * PAD)
     return pl.pallas_call(
         functools.partial(front_kernel, cap=cap, half=half),
         out_shape=(
             jax.ShapeDtypeStruct((images, PAD, width), BF16),
             jax.ShapeDtypeStruct((experts, chunks, block, width), BF16),
-            jax.ShapeDtypeStruct(down.shape, jnp.int32),
+            jax.ShapeDtypeStruct(down.shape[::-1], jnp.int32),
             jax.ShapeDtypeStruct(across.shape, jnp.int32),
         ),
         in_specs=[pl.BlockSpec(memory_space=pltpu.SMEM)] + [VMEM] * 3,
@@ -367,7 +365,7 @@
     x = x_ref[...]
     rows, width = x.shape
     cot = cot_ref[...].reshape(rows, width).astype(F32)
-    logits = nn(x, wr_ref[...])
+    logits = nt(x, wr_ref[...])
     ex = jnp.exp(logits - jnp.max(logits, axis=1, keepdims=True))
     mine = iota(ex.shape, 1) == expert
     gate = jnp.sum(jnp.where(mine, ex, 0.0), axis=1, keepdims=True) / jnp.sum(
@@ -479,7 +477,7 @@
         grid_spec=pltpu.PrefetchScalarGridSpec(
             num_scalar_prefetch=1,
             grid=(1,),
-            in_specs=[row_spec, chunk_spec, full(w_router.shape)] + [anywhere] * (len(weights) + len(old)),
+            in_specs=[row_spec, chunk_spec, full(w_router.shape[::-1])] + [anywhere] * (len(weights) + len(old)),
             out_specs=(row_spec, chunk_spec) + (anywhere,) * len(shapes),
             scratch_shapes=[
                 pltpu.VMEM((shards, width, hidden), BF16),
@@ -499,7 +497,7 @@
         compiler_params=params(62),
         cost_estimate=cost(20),
         name="experts",
-    )(expert, x, cot, w_router, *weights, *old)
+    )(expert, x, cot, w_router.T, *weights, *old)
 
 
 def collect_kernel(first_ref, code_ref, *rest, numbers, half, block, probs, before):
@@ -512,8 +510,11 @@
     rows = PAD
     codes = code_ref[...]
     across = iota(codes.shape, 1)
-    at = (first_ref[0] + pl.program_id(0)) * 2
-    columns = [jnp.sum(jnp.where(across == at + c, codes, 0), axis=1, keepdims=True) for c in range(2)]
+    at = first_ref[0] + pl.program_id(0)
+    images = codes.shape[1] // 2
+    columns = [
+        jnp.sum(jnp.where(across == at + c * images, codes, 0), axis=1, keepdims=True) for c in range(2)
+    ]
     lane = iota((rows, count), 1)
     total = old[0][0] if old else None
     grads = None
@@ -575,11 +576,12 @@
     )(first, code_col, *parts, *before)
 
 
-def back_kernel(first_ref, *rest, steps, received):
+def back_kernel(place_ref, *rest, steps, received, split):
     (sum_ref, gp_ref), rest = rest[:2], rest[2:]
     more, rest = rest[: 2 * received], rest[2 * received :]
     (res_ref, cot_ref, tok_ref, ga_ref, gm_ref, wrt_ref, wq, wo, qkv_ref, prob_ref, att_ref), rest = rest[:11], rest[11:]
-    gtok_ref, pack_ref, dwq, dwo, small, gatt_all, dqkv_all, wq_here, qkv_here, prob_here, sems = rest
+    gtok_ref, packs, rest = rest[0], rest[1 : 2 + split], rest[2 + split :]
+    dwq, dwo, small, gatt_all, dqkv_all, wq_here, qkv_here, prob_here, pack_ref, sems = rest
     experts = wrt_ref.shape[0]
     batch, _, model = res_ref.shape
     rows = batch * PAD
@@ -691,6 +693,13 @@
                     at += value.shape[0]
             if at < pack_ref.shape[1]:
                 pack_ref[s, at:, :] = jnp.zeros((pack_ref.shape[1] - at, 256), BF16)
+        if split:
+            size = packs[0].shape[1]
+            at = pl.multiple_of(place_ref[1] * size, size)
+            packs[0][...] = pack_ref[:, pl.ds(at, size), :]
+            packs[1][...] = pack_ref[:, pl.ds(pl.multiple_of(size - at, size), size), :]
+        else:
+            packs[0][...] = pack_ref[...]
 
 
 def small_rows(experts):
@@ -702,11 +711,12 @@
     return -(-rows // align) * align
 
 
-def back(first, sums, residual, cot_pad, tok_pad, qkv, probs, att, gain_attn, gain_moe, w_router, wq, wo, shards, align, batch=2):
+def back(place, sums, residual, cot_pad, tok_pad, qkv, probs, att, gain_attn, gain_moe, w_router, wq, wo, shards, align, batch=2):
     own, _, width = residual.shape
     batch = batch if own % batch == 0 else 1
     experts = w_router.shape[1]
     rows = pack_rows(width, width // shards, experts, align)
+    split = int(shards == 2)
 
     def mine(*shape):
         return pl.BlockSpec((batch,) + shape, lambda i, f: (i,) + (0,) * len(shape))
@@ -714,11 +724,9 @@
     image = pl.BlockSpec((batch, PAD, width), lambda i, f: (i + f[0] // batch, 0, 0))
     flat = [v for pair in sums for v in pair]
     return pl.pallas_call(
-        functools.partial(back_kernel, steps=own // batch, received=len(sums) - 1),
-        out_shape=(
-            jax.ShapeDtypeStruct((own, PAD, width), BF16),
-            jax.ShapeDtypeStruct((shards, rows, 256), BF16),
-        ),
+        functools.partial(back_kernel, steps=own // batch, received=len(sums) - 1, split=split),
+        out_shape=(jax.ShapeDtypeStruct((own, PAD, width), BF16),)
+        + (jax.ShapeDtypeStruct((shards, rows // (1 + split), 256), BF16),) * (1 + split),
         grid_spec=pltpu.PrefetchScalarGridSpec(
             num_scalar_prefetch=1,
             grid=(own // batch,),
@@ -736,7 +744,7 @@
                 pl.BlockSpec(memory_space=pl.ANY),
                 mine(*att.shape[1:]),
             ],
-            out_specs=(mine(PAD, width), full((shards, rows, 256))),
+            out_specs=(mine(PAD, width),) + (full((shards, rows // (1 + split), 256)),) * (1 + split),
             scratch_shapes=[
                 pltpu.VMEM((width, 3 * width), F32),
                 pltpu.VMEM((width, width), F32),
@@ -746,6 +754,7 @@
                 pltpu.VMEM(wq.shape, BF16),
                 pltpu.VMEM(qkv.shape, BF16),
                 pltpu.VMEM(probs.shape, BF16),
+                pltpu.VMEM((shards, rows, 256), BF16),
                 pltpu.SemaphoreType.DMA((own // batch, 3)),
             ],
         ),
@@ -753,7 +762,7 @@
         cost_estimate=cost(16),
         name="back",
     )(
-        first,
+        place,
         *flat,
         residual,
         cot_pad,
@@ -912,8 +921,8 @@
         ]
         grad_w1 = lax.psum_scatter(dw[0].astype(BF16), "tensor", scatter_dimension=1, tiled=True).astype(F32)
         grad_w2 = lax.psum_scatter(dw[1].astype(BF16), "tensor", scatter_dimension=0, tiled=True).astype(F32)
-    grad_tok, pack = back(
-        first, sums, residual, cot_pad, tok_pad, qkv, probs, att, gain_attn, gain_moe, w_router, wq, wo,
+    grad_tok, *pack = back(
+        place, sums, residual, cot_pad, tok_pad, qkv, probs, att, gain_attn, gain_moe, w_router, wq, wo,
         2 if ways == 2 else 1, groups * 8,
     )
 
@@ -933,17 +942,17 @@
             give = lax.dynamic_slice_in_dim(v, (1 - upper) * size, size, v.ndim - 2)
             return keep, give
 
-        pack, grad_tok, gated, dw2_peer[1] = lax.optimization_barrier((pack, grad_tok, gated, dw2_peer[1]))
+        keep, give, grad_tok, gated, dw2_peer[1] = lax.optimization_barrier((*pack, grad_tok, gated, dw2_peer[1]))
         grad_peer = other(grad_tok)
         gated = [rows_of(gated[:, c]) for c in range(chunks)]
         (mix,) = collect(zero, code_col, gated, images, BF16, half, block)
         mix_there = lax.dynamic_slice_in_dim(mix, (1 - rank) * own, own, 0)
         mix_here = lax.dynamic_slice_in_dim(mix, rank * own, own, 0)
-        for bit in bits[:2]:
-            keep, give = halves(pack, bit)
-            pack = add(keep, swap_bit(give, bit))
+        pack = add(keep, swap_bit(give, bits[0]))
+        keep, give = halves(pack, bits[1])
+        pack = add(keep, swap_bit(give, bits[1]))
+        mix_peer = other(mix_there)
         pack, mix_there, grad_peer = lax.optimization_barrier((pack, mix_there, grad_peer))
-        mix_peer = other(mix_there)
         keep, give = halves(pack, bits[2])
         pack = add(keep, swap_bit(give, bits[2]))
         grad_tokens = unpad(first, [grad_tok], [grad_peer], F32)
@@ -981,7 +990,7 @@
 
         result = whole((residual + mixture).astype(BF16))
         grad_tokens = whole(grad_tok).astype(F32)
-        total = lax.psum(pack[0], ("expert", "tensor")).astype(F32)
+        total = lax.psum(pack[0][0], ("expert", "tensor")).astype(F32)
         part = width
 
     def take(at, rows, cols):

time: 326 us -> 324 us (level)
  local copies, waits for them, and re-layouts: 16.9 us -> 12.1 us
    unnamed x46 -> x36, local copies, waits for them, and re-layouts: 5.53 us -> 1.96 us
  transfers between devices with their start and end apart: 30 -> 30, of which waited for: 19 -> 18; matrix products, arithmetic and copies ran while one was open for 6% -> 6% of each run, Pallas kernels for 42% -> 42%
where the time goes in v2:
time: 324 us; the launch traced here: 323 us
  Pallas kernels  146 us (45%)
  waiting for transfers between devices  77.3 us (24%)
  starting transfers between devices  71.4 us (22%)
  other arithmetic  14.9 us (5%)
  local copies, waits for them, and re-layouts  12.1 us (4%)
    pallas_call x2, Pallas kernels, experts_step(): pl.pallas_call(functools.partial(expert_kernel, parts=parts, half=half, b...  45.2 us
    all_to_all x6, starting transfers between devices, exchange(): lax.all_to_all(rows, 'expert', split_axis=0, concat_axis=0, tiled=True)  40.7 us
    ppermute x14, waiting for transfers between devices, other(): return lax.ppermute(v, 'tensor', swap)  39.8 us
    pallas_call x4, Pallas kernels, collect(): pl.pallas_call(functools.partial(collect_kernel, numbers=numbers, half=ha...  28.9 us
    pallas_call x1, Pallas kernels, attend(): pl.pallas_call(functools.partial(attend_kernel, pieces=pieces, own=own),...  22.2 us
    ppermute x8, waiting for transfers between devices, swap_bit(): return lax.ppermute(v, 'expert', [(i, i ^ bit) for i in range(groups)])  21.4 us
    pallas_call x1, Pallas kernels, back(): pl.pallas_call(functools.partial(back_kernel, steps=own // batch, receive...  19.2 us
    ppermute x14, starting transfers between devices, other(): return lax.ppermute(v, 'tensor', swap)  17.5 us
  transfers between devices with their start and end apart: 30, of which 18 were waited for; matrix products, arithmetic and copies ran while one was open for 6% of the time, Pallas kernels for 42%

profile of v2, /device:TPU:0, one launch (start us, length us, event | category | flops | bytes accessed | tf_op | source)
XLA Modules:
  0.0 322.7 jit_solution(5724490895777373174)
XLA Ops:
  2.8 9.6 %front.1 = (bf16[8,208,512]{2,1,0:T(8,128)(2,1)}, bf16[16,2,64,512]{3,2,1,0:T(8,128)(2,1)}, s32[208,16]{1,0:T(8,128)}, s32[2,1664]{1,0:T(2,128)}) custom-call(s32[1]{0:T(128)} %bitcast.2.rank_ref, bf16[1576,512]{1,0:T(8,128)(2,1)} %cot_ref.1, s32[16,208]{1,0:T(8,128)} %get-tuple-element.163.col_ref, s32[2,1664]{1,0:T(2,128)} %reshape.75.row_ref), custom_call_target="tpu_custom_call" | custom-call | bytes 36900000 | tf_op jit(solution)/shard_map/front/pallas_call | solution.py:150
  12.4 7.5 %all-to-all-start.1 = ((bf16[16,2,64,512]{3,2,1,0:T(8,128)(2,1)}), bf16[16,2,64,512]{3,2,1,0:T(8,128)(2,1)S(1)}, u32[]{:S(2)}, u32[]{:S(2)}) async-start(bf16[16,2,64,512]{3,2,1,0:T(8,128)(2,1)} %get-tuple-element.81), calls=%async_computation.1 | async-start | bytes 4194304 | tf_op jit(solution)/shard_map/all_to_all | solution.py:833
  20.0 1.6 collective-permute-start
  22.2 4.2 %pad.74.tok_ref.rest_6_ = bf16[8,208,512]{2,1,0:T(8,128)(2,1)} custom-call(bf16[1576,512]{1,0:T(8,128)(2,1)} %source), custom_call_target="tpu_custom_call" | custom-call | bytes 7380000 | tf_op jit(solution)/shard_map/pad/pallas_call | solution.py:66
  26.4 7.9 %collective-permute-done.1.rest_4_ = bf16[128,512]{1,0:T(8,128)(2,1)S(1)} collective-permute-done((bf16[128,512]{1,0:T(8,128)(2,1)S(1)}, bf16[128,512]{1,0:T(8,128)(2,1)S(1)}, u32[]{:S(2)}, u32[]{:S(2)}) %collective-permute-start.1) | collective-permute-done | bytes 131104 | tf_op jit(solution)/shard_map/ppermute | solution.py:825
  36.3 1.6 collective-permute-start.5
  39.8 22.2 %attend.1 = (bf16[8,208,512]{2,1,0:T(8,128)(2,1)}, f32[4,208,512]{2,1,0:T(8,128)}, bf16[4,208,1536]{2,1,0:T(8,128)(2,1)}, bf16[4,2,832,208]{3,2,1,0:T(8,128)(2,1...) custom-call(s32[2]{0:T(128)} %pad_add_fusion.place_ref, ...), custom_call_target="tpu_custom_call" | custom-call | bytes 92250000 | tf_op jit(solution)/shard_map/attend/pallas_call | solution.py:299
  62.0 4.9 %spread.3 = bf16[16,64,512]{2,1,0:T(8,128)(2,1)} custom-call(s32[2,1664]{1,0:T(2,128)} %get-tuple-element.80.code_ref, bf16[1664,512]{1,0:T(8,128)(2,1)} %bitcast.47), custom_call_target="tpu_custom_call" | custom-call | bytes 18450000 | tf_op jit(solution)/shard_map/spread/pallas_call | solution.py:177
  67.3 5.8 %all-to-all-start.2 = ((bf16[16,64,512]{2,1,0:T(8,128)(2,1)}), bf16[16,64,512]{2,1,0:T(8,128)(2,1)}, u32[]{:S(2)}, u32[]{:S(2)}) async-start(bf16[16,64,512]{2,1,0:T(8,128)(2,1)} %spread.3), calls=%async_computation.2 | async-start | bytes 2097152 | tf_op jit(solution)/shard_map/all_to_all | solution.py:833
  73.2 1.6 collective-permute-start.4
  74.8 4.8 %spread.2 = bf16[16,64,512]{2,1,0:T(8,128)(2,1)} custom-call(s32[2,1664]{1,0:T(2,128)} %get-tuple-element.80.code_ref, bf16[1664,512]{1,0:T(8,128)(2,1)} %bitcast.48), custom_call_target="tpu_custom_call" | custom-call | bytes 18450000 | tf_op jit(solution)/shard_map/spread/pallas_call | solution.py:177
  79.6 13.5 %collective-permute-done.4.rest_4_ = bf16[768,512]{1,0:T(8,128)(2,1)S(1)} collective-permute-done((bf16[768,512]{1,0:T(8,128)(2,1)S(1)}, bf16[768,512]{1,0:T(8,128)(2,1)S(1)}, u32[]{:S(2)}, u32[]{:S(2)}) %collective-permute-start.4) | collective-permute-done | bytes 786464 | tf_op jit(solution)/shard_map/ppermute | solution.py:825
  93.1 3.0 all-to-all-done.2
  96.1 6.9 %all-to-all-start = ((bf16[16,64,512]{2,1,0:T(8,128)(2,1)}), bf16[16,64,512]{2,1,0:T(8,128)(2,1)S(1)}, u32[]{:S(2)}, u32[]{:S(2)}) async-start(bf16[16,64,512]{2,1,0:T(8,128)(2,1)} %spread.2), calls=%async_computation | async-start | bytes 2097152 | tf_op jit(solution)/shard_map/all_to_all | solution.py:833
  103.0 22.1 %experts.2 = (bf16[1024,512]{1,0:T(8,128)(2,1)}, bf16[16,2,64,512]{3,2,1,0:T(8,128)(2,1)}, f32[512,1024]{1,0:T(8,128)}, f32[512,1024]{1,0:T(8,128)}, f32[1024,512]{1,0:T(8,128)}, /*index=5*/f32[1024,512]{1,0:T(8,128)}) custom-call(s32[1]{0:T(128)} %bitcast.5.expert_ref, bf16[1024,512]{1,0:T(8,128)(2,1)} %bitcast.15.x_ref, bf16[16,2,64,512]{3,2,1,0:T(8,128)(2,1)} %copy-done, ...), custom_call_target="tpu_custom_call" | custom-call | bytes 73800000 | tf_op jit(solution)/shard_map/experts/pallas_call | solution.py:463
  125.9 6.9 %all-to-all-start.4 = ((bf16[16,64,512]{2,1,0:T(8,128)(2,1)}), bf16[16,64,512]{2,1,0:T(8,128)(2,1)}, u32[]{:S(2)}, u32[]{:S(2)}) async-start(bf16[16,64,512]{2,1,0:T(8,128)(2,1)} %bitcast.55), calls=%async_computation.4 | async-start | bytes 2097152 | tf_op jit(solution)/shard_map/all_to_all | solution.py:833
  132.9 23.1 %experts.3 = (bf16[1024,512]{1,0:T(8,128)(2,1)}, bf16[16,2,64,512]{3,2,1,0:T(8,128)(2,1)}, f32[512,1024]{1,0:T(8,128)}, bf16[512,1024]{1,0:T(8,128)(2,1)}, f32[1...) custom-call(s32[1]{0:T(128)} %bitcast.5.expert_ref, bf16[1024,512]{1,0:T(8,128)(2,1)} %bitcast.49, ...), custom_call_target="tpu_custom_call", output_to_operand_aliasing={{1}: (13, {})} | custom-call | bytes 73800000 | tf_op jit(solution)/shard_map/experts/pallas_call | solution.py:463
  155.9 6.8 %all-to-all-start.3 = ((bf16[16,64,512]{2,1,0:T(8,128)(2,1)}), bf16[16,64,512]{2,1,0:T(8,128)(2,1)S(1)}, u32[]{:S(2)}, u32[]{:S(2)}) async-start(bf16[16,64,512]{2,1,0:T(8,128)(2,1)} %bitcast.54), calls=%async_computation.3 | async-start | bytes 2097152 | tf_op jit(solution)/shard_map/all_to_all | solution.py:833
  162.7 1.6 collective-permute-start.9
  165.8 8.9 %collect.4 = (f32[8,208,512]{2,1,0:T(8,128)}, f32[8,16,208]{2,1,0:T(8,128)}) custom-call(s32[1]{0:T(128)} %constant.99.clone.1.first_ref, s32[208,16]{1,0:T(8,128)} %get-tuple-element.79.code_ref, bf16[1024,512]{1,0:T(8,128)(2,1)} %bitcast.19.rest_0_), custom_call_target="tpu_custom_call" | custom-call | bytes 25830000 | tf_op jit(solution)/shard_map/collect/pallas_call | solution.py:559
  174.7 10.9 %all-to-all-done.3 = bf16[16,64,512]{2,1,0:T(8,128)(2,1)S(1)} async-done(((bf16[16,64,512]{2,1,0:T(8,128)(2,1)}), bf16[16,64,512]{2,1,0:T(8,128)(2,1)S(1)}, u32[]{:S(2)}, u32[]{:S(2)}) %all-to-all-start.3) | async-done | bytes 1048608 | tf_op jit(solution)/shard_map/all_to_all | solution.py:833
  186.6 5.9 %collect.6 = (bf16[4,208,512]{2,1,0:T(8,128)(2,1)}, f32[4,16,208]{2,1,0:T(8,128)}) custom-call(s32[1]{0:T(128)} %bitcast.20.first_ref, s32[208,16]{1,0:T(8,128)} %get-tuple-element.79.code_ref, bf16[1024,512]{1,0:T(8,128)(2,1)} %bitcast.43, f32[8,208,512]{2,1,0:T(8,128)} %get-tuple-element.107.rest_1_, f32[8,16,208]{2,1,0:T(8,128)} %get-tuple-element.108.rest_2_), custom_call_target="tpu_custom_call" | custom-call | bytes 25830000 | tf_op jit(solution)/shard_map/collect/pallas_call | solution.py:559
  192.6 6.8 %all-to-all-start.5 = ((bf16[16,2,64,512]{3,2,1,0:T(8,128)(2,1)}), bf16[16,2,64,512]{3,2,1,0:T(8,128)(2,1)S(1)}, u32[]{:S(2)}, u32[]{:S(2)}) async-start(bf16[16,2,64,512]{3,2,1,0:T(8,128)(2,1)} %get-tuple-element.128), calls=%async_computation.5 | async-start | bytes 4194304 | tf_op jit(solution)/shard_map/all_to_all | solution.py:833
  199.4 1.6 collective-permute-start.7
  202.8 3.4 %convert_add_fusion.1 = f32[512,1024]{1,0:T(8,128)} fusion(f32[512,1024]{1,0:T(8,128)} %get-tuple-element.113, bf16[512,1024]{1,0:T(8,128)(2,1)S(1)} %collective-permute-done.9), kind=kLoop, calls=%fused_computation.2 | loop fusion | flops 1048576 | bytes 5242880 | tf_op jit(solution)/shard_map/add | solution.py:909
  206.2 5.9 %collect.5 = (f32[4,208,512]{2,1,0:T(8,128)}, f32[4,16,208]{2,1,0:T(8,128)}) custom-call(s32[1]{0:T(128)} %bitcast.first_ref, s32[208,16]{1,0:T(8,128)} %get-tuple-element.79.code_ref, bf16[1024,512]{1,0:T(8,128)(2,1)} %bitcast.44, f32[8,208,512]{2,1,0:T(8,128)} %get-tuple-element.107.rest_1_, f32[8,16,208]{2,1,0:T(8,128)} %get-tuple-element.108.rest_2_), custom_call_target="tpu_custom_call" | custom-call | bytes 25830000 | tf_op jit(solution)/shard_map/collect/pallas_call | solution.py:559
  212.0 10.4 %collective-permute-done.8.rest_3_ = f32[4,16,208]{2,1,0:T(8,128)S(1)} collective-permute-done((f32[4,16,208]{2,1,0:T(8,128)S(1)}, f32[4,16,208]{2,1,0:T(8,128)S(1)}, u32[]{:S(2)}, u32[]{:S(2)}) %collective-permute-start.8) | collective-permute-done | bytes 53280 | tf_op jit(solution)/shard_map/ppermute | solution.py:825
  222.4 1.6 collective-permute-start.11
  224.0 19.2 %back.1 = (bf16[4,208,512]{2,1,0:T(8,128)(2,1)}, bf16[2,1088,256]{2,1,0:T(8,128)(2,1)}, bf16[2,1088,256]{2,1,0:T(8,128)(2,1)}) custom-call(s32[2]{0:T(128)} %pad_add_fusion.place_ref, f32[4,208,512]{2,1,0:T(8,128)} %get-tuple-element.109.rest_0_, f32[4,16,208]{2,1,0:T(8,128)} %get-tuple-element.110.rest_1_, bf16[4,208,512]{2,1,0:T(8,128)(2,1)} %copy-done.10, ...), custom_call_target="tpu_custom_call" | custom-call | bytes 59040000 | tf_op jit(solution)/shard_map/back/pallas_call | solution.py:726
  244.6 1.8 collective-permute-done.12
  246.4 1.9 add_convert_fusion
  249.1 1.6 collective-permute-start.13
  252.2 8.2 %collect.7 = bf16[8,208,512]{2,1,0:T(8,128)(2,1)} custom-call(s32[1]{0:T(128)} %constant.99.clone.1.first_ref, s32[208,16]{1,0:T(8,128)} %get-tuple-element.79.code_ref, bf16[1024,512]{1,0:T(8,128)(2,1)} %bitcast.51, bf16[1024,512]{1,0:T(8,128)(2,1)} %bitcast.50), custom_call_target="tpu_custom_call" | custom-call | bytes 25830000 | tf_op jit(solution)/shard_map/collect/pallas_call | solution.py:559
  260.4 2.5 constant_dynamic-slice_fusion
  265.3 5.2 %collective-permute-start.15 = (bf16[2,272,256]{2,1,0:T(8,128)(2,1)S(1)}, bf16[2,272,256]{2,1,0:T(8,128)(2,1)S(1)}, u32[]{:S(2)}, u32[]{:S(2)}) collective-permute-start(bf16[2,272,256]{2,1,0:T(8,128)(2,1)S(1)} %constant_dynamic-slice_fusion.2), channel_id=1, source_target_pairs={{0,8},{2,10},{4,12},{6,14},{8,0},{10,2},{12,4},{14,6},{16,24},{18,... | collective-permute-start | bytes 835592 | tf_op jit(solution)/shard_map/ppermute | solution.py:933
  270.6 1.5 collective-permute-start.17
  272.1 5.1 %collective-permute-done.15 = bf16[2,272,256]{2,1,0:T(8,128)(2,1)S(1)} collective-permute-done((bf16[2,272,256]{2,1,0:T(8,128)(2,1)S(1)}, bf16[2,272,256]{2,1,0:T(8,128)(2,1)S(1)}, u32[]{:S(2)}, u32[]{:S(2)}) %collective-permute-start.15) | collective-permute-done | bytes 278560 | tf_op jit(solution)/shard_map/ppermute | solution.py:933
  277.3 2.8 collective-permute-start.16
  280.1 3.4 %convert_add_fusion = f32[1024,512]{1,0:T(8,128)} fusion(f32[1024,512]{1,0:T(8,128)} %get-tuple-element.135, bf16[832,512]{1,0:T(8,128)(2,1)} %collective-permute-done.11, bf16[192,512]{1,0:T(8,128)(2,1)S(1)} %collective-permute-done.10), kind=kLoop, calls=%fused_computation.1 | loop fusion | flops 2621440 | bytes 5242880 | tf_op jit(solution)/shard_map/add | solution.py:961
  283.5 3.8 %unpad.2 = f32[1576,512]{1,0:T(8,128)} custom-call(s32[1]{0:T(128)} %bitcast.first_ref, bf16[4,208,512]{2,1,0:T(8,128)(2,1)} %get-tuple-element.133.refs_0_, bf16[4,208,512]{2,1,0:T(8,128)(2,1)} %collective-permute-done.14.refs_1_), custom_call_target="tpu_custom_call" | custom-call | bytes 7380000 | tf_op jit(solution)/shard_map/unpad/pallas_call | solution.py:797
  287.4 3.8 %collective-permute-done.17 = bf16[4,208,512]{2,1,0:T(8,128)(2,1)S(1)} collective-permute-done((bf16[4,208,512]{2,1,0:T(8,128)(2,1)}, bf16[4,208,512]{2,1,0:T(8,128)(2,1)S(1)}, u32[]{:S(2)}, u32[]{:S(2)}) %collective-permute-start.17) | collective-permute-done | bytes 852000 | tf_op jit(solution)/shard_map/ppermute | solution.py:825
  291.2 1.5 collective-permute-start.18
  293.1 2.4 collective-permute-done.18
  297.0 1.5 collective-permute-start.22
  298.5 3.0 collective-permute-done.19
  301.6 5.0 %collective-permute-done.20 = bf16[272,256]{1,0:T(8,128)(2,1)S(1)} collective-permute-done((bf16[272,256]{1,0:T(8,128)(2,1)S(1)}, bf16[272,256]{1,0:T(8,128)(2,1)S(1)}, u32[]{:S(2)}, u32[]{:S(2)}) %collective-permute-start.20) | collective-permute-done | bytes 139296 | tf_op jit(solution)/shard_map/ppermute | solution.py:933
  308.2 5.2 %collective-permute-done.21 = bf16[544,256]{1,0:T(8,128)(2,1)S(1)} collective-permute-done((bf16[544,256]{1,0:T(8,128)(2,1)S(1)}, bf16[544,256]{1,0:T(8,128)(2,1)S(1)}, u32[]{:S(2)}, u32[]{:S(2)}) %collective-permute-start.21) | collective-permute-done | bytes 278560 | tf_op jit(solution)/shard_map/ppermute | solution.py:933
  315.8 3.1 unpad.3
  (97 shorter events, 28.3 us)
Async XLA Ops:
  12.4 7.5 %copy-start.7 = (bf16[3,512,256]{2,1,0:T(8,128)(2,1)S(1)}, bf16[3,512,256]{2,1,0:T(8,128)(2,1)}, u32[]{:S(2)}) copy-start(bf16[3,512,256]{2,1,0:T(8,128)(2,1)} %rest_0_.1) | copy-start | bytes 2359300
  12.4 9.2 %copy-start.11 = (bf16[256,512]{1,0:T(8,128)(2,1)S(1)}, bf16[256,512]{1,0:T(8,128)(2,1)}, u32[]{:S(2)}) copy-start(bf16[256,512]{1,0:T(8,128)(2,1)} %rest_3_.1) | copy-start | bytes 786436
  12.4 54.5 %all-to-all-start.1 = ((bf16[16,2,64,512]{3,2,1,0:T(8,128)(2,1)}), bf16[16,2,64,512]{3,2,1,0:T(8,128)(2,1)S(1)}, u32[]{:S(2)}, u32[]{:S(2)}) async-start(bf16[16,2,64,512]{3,2,1,0:T(8,128)(2,1)} %get-tuple-element.81), calls=%async_computation.1 | async-start | bytes 4194304 | tf_op jit(solution)/shard_map/all_to_all | solution.py:833
  20.0 14.3 %collective-permute-start = (bf16[3,512,128]{2,1,0:T(8,128)(2,1)S(1)}, bf16[3,512,128]{2,1,0:T(8,128)(2,1)S(1)}, u32[]{:S(2)}, u32[]{:S(2)}) collective-permute-start(bf16[3,512,128]{2,1,0:T(8,128)(2,1)S(1)} %constant_dynamic-slice_fusion.6), channel_id=1, source_target_pairs={{0,1},{1,0},{2,3},{3,2},{4,5},{5,4},{6,7},{7,6},{8,9},{9,8},{10,11... | collective-permute-start | bytes 1179656 | tf_op jit(solution)/shard_map/ppermute | solution.py:825
  21.6 16.2 %copy-start.2 = (bf16[1,1024,512]{2,1,0:T(8,128)(2,1)S(1)}, bf16[1,1024,512]{2,1,0:T(8,128)(2,1)}, u32[]{:S(2)}) copy-start(bf16[1,1024,512]{2,1,0:T(8,128)(2,1)} %param.18) | copy-start | bytes 3145732
  21.6 12.7 %collective-permute-start.1 = (bf16[128,512]{1,0:T(8,128)(2,1)S(1)}, bf16[128,512]{1,0:T(8,128)(2,1)S(1)}, u32[]{:S(2)}, u32[]{:S(2)}) collective-permute-start(bf16[128,512]{1,0:T(8,128)(2,1)S(1)} %constant_dynamic-slice_fusion.5), channel_id=1, source_target_pairs={{0,1},{1,0},{2,3},{3,2},{4,5},{5,4},{6,7},{7,6},{8,9},{9,8},{10,11... | collective-permute-start | bytes 393224 | tf_op jit(solution)/shard_map/ppermute | solution.py:825
  34.3 5.5 %copy-start.14 = (bf16[128,512]{1,0:T(8,128)(2,1)}, bf16[128,512]{1,0:T(8,128)(2,1)S(1)}, u32[]{:S(2)}) copy-start(bf16[128,512]{1,0:T(8,128)(2,1)S(1)} %collective-permute-done.1.rest_4_) | copy-start | bytes 393220
  34.3 3.5 %copy-start.12 = (bf16[3,512,128]{2,1,0:T(8,128)(2,1)}, bf16[3,512,128]{2,1,0:T(8,128)(2,1)S(1)}, u32[]{:S(2)}) copy-start(bf16[3,512,128]{2,1,0:T(8,128)(2,1)S(1)} %collective-permute-done.rest_1_) | copy-start | bytes 1179652
  34.3 2.0 collective-permute-start.2
  34.4 1.9 collective-permute-start.3
  36.3 1.6 copy-start.15
  36.3 2.3 copy-start.13
  36.3 31.0 %collective-permute-start.5 = (bf16[512,1024]{1,0:T(8,128)(2,1)}, bf16[512,1024]{1,0:T(8,128)(2,1)}, u32[]{:S(2)}, u32[]{:S(2)}) collective-permute-start(bf16[512,1024]{1,0:T(8,128)(2,1)} %bitcast.12.rest_0_), channel_id=1, source_target_pairs={{0,1},{1,0},{2,3},{3,2},{4,5},{5,4},{6,7},{7,6},{8,9},{9,8},{10,11... | collective-permute-start | bytes 3145736 | tf_op jit(solution)/shard_map/ppermute | solution.py:825
  38.6 28.7 %collective-permute-start.6 = (bf16[256,512]{1,0:T(8,128)(2,1)}, bf16[256,512]{1,0:T(8,128)(2,1)S(1)}, u32[]{:S(2)}, u32[]{:S(2)}) collective-permute-start(bf16[256,512]{1,0:T(8,128)(2,1)} %slice_bitcast_fusion.4), channel_id=1, source_target_pairs={{0,1},{1,0},{2,3},{3,2},{4,5},{5,4},{6,7},{7,6},{8,9},{9,8},{10,11... | collective-permute-start | bytes 786440 | tf_op jit(solution)/shard_map/ppermute | solution.py:825
  66.9 6.3 %copy-start = (bf16[16,2,64,512]{3,2,1,0:T(8,128)(2,1)}, bf16[16,2,64,512]{3,2,1,0:T(8,128)(2,1)S(1)}, u32[]{:S(2)}) copy-start(bf16[16,2,64,512]{3,2,1,0:T(8,128)(2,1)S(1)} %all-to-all-done.1.cot_ref) | copy-start | bytes 6291460
  67.3 5.8 %copy-start.8 = (bf16[256,512]{1,0:T(8,128)(2,1)}, bf16[256,512]{1,0:T(8,128)(2,1)S(1)}, u32[]{:S(2)}) copy-start(bf16[256,512]{1,0:T(8,128)(2,1)S(1)} %collective-permute-done.6.rest_3_) | copy-start | bytes 786436
  67.3 28.8 %all-to-all-start.2 = ((bf16[16,64,512]{2,1,0:T(8,128)(2,1)}), bf16[16,64,512]{2,1,0:T(8,128)(2,1)}, u32[]{:S(2)}, u32[]{:S(2)}) async-start(bf16[16,64,512]{2,1,0:T(8,128)(2,1)} %spread.3), calls=%async_computation.2 | async-start | bytes 2097152 | tf_op jit(solution)/shard_map/all_to_all | solution.py:833
  73.2 19.9 %collective-permute-start.4 = (bf16[768,512]{1,0:T(8,128)(2,1)S(1)}, bf16[768,512]{1,0:T(8,128)(2,1)S(1)}, u32[]{:S(2)}, u32[]{:S(2)}) collective-permute-start(bf16[768,512]{1,0:T(8,128)(2,1)S(1)} %slice_bitcast_fusion), channel_id=1, source_target_pairs={{0,1},{1,0},{2,3},{3,2},{4,5},{5,4},{6,7},{7,6},{8,9},{9,8},{10,11... | collective-permute-start | bytes 2359304 | tf_op jit(solution)/shard_map/ppermute | solution.py:825
  93.1 9.9 %copy-start.6 = (bf16[768,512]{1,0:T(8,128)(2,1)}, bf16[768,512]{1,0:T(8,128)(2,1)S(1)}, u32[]{:S(2)}) copy-start(bf16[768,512]{1,0:T(8,128)(2,1)S(1)} %collective-permute-done.4.rest_4_) | copy-start | bytes 2359300
  96.1 29.8 %all-to-all-start = ((bf16[16,64,512]{2,1,0:T(8,128)(2,1)}), bf16[16,64,512]{2,1,0:T(8,128)(2,1)S(1)}, u32[]{:S(2)}, u32[]{:S(2)}) async-start(bf16[16,64,512]{2,1,0:T(8,128)(2,1)} %spread.2), calls=%async_computation | async-start | bytes 2097152 | tf_op jit(solution)/shard_map/all_to_all | solution.py:833
  125.9 6.9 %copy-start.4 = (bf16[16,64,512]{2,1,0:T(8,128)(2,1)}, bf16[16,64,512]{2,1,0:T(8,128)(2,1)S(1)}, u32[]{:S(2)}) copy-start(bf16[16,64,512]{2,1,0:T(8,128)(2,1)S(1)} %all-to-all-done) | copy-start | bytes 3145732
  125.9 30.0 %all-to-all-start.4 = ((bf16[16,64,512]{2,1,0:T(8,128)(2,1)}), bf16[16,64,512]{2,1,0:T(8,128)(2,1)}, u32[]{:S(2)}, u32[]{:S(2)}) async-start(bf16[16,64,512]{2,1,0:T(8,128)(2,1)} %bitcast.55), calls=%async_computation.4 | async-start | bytes 2097152 | tf_op jit(solution)/shard_map/all_to_all | solution.py:833
  155.9 29.7 %all-to-all-start.3 = ((bf16[16,64,512]{2,1,0:T(8,128)(2,1)}), bf16[16,64,512]{2,1,0:T(8,128)(2,1)S(1)}, u32[]{:S(2)}, u32[]{:S(2)}) async-start(bf16[16,64,512]{2,1,0:T(8,128)(2,1)} %bitcast.54), calls=%async_computation.3 | async-start | bytes 2097152 | tf_op jit(solution)/shard_map/all_to_all | solution.py:833
  162.7 29.9 %collective-permute-start.9 = (bf16[512,1024]{1,0:T(8,128)(2,1)}, bf16[512,1024]{1,0:T(8,128)(2,1)S(1)}, u32[]{:S(2)}, u32[]{:S(2)}) collective-permute-start(bf16[512,1024]{1,0:T(8,128)(2,1)} %get-tuple-element.114), channel_id=1, source_target_pairs={{0,1},{1,0},{2,3},{3,2},{4,5},{5,4},{6,7},{7,6},{8,9},{9,8},{10,11... | collective-permute-start | bytes 3145736 | tf_op jit(solution)/shard_map/ppermute | solution.py:825
  165.2 27.4 %collective-permute-start.10 = (bf16[192,512]{1,0:T(8,128)(2,1)S(1)}, bf16[192,512]{1,0:T(8,128)(2,1)S(1)}, u32[]{:S(2)}, u32[]{:S(2)}) collective-permute-start(bf16[192,512]{1,0:T(8,128)(2,1)S(1)} %slice.56), channel_id=1, source_target_pairs={{0,1},{1,0},{2,3},{3,2},{4,5},{5,4},{6,7},{7,6},{8,9},{9,8},{10,11... | collective-permute-start | bytes 589832 | tf_op jit(solution)/shard_map/ppermute | solution.py:825
  185.7 1.0 copy-start.1
  192.6 50.6 %all-to-all-start.5 = ((bf16[16,2,64,512]{3,2,1,0:T(8,128)(2,1)}), bf16[16,2,64,512]{3,2,1,0:T(8,128)(2,1)S(1)}, u32[]{:S(2)}, u32[]{:S(2)}) async-start(bf16[16,2,64,512]{3,2,1,0:T(8,128)(2,1)} %get-tuple-element.128), calls=%async_computation.5 | async-start | bytes 4194304 | tf_op jit(solution)/shard_map/all_to_all | solution.py:833
  199.4 2.8 copy-start.17
  199.4 23.0 %collective-permute-start.7 = (bf16[4,208,512]{2,1,0:T(8,128)(2,1)}, bf16[4,208,512]{2,1,0:T(8,128)(2,1)S(1)}, u32[]{:S(2)}, u32[]{:S(2)}) collective-permute-start(bf16[4,208,512]{2,1,0:T(8,128)(2,1)} %get-tuple-element.111), channel_id=1, source_target_pairs={{0,1},{1,0},{2,3},{3,2},{4,5},{5,4},{6,7},{7,6},{8,9},{9,8},{10,11... | collective-permute-start | bytes 2555912 | tf_op jit(solution)/shard_map/ppermute | solution.py:825
  202.2 20.2 %collective-permute-start.8 = (f32[4,16,208]{2,1,0:T(8,128)S(1)}, f32[4,16,208]{2,1,0:T(8,128)S(1)}, u32[]{:S(2)}, u32[]{:S(2)}) collective-permute-start(f32[4,16,208]{2,1,0:T(8,128)S(1)} %copy-done.17), channel_id=1, source_target_pairs={{0,1},{1,0},{2,3},{3,2},{4,5},{5,4},{6,7},{7,6},{8,9},{9,8},{10,11... | collective-permute-start | bytes 159752 | tf_op jit(solution)/shard_map/ppermute | solution.py:825
  222.4 1.6 copy-start.16
  222.4 1.6 copy-start.10
  222.4 20.8 %collective-permute-start.11 = (bf16[832,512]{1,0:T(8,128)(2,1)S(1)}, bf16[832,512]{1,0:T(8,128)(2,1)}, u32[]{:S(2)}, u32[]{:S(2)}) collective-permute-start(bf16[832,512]{1,0:T(8,128)(2,1)S(1)} %slice.57), channel_id=1, source_target_pairs={{0,1},{1,0},{2,3},{3,2},{4,5},{5,4},{6,7},{7,6},{8,9},{9,8},{10,11... | collective-permute-start | bytes 2555912 | tf_op jit(solution)/shard_map/ppermute | solution.py:825
  243.2 3.2 collective-permute-start.12
  243.3 21.9 %collective-permute-start.14 = (bf16[4,208,512]{2,1,0:T(8,128)(2,1)}, bf16[4,208,512]{2,1,0:T(8,128)(2,1)}, u32[]{:S(2)}, u32[]{:S(2)}) collective-permute-start(bf16[4,208,512]{2,1,0:T(8,128)(2,1)} %get-tuple-element.133.refs_0_), channel_id=1, source_target_pairs={{0,1},{1,0},{2,3},{3,2},{4,5},{5,4},{6,7},{7,6},{8,9},{9,8},{10,11... | collective-permute-start | bytes 2555912 | tf_op jit(solution)/shard_map/ppermute | solution.py:825
  249.1 15.0 %collective-permute-start.13 = (bf16[2,544,256]{2,1,0:T(8,128)(2,1)}, bf16[2,544,256]{2,1,0:T(8,128)(2,1)}, u32[]{:S(2)}, u32[]{:S(2)}) collective-permute-start(bf16[2,544,256]{2,1,0:T(8,128)(2,1)} %constant_dynamic-slice_fusion.4), channel_id=1, source_target_pairs={{0,4},{2,6},{4,0},{6,2},{8,12},{10,14},{12,8},{14,10},{16,20},{18,... | collective-permute-start | bytes 1671176 | tf_op jit(solution)/shard_map/ppermute | solution.py:933
  265.3 11.9 %collective-permute-start.15 = (bf16[2,272,256]{2,1,0:T(8,128)(2,1)S(1)}, bf16[2,272,256]{2,1,0:T(8,128)(2,1)S(1)}, u32[]{:S(2)}, u32[]{:S(2)}) collective-permute-start(bf16[2,272,256]{2,1,0:T(8,128)(2,1)S(1)} %constant_dynamic-slice_fusion.2), channel_id=1, source_target_pairs={{0,8},{2,10},{4,12},{6,14},{8,0},{10,2},{12,4},{14,6},{16,24},{18,... | collective-permute-start | bytes 835592 | tf_op jit(solution)/shard_map/ppermute | solution.py:933
  270.6 20.6 %collective-permute-start.17 = (bf16[4,208,512]{2,1,0:T(8,128)(2,1)}, bf16[4,208,512]{2,1,0:T(8,128)(2,1)S(1)}, u32[]{:S(2)}, u32[]{:S(2)}) collective-permute-start(bf16[4,208,512]{2,1,0:T(8,128)(2,1)} %get-tuple-element.159), channel_id=1, source_target_pairs={{0,1},{1,0},{2,3},{3,2},{4,5},{5,4},{6,7},{7,6},{8,9},{9,8},{10,11... | collective-permute-start | bytes 2555912 | tf_op jit(solution)/shard_map/ppermute | solution.py:825
  277.3 10.0 %collective-permute-start.16 = (bf16[2,136,256]{2,1,0:T(8,128)(2,1)S(1)}, bf16[2,136,256]{2,1,0:T(8,128)(2,1)S(1)}, u32[]{:S(2)}, u32[]{:S(2)}) collective-permute-start(bf16[2,136,256]{2,1,0:T(8,128)(2,1)S(1)} %constant_dynamic-slice_fusion.1), channel_id=1, source_target_pairs={{0,16},{2,18},{4,20},{6,22},{8,24},{10,26},{12,28},{14,30},{16,0},... | collective-permute-start | bytes 417800 | tf_op jit(solution)/shard_map/ppermute | solution.py:933
  283.5 9.2 %copy-start.3 = (f32[4,208,512]{2,1,0:T(8,128)S(1)}, f32[4,208,512]{2,1,0:T(8,128)}, u32[]{:S(2)}) copy-start(f32[4,208,512]{2,1,0:T(8,128)} %get-tuple-element.117.rest_4_) | copy-start | bytes 5111812
  291.2 4.3 %collective-permute-start.18 = (bf16[136,256]{1,0:T(8,128)(2,1)S(1)}, bf16[136,256]{1,0:T(8,128)(2,1)S(1)}, u32[]{:S(2)}, u32[]{:S(2)}) collective-permute-start(bf16[136,256]{1,0:T(8,128)(2,1)S(1)} %slice_bitcast_fusion.5), channel_id=1, source_target_pairs={{0,1},{1,0},{2,3},{3,2},{4,5},{5,4},{6,7},{7,6},{8,9},{9,8},{10,11... | collective-permute-start | bytes 208904 | tf_op jit(solution)/shard_map/ppermute | solution.py:825
  293.0 21.9 %copy-start.5 = (bf16[4,208,512]{2,1,0:T(8,128)(2,1)}, bf16[4,208,512]{2,1,0:T(8,128)(2,1)S(1)}, u32[]{:S(2)}) copy-start(bf16[4,208,512]{2,1,0:T(8,128)(2,1)S(1)} %add_convert_fusion.1.refs_0_) | copy-start | bytes 2555908
  295.5 6.0 %collective-permute-start.19 = (bf16[136,256]{1,0:T(8,128)(2,1)S(1)}, bf16[136,256]{1,0:T(8,128)(2,1)S(1)}, u32[]{:S(2)}, u32[]{:S(2)}) collective-permute-start(bf16[136,256]{1,0:T(8,128)(2,1)S(1)} %fusion.1), channel_id=1, source_target_pairs={{0,16},{2,18},{4,20},{6,22},{8,24},{10,26},{12,28},{14,30},{16,0},... | collective-permute-start | bytes 208904 | tf_op jit(solution)/shard_map/ppermute | solution.py:933
  297.0 17.9 %collective-permute-start.22 = (bf16[4,208,512]{2,1,0:T(8,128)(2,1)S(1)}, bf16[4,208,512]{2,1,0:T(8,128)(2,1)S(1)}, u32[]{:S(2)}, u32[]{:S(2)}) collective-permute-start(bf16[4,208,512]{2,1,0:T(8,128)(2,1)S(1)} %add_convert_fusion.1.refs_0_), channel_id=1, source_target_pairs={{0,1},{1,0},{2,3},{3,2},{4,5},{5,4},{6,7},{7,6},{8,9},{9,8},{10,11... | collective-permute-start | bytes 2555912 | tf_op jit(solution)/shard_map/ppermute | solution.py:825
  301.5 5.1 %collective-permute-start.20 = (bf16[272,256]{1,0:T(8,128)(2,1)S(1)}, bf16[272,256]{1,0:T(8,128)(2,1)S(1)}, u32[]{:S(2)}, u32[]{:S(2)}) collective-permute-start(bf16[272,256]{1,0:T(8,128)(2,1)S(1)} %maximum_select_fusion.3), channel_id=1, source_target_pairs={{0,8},{2,10},{4,12},{6,14},{8,0},{10,2},{12,4},{14,6},{16,24},{18,... | collective-permute-start | bytes 417800 | tf_op jit(solution)/shard_map/ppermute | solution.py:933
  306.8 6.6 %collective-permute-start.21 = (bf16[544,256]{1,0:T(8,128)(2,1)S(1)}, bf16[544,256]{1,0:T(8,128)(2,1)S(1)}, u32[]{:S(2)}, u32[]{:S(2)}) collective-permute-start(bf16[544,256]{1,0:T(8,128)(2,1)S(1)} %maximum_select_fusion.2), channel_id=1, source_target_pairs={{0,4},{2,6},{4,0},{6,2},{8,12},{10,14},{12,8},{14,10},{16,20},{18,... | collective-permute-start | bytes 835592 | tf_op jit(solution)/shard_map/ppermute | solution.py:933
  314.9 0.9 copy-start.9
  314.9 4.0 %collective-permute-start.23 = (bf16[1088,256]{1,0:T(8,128)(2,1)S(1)}, bf16[1088,256]{1,0:T(8,128)(2,1)S(1)}, u32[]{:S(2)}, u32[]{:S(2)}) collective-permute-start(bf16[1088,256]{1,0:T(8,128)(2,1)S(1)} %maximum_select_fusion.1), channel_id=1, source_target_pairs={{0,2},{2,0},{4,6},{6,4},{8,10},{10,8},{12,14},{14,12},{16,18},{18,... | collective-permute-start | bytes 1671176 | tf_op jit(solution)/shard_map/ppermute | solution.py:933

commit v3 on v2

--- a/solution.py
+++ b/solution.py
@@ -10,6 +10,7 @@
 HEAD_DIM = 64
 SEQ = 197
 PAD = 208
+SENT = 200
 EPS = 1e-06
 F32 = jnp.float32
 BF16 = jnp.bfloat16
@@ -543,17 +544,17 @@
 
             value = nn(match, slot_grads[...])
             grads = value if grads is None else grads + value
-    out_ref[0] = total.astype(out_ref.dtype)
+    out_ref[0] = total[: out_ref.shape[1]].astype(out_ref.dtype)
     if probs:
         turned = grads.T
         value = turned[:experts] + turned[experts:]
         rest[0][0] = value + old[1][0] if old else value
 
 
-def collect(first, code_col, parts, own, dtype, half, block, probs=False, numbers=None, before=()):
+def collect(first, code_col, parts, own, dtype, half, block, probs=False, numbers=None, before=(), rows=PAD):
     numbers = tuple(range(len(parts))) if numbers is None else numbers
     count, width = parts[0].shape
-    outs = [jax.ShapeDtypeStruct((own, PAD, width), dtype)]
+    outs = [jax.ShapeDtypeStruct((own, rows, width), dtype)]
     if probs:
         outs.append(jax.ShapeDtypeStruct((own, count // block, PAD), F32))
     return pl.pallas_call(
@@ -619,7 +620,9 @@
     grad_probs = gp_ref[...]
     grad_routed = flat(sum_ref)
     if received:
-        grad_routed = grad_routed + flat(more[0])
+        tail = jnp.zeros((PAD - more[0].shape[1], model), F32)
+        both = [v for b in range(batch) for v in (more[0][b].astype(F32), tail)]
+        grad_routed = grad_routed + jnp.concatenate(both, axis=0)
         grad_probs = grad_probs + more[1][...]
     grad_probs = jnp.concatenate([grad_probs[g] for g in range(batch)], axis=1)
     grad_logits = probs * (grad_probs - jnp.sum(probs * grad_probs, axis=0, keepdims=True))
@@ -678,7 +681,8 @@
     small[experts : experts + 1, :] += jnp.sum(grad_normed * xin, axis=0, keepdims=True)
     h = grad_normed * ga
     grad_tok = grad_res + tok_scale * (h - row_mean(h) - xin * row_mean(h * xin))
-    gtok_ref[...] = grad_tok.astype(BF16).reshape(gtok_ref.shape)
+    for b in range(batch):
+        gtok_ref[b] = grad_tok[b * PAD : b * PAD + gtok_ref.shape[1]].astype(BF16)
 
     @pl.when(step == steps - 1)
     def _():
@@ -725,12 +729,12 @@
     flat = [v for pair in sums for v in pair]
     return pl.pallas_call(
         functools.partial(back_kernel, steps=own // batch, received=len(sums) - 1, split=split),
-        out_shape=(jax.ShapeDtypeStruct((own, PAD, width), BF16),)
+        out_shape=(jax.ShapeDtypeStruct((own, SENT, width), BF16),)
         + (jax.ShapeDtypeStruct((shards, rows // (1 + split), 256), BF16),) * (1 + split),
         grid_spec=pltpu.PrefetchScalarGridSpec(
             num_scalar_prefetch=1,
             grid=(own // batch,),
-            in_specs=[mine(PAD, width), mine(experts, PAD)] * len(sums)
+            in_specs=[mine(*v.shape[1:]) for v in flat]
             + [
                 mine(PAD, width),
                 image,
@@ -744,7 +748,7 @@
                 pl.BlockSpec(memory_space=pl.ANY),
                 mine(*att.shape[1:]),
             ],
-            out_specs=(mine(PAD, width),) + (full((shards, rows // (1 + split), 256)),) * (1 + split),
+            out_specs=(mine(SENT, width),) + (full((shards, rows // (1 + split), 256)),) * (1 + split),
             scratch_shapes=[
                 pltpu.VMEM((width, 3 * width), F32),
                 pltpu.VMEM((width, width), F32),
@@ -838,8 +842,8 @@
     def rows_of(v):
         return v.reshape(-1, width)
 
-    def collected(number, parts, dtype, probs=False, numbers=None, before=()):
-        return collect(number, code_col, parts, own, dtype, half, block, probs, numbers, before)
+    def collected(number, parts, dtype, probs=False, numbers=None, before=(), rows=PAD):
+        return collect(number, code_col, parts, own, dtype, half, block, probs, numbers, before, rows)
 
     if ways == 2:
         core = expert % 2
@@ -902,7 +906,7 @@
         zero = jnp.zeros((1,), jnp.int32)
         start = collect(zero, code_col, gin[:1], images, F32, half, block, True, (0,))
         gin[1], *start = lax.optimization_barrier((gin[1], *start))
-        sent = collected(there, gin[1:], BF16, True, (1,), start)
+        sent = collected(there, gin[1:], BF16, True, (1,), start, SENT)
         received = tuple(other(v) for v in sent)
         mine = collected(first, gin[1:], F32, True, (1,), start)
         gated = exchange(after(gated, *sent, dw1_peer, dw2_peer[0]))
@@ -945,7 +949,7 @@
         keep, give, grad_tok, gated, dw2_peer[1] = lax.optimization_barrier((*pack, grad_tok, gated, dw2_peer[1]))
         grad_peer = other(grad_tok)
         gated = [rows_of(gated[:, c]) for c in range(chunks)]
-        (mix,) = collect(zero, code_col, gated, images, BF16, half, block)
+        (mix,) = collect(zero, code_col, gated, images, BF16, half, block, rows=SENT)
         mix_there = lax.dynamic_slice_in_dim(mix, (1 - rank) * own, own, 0)
         mix_here = lax.dynamic_slice_in_dim(mix, rank * own, own, 0)
         pack = add(keep, swap_bit(give, bits[0]))
@@ -962,7 +966,7 @@
         )
         pack, mix_peer, grad_tokens = lax.optimization_barrier((pack, mix_peer, grad_tokens))
         swapped = other(pack[1])
-        result = (residual + (mix_here.astype(F32) + mix_peer.astype(F32))).astype(BF16)
+        result = (residual[:, :SENT] + (mix_here.astype(F32) + mix_peer.astype(F32))).astype(BF16)
         swapped, result = lax.optimization_barrier((swapped, result))
         result_peer = other(result)
         total = add(pack[0], swapped)

time: 324 us -> 323 us (level)
  no operation moved by 1% of the time
where the time goes in v3:
time: 323 us; the launch traced here: 321 us
  Pallas kernels  146 us (45%)
  waiting for transfers between devices  75.4 us (23%)
  starting transfers between devices  72 us (22%)
  other arithmetic  14.9 us (5%)
  local copies, waits for them, and re-layouts  12 us (4%)
    pallas_call x2, Pallas kernels, experts_step(): pl.pallas_call(functools.partial(expert_kernel, parts=parts, half=half, b...  45.2 us
    all_to_all x6, starting transfers between devices, exchange(): lax.all_to_all(rows, 'expert', split_axis=0, concat_axis=0, tiled=True)  40.7 us
    ppermute x14, waiting for transfers between devices, other(): return lax.ppermute(v, 'tensor', swap)  37.7 us
    pallas_call x4, Pallas kernels, collect(): pl.pallas_call(functools.partial(collect_kernel, numbers=numbers, half=ha...  28.9 us
    pallas_call x1, Pallas kernels, attend(): pl.pallas_call(functools.partial(attend_kernel, pieces=pieces, own=own),...  22.2 us
    ppermute x8, waiting for transfers between devices, swap_bit(): return lax.ppermute(v, 'expert', [(i, i ^ bit) for i in range(groups)])  21.5 us
    pallas_call x1, Pallas kernels, back(): pl.pallas_call(functools.partial(back_kernel, steps=own // batch, receive...  19.2 us
    ppermute x14, starting transfers between devices, other(): return lax.ppermute(v, 'tensor', swap)  17.5 us
  transfers between devices with their start and end apart: 30, of which 18 were waited for; matrix products, arithmetic and copies ran while one was open for 6% of the time, Pallas kernels for 42%

profile of v3, /device:TPU:0, one launch (start us, length us, event | category | flops | bytes accessed | tf_op | source)
XLA Modules:
  0.0 321.2 jit_solution(8891322634097757090)
XLA Ops:
  2.8 9.6 %front.1 = (bf16[8,208,512]{2,1,0:T(8,128)(2,1)}, bf16[16,2,64,512]{3,2,1,0:T(8,128)(2,1)}, s32[208,16]{1,0:T(8,128)}, s32[2,1664]{1,0:T(2,128)}) custom-call(s32[1]{0:T(128)} %bitcast.2.rank_ref, bf16[1576,512]{1,0:T(8,128)(2,1)} %cot_ref.1, s32[16,208]{1,0:T(8,128)} %get-tuple-element.163.col_ref, s32[2,1664]{1,0:T(2,128)} %reshape.75.row_ref), custom_call_target="tpu_custom_call" | custom-call | bytes 36900000 | tf_op jit(solution)/shard_map/front/pallas_call | solution.py:151
  12.4 7.5 %all-to-all-start.1 = ((bf16[16,2,64,512]{3,2,1,0:T(8,128)(2,1)}), bf16[16,2,64,512]{3,2,1,0:T(8,128)(2,1)S(1)}, u32[]{:S(2)}, u32[]{:S(2)}) async-start(bf16[16,2,64,512]{3,2,1,0:T(8,128)(2,1)} %get-tuple-element.81), calls=%async_computation.1 | async-start | bytes 4194304 | tf_op jit(solution)/shard_map/all_to_all | solution.py:837
  20.0 1.6 collective-permute-start
  22.2 4.2 %pad.74.tok_ref.rest_6_ = bf16[8,208,512]{2,1,0:T(8,128)(2,1)} custom-call(bf16[1576,512]{1,0:T(8,128)(2,1)} %source), custom_call_target="tpu_custom_call" | custom-call | bytes 7380000 | tf_op jit(solution)/shard_map/pad/pallas_call | solution.py:67
  26.4 7.9 %collective-permute-done.1.rest_4_ = bf16[128,512]{1,0:T(8,128)(2,1)S(1)} collective-permute-done((bf16[128,512]{1,0:T(8,128)(2,1)S(1)}, bf16[128,512]{1,0:T(8,128)(2,1)S(1)}, u32[]{:S(2)}, u32[]{:S(2)}) %collective-permute-start.1) | collective-permute-done | bytes 131104 | tf_op jit(solution)/shard_map/ppermute | solution.py:829
  36.3 1.6 collective-permute-start.5
  39.8 22.2 %attend.1 = (bf16[8,208,512]{2,1,0:T(8,128)(2,1)}, f32[4,208,512]{2,1,0:T(8,128)}, bf16[4,208,1536]{2,1,0:T(8,128)(2,1)}, bf16[4,2,832,208]{3,2,1,0:T(8,128)(2,1...) custom-call(s32[2]{0:T(128)} %pad_add_fusion.place_ref, ...), custom_call_target="tpu_custom_call" | custom-call | bytes 92250000 | tf_op jit(solution)/shard_map/attend/pallas_call | solution.py:300
  62.0 4.9 %spread.3 = bf16[16,64,512]{2,1,0:T(8,128)(2,1)} custom-call(s32[2,1664]{1,0:T(2,128)} %get-tuple-element.80.code_ref, bf16[1664,512]{1,0:T(8,128)(2,1)} %bitcast.47), custom_call_target="tpu_custom_call" | custom-call | bytes 18450000 | tf_op jit(solution)/shard_map/spread/pallas_call | solution.py:178
  67.3 5.8 %all-to-all-start.2 = ((bf16[16,64,512]{2,1,0:T(8,128)(2,1)}), bf16[16,64,512]{2,1,0:T(8,128)(2,1)}, u32[]{:S(2)}, u32[]{:S(2)}) async-start(bf16[16,64,512]{2,1,0:T(8,128)(2,1)} %spread.3), calls=%async_computation.2 | async-start | bytes 2097152 | tf_op jit(solution)/shard_map/all_to_all | solution.py:837
  73.2 1.6 collective-permute-start.4
  74.8 4.8 %spread.2 = bf16[16,64,512]{2,1,0:T(8,128)(2,1)} custom-call(s32[2,1664]{1,0:T(2,128)} %get-tuple-element.80.code_ref, bf16[1664,512]{1,0:T(8,128)(2,1)} %bitcast.48), custom_call_target="tpu_custom_call" | custom-call | bytes 18450000 | tf_op jit(solution)/shard_map/spread/pallas_call | solution.py:178
  79.6 13.5 %collective-permute-done.4.rest_4_ = bf16[768,512]{1,0:T(8,128)(2,1)S(1)} collective-permute-done((bf16[768,512]{1,0:T(8,128)(2,1)S(1)}, bf16[768,512]{1,0:T(8,128)(2,1)S(1)}, u32[]{:S(2)}, u32[]{:S(2)}) %collective-permute-start.4) | collective-permute-done | bytes 786464 | tf_op jit(solution)/shard_map/ppermute | solution.py:829
  93.1 3.0 all-to-all-done.2
  96.1 6.9 %all-to-all-start = ((bf16[16,64,512]{2,1,0:T(8,128)(2,1)}), bf16[16,64,512]{2,1,0:T(8,128)(2,1)S(1)}, u32[]{:S(2)}, u32[]{:S(2)}) async-start(bf16[16,64,512]{2,1,0:T(8,128)(2,1)} %spread.2), calls=%async_computation | async-start | bytes 2097152 | tf_op jit(solution)/shard_map/all_to_all | solution.py:837
  103.0 22.1 %experts.2 = (bf16[1024,512]{1,0:T(8,128)(2,1)}, bf16[16,2,64,512]{3,2,1,0:T(8,128)(2,1)}, f32[512,1024]{1,0:T(8,128)}, f32[512,1024]{1,0:T(8,128)}, f32[1024,512]{1,0:T(8,128)}, /*index=5*/f32[1024,512]{1,0:T(8,128)}) custom-call(s32[1]{0:T(128)} %bitcast.5.expert_ref, bf16[1024,512]{1,0:T(8,128)(2,1)} %bitcast.15.x_ref, bf16[16,2,64,512]{3,2,1,0:T(8,128)(2,1)} %copy-done, ...), custom_call_target="tpu_custom_call" | custom-call | bytes 73800000 | tf_op jit(solution)/shard_map/experts/pallas_call | solution.py:464
  125.9 6.9 %all-to-all-start.4 = ((bf16[16,64,512]{2,1,0:T(8,128)(2,1)}), bf16[16,64,512]{2,1,0:T(8,128)(2,1)}, u32[]{:S(2)}, u32[]{:S(2)}) async-start(bf16[16,64,512]{2,1,0:T(8,128)(2,1)} %bitcast.55), calls=%async_computation.4 | async-start | bytes 2097152 | tf_op jit(solution)/shard_map/all_to_all | solution.py:837
  132.9 23.1 %experts.3 = (bf16[1024,512]{1,0:T(8,128)(2,1)}, bf16[16,2,64,512]{3,2,1,0:T(8,128)(2,1)}, f32[512,1024]{1,0:T(8,128)}, bf16[512,1024]{1,0:T(8,128)(2,1)}, f32[1...) custom-call(s32[1]{0:T(128)} %bitcast.5.expert_ref, bf16[1024,512]{1,0:T(8,128)(2,1)} %bitcast.49, ...), custom_call_target="tpu_custom_call", output_to_operand_aliasing={{1}: (13, {})} | custom-call | bytes 73800000 | tf_op jit(solution)/shard_map/experts/pallas_call | solution.py:464
  155.9 6.8 %all-to-all-start.3 = ((bf16[16,64,512]{2,1,0:T(8,128)(2,1)}), bf16[16,64,512]{2,1,0:T(8,128)(2,1)S(1)}, u32[]{:S(2)}, u32[]{:S(2)}) async-start(bf16[16,64,512]{2,1,0:T(8,128)(2,1)} %bitcast.54), calls=%async_computation.3 | async-start | bytes 2097152 | tf_op jit(solution)/shard_map/all_to_all | solution.py:837
  162.7 1.6 collective-permute-start.9
  165.8 8.9 %collect.4 = (f32[8,208,512]{2,1,0:T(8,128)}, f32[8,16,208]{2,1,0:T(8,128)}) custom-call(s32[1]{0:T(128)} %constant.99.clone.1.first_ref, s32[208,16]{1,0:T(8,128)} %get-tuple-element.79.code_ref, bf16[1024,512]{1,0:T(8,128)(2,1)} %bitcast.19.rest_0_), custom_call_target="tpu_custom_call" | custom-call | bytes 25830000 | tf_op jit(solution)/shard_map/collect/pallas_call | solution.py:560
  174.7 10.9 %all-to-all-done.3 = bf16[16,64,512]{2,1,0:T(8,128)(2,1)S(1)} async-done(((bf16[16,64,512]{2,1,0:T(8,128)(2,1)}), bf16[16,64,512]{2,1,0:T(8,128)(2,1)S(1)}, u32[]{:S(2)}, u32[]{:S(2)}) %all-to-all-start.3) | async-done | bytes 1048608 | tf_op jit(solution)/shard_map/all_to_all | solution.py:837
  186.6 5.9 %collect.6 = (bf16[4,200,512]{2,1,0:T(8,128)(2,1)}, f32[4,16,208]{2,1,0:T(8,128)}) custom-call(s32[1]{0:T(128)} %bitcast.20.first_ref, s32[208,16]{1,0:T(8,128)} %get-tuple-element.79.code_ref, bf16[1024,512]{1,0:T(8,128)(2,1)} %bitcast.43, f32[8,208,512]{2,1,0:T(8,128)} %get-tuple-element.107.rest_1_, f32[8,16,208]{2,1,0:T(8,128)} %get-tuple-element.108.rest_2_), custom_call_target="tpu_custom_call" | custom-call | bytes 25830000 | tf_op jit(solution)/shard_map/collect/pallas_call | solution.py:560
  192.6 6.8 %all-to-all-start.5 = ((bf16[16,2,64,512]{3,2,1,0:T(8,128)(2,1)}), bf16[16,2,64,512]{3,2,1,0:T(8,128)(2,1)S(1)}, u32[]{:S(2)}, u32[]{:S(2)}) async-start(bf16[16,2,64,512]{3,2,1,0:T(8,128)(2,1)} %get-tuple-element.128), calls=%async_computation.5 | async-start | bytes 4194304 | tf_op jit(solution)/shard_map/all_to_all | solution.py:837
  199.4 1.6 collective-permute-start.7
  202.8 3.4 %convert_add_fusion.1 = f32[512,1024]{1,0:T(8,128)} fusion(f32[512,1024]{1,0:T(8,128)} %get-tuple-element.113, bf16[512,1024]{1,0:T(8,128)(2,1)S(1)} %collective-permute-done.9), kind=kLoop, calls=%fused_computation.2 | loop fusion | flops 1048576 | bytes 5242880 | tf_op jit(solution)/shard_map/add | solution.py:913
  206.2 5.9 %collect.5 = (f32[4,208,512]{2,1,0:T(8,128)}, f32[4,16,208]{2,1,0:T(8,128)}) custom-call(s32[1]{0:T(128)} %bitcast.first_ref, s32[208,16]{1,0:T(8,128)} %get-tuple-element.79.code_ref, bf16[1024,512]{1,0:T(8,128)(2,1)} %bitcast.44, f32[8,208,512]{2,1,0:T(8,128)} %get-tuple-element.107.rest_1_, f32[8,16,208]{2,1,0:T(8,128)} %get-tuple-element.108.rest_2_), custom_call_target="tpu_custom_call" | custom-call | bytes 25830000 | tf_op jit(solution)/shard_map/collect/pallas_call | solution.py:560
  212.0 9.7 %collective-permute-done.8.rest_3_ = f32[4,16,208]{2,1,0:T(8,128)S(1)} collective-permute-done((f32[4,16,208]{2,1,0:T(8,128)S(1)}, f32[4,16,208]{2,1,0:T(8,128)S(1)}, u32[]{:S(2)}, u32[]{:S(2)}) %collective-permute-start.8) | collective-permute-done | bytes 53280 | tf_op jit(solution)/shard_map/ppermute | solution.py:829
  221.7 1.6 collective-permute-start.11
  223.3 19.2 %back.1 = (bf16[4,200,512]{2,1,0:T(8,128)(2,1)}, bf16[2,1088,256]{2,1,0:T(8,128)(2,1)}, bf16[2,1088,256]{2,1,0:T(8,128)(2,1)}) custom-call(s32[2]{0:T(128)} %pad_add_fusion.place_ref, f32[4,208,512]{2,1,0:T(8,128)} %get-tuple-element.109.rest_0_, f32[4,16,208]{2,1,0:T(8,128)} %get-tuple-element.110.rest_1_, bf16[4,200,512]{2,1,0:T(8,128)(2,1)} %copy-done.10, ...), custom_call_target="tpu_custom_call" | custom-call | bytes 59040000 | tf_op jit(solution)/shard_map/back/pallas_call | solution.py:730
  243.9 1.8 collective-permute-done.12
  245.7 1.9 add_convert_fusion
  248.4 1.7 collective-permute-start.13
  251.6 8.2 %collect.7 = bf16[8,200,512]{2,1,0:T(8,128)(2,1)} custom-call(s32[1]{0:T(128)} %constant.99.clone.1.first_ref, s32[208,16]{1,0:T(8,128)} %get-tuple-element.79.code_ref, bf16[1024,512]{1,0:T(8,128)(2,1)} %bitcast.51, bf16[1024,512]{1,0:T(8,128)(2,1)} %bitcast.50), custom_call_target="tpu_custom_call" | custom-call | bytes 25830000 | tf_op jit(solution)/shard_map/collect/pallas_call | solution.py:560
  259.8 2.4 constant_dynamic-slice_fusion
  264.8 5.8 %collective-permute-start.15 = (bf16[2,272,256]{2,1,0:T(8,128)(2,1)S(1)}, bf16[2,272,256]{2,1,0:T(8,128)(2,1)S(1)}, u32[]{:S(2)}, u32[]{:S(2)}) collective-permute-start(bf16[2,272,256]{2,1,0:T(8,128)(2,1)S(1)} %constant_dynamic-slice_fusion.2), channel_id=1, source_target_pairs={{0,8},{2,10},{4,12},{6,14},{8,0},{10,2},{12,4},{14,6},{16,24},{18,... | collective-permute-start | bytes 835592 | tf_op jit(solution)/shard_map/ppermute | solution.py:937
  270.6 1.5 collective-permute-start.17
  272.1 5.1 %collective-permute-done.15 = bf16[2,272,256]{2,1,0:T(8,128)(2,1)S(1)} collective-permute-done((bf16[2,272,256]{2,1,0:T(8,128)(2,1)S(1)}, bf16[2,272,256]{2,1,0:T(8,128)(2,1)S(1)}, u32[]{:S(2)}, u32[]{:S(2)}) %collective-permute-start.15) | collective-permute-done | bytes 278560 | tf_op jit(solution)/shard_map/ppermute | solution.py:937
  277.3 2.7 collective-permute-start.16
  280.0 3.4 %convert_add_fusion = f32[1024,512]{1,0:T(8,128)} fusion(f32[1024,512]{1,0:T(8,128)} %get-tuple-element.135, bf16[832,512]{1,0:T(8,128)(2,1)} %collective-permute-done.11, bf16[192,512]{1,0:T(8,128)(2,1)S(1)} %collective-permute-done.10), kind=kLoop, calls=%fused_computation.1 | loop fusion | flops 2621440 | bytes 5242880 | tf_op jit(solution)/shard_map/add | solution.py:965
  283.5 3.8 %unpad.2 = f32[1576,512]{1,0:T(8,128)} custom-call(s32[1]{0:T(128)} %bitcast.first_ref, bf16[4,200,512]{2,1,0:T(8,128)(2,1)} %get-tuple-element.133.refs_0_, bf16[4,200,512]{2,1,0:T(8,128)(2,1)} %collective-permute-done.14.refs_1_), custom_call_target="tpu_custom_call" | custom-call | bytes 7380000 | tf_op jit(solution)/shard_map/unpad/pallas_call | solution.py:801
  287.3 3.2 collective-permute-done.17
  290.5 1.5 collective-permute-start.18
  292.4 2.4 collective-permute-done.18
  296.3 1.5 collective-permute-start.22
  297.8 3.0 collective-permute-done.19
  300.9 5.0 %collective-permute-done.20 = bf16[272,256]{1,0:T(8,128)(2,1)S(1)} collective-permute-done((bf16[272,256]{1,0:T(8,128)(2,1)S(1)}, bf16[272,256]{1,0:T(8,128)(2,1)S(1)}, u32[]{:S(2)}, u32[]{:S(2)}) %collective-permute-start.20) | collective-permute-done | bytes 139296 | tf_op jit(solution)/shard_map/ppermute | solution.py:937
  307.5 5.2 %collective-permute-done.21 = bf16[544,256]{1,0:T(8,128)(2,1)S(1)} collective-permute-done((bf16[544,256]{1,0:T(8,128)(2,1)S(1)}, bf16[544,256]{1,0:T(8,128)(2,1)S(1)}, u32[]{:S(2)}, u32[]{:S(2)}) %collective-permute-start.21) | collective-permute-done | bytes 278560 | tf_op jit(solution)/shard_map/ppermute | solution.py:937
  314.4 3.1 unpad.3
  (97 shorter events, 27.7 us)
Async XLA Ops:
  12.4 7.5 %copy-start.7 = (bf16[3,512,256]{2,1,0:T(8,128)(2,1)S(1)}, bf16[3,512,256]{2,1,0:T(8,128)(2,1)}, u32[]{:S(2)}) copy-start(bf16[3,512,256]{2,1,0:T(8,128)(2,1)} %rest_0_.1) | copy-start | bytes 2359300
  12.4 9.2 %copy-start.11 = (bf16[256,512]{1,0:T(8,128)(2,1)S(1)}, bf16[256,512]{1,0:T(8,128)(2,1)}, u32[]{:S(2)}) copy-start(bf16[256,512]{1,0:T(8,128)(2,1)} %rest_3_.1) | copy-start | bytes 786436
  12.4 54.5 %all-to-all-start.1 = ((bf16[16,2,64,512]{3,2,1,0:T(8,128)(2,1)}), bf16[16,2,64,512]{3,2,1,0:T(8,128)(2,1)S(1)}, u32[]{:S(2)}, u32[]{:S(2)}) async-start(bf16[16,2,64,512]{3,2,1,0:T(8,128)(2,1)} %get-tuple-element.81), calls=%async_computation.1 | async-start | bytes 4194304 | tf_op jit(solution)/shard_map/all_to_all | solution.py:837
  20.0 14.3 %collective-permute-start = (bf16[3,512,128]{2,1,0:T(8,128)(2,1)S(1)}, bf16[3,512,128]{2,1,0:T(8,128)(2,1)S(1)}, u32[]{:S(2)}, u32[]{:S(2)}) collective-permute-start(bf16[3,512,128]{2,1,0:T(8,128)(2,1)S(1)} %constant_dynamic-slice_fusion.6), channel_id=1, source_target_pairs={{0,1},{1,0},{2,3},{3,2},{4,5},{5,4},{6,7},{7,6},{8,9},{9,8},{10,11... | collective-permute-start | bytes 1179656 | tf_op jit(solution)/shard_map/ppermute | solution.py:829
  21.6 16.2 %copy-start.2 = (bf16[1,1024,512]{2,1,0:T(8,128)(2,1)S(1)}, bf16[1,1024,512]{2,1,0:T(8,128)(2,1)}, u32[]{:S(2)}) copy-start(bf16[1,1024,512]{2,1,0:T(8,128)(2,1)} %param.18) | copy-start | bytes 3145732
  21.6 12.7 %collective-permute-start.1 = (bf16[128,512]{1,0:T(8,128)(2,1)S(1)}, bf16[128,512]{1,0:T(8,128)(2,1)S(1)}, u32[]{:S(2)}, u32[]{:S(2)}) collective-permute-start(bf16[128,512]{1,0:T(8,128)(2,1)S(1)} %constant_dynamic-slice_fusion.5), channel_id=1, source_target_pairs={{0,1},{1,0},{2,3},{3,2},{4,5},{5,4},{6,7},{7,6},{8,9},{9,8},{10,11... | collective-permute-start | bytes 393224 | tf_op jit(solution)/shard_map/ppermute | solution.py:829
  34.3 5.5 %copy-start.14 = (bf16[128,512]{1,0:T(8,128)(2,1)}, bf16[128,512]{1,0:T(8,128)(2,1)S(1)}, u32[]{:S(2)}) copy-start(bf16[128,512]{1,0:T(8,128)(2,1)S(1)} %collective-permute-done.1.rest_4_) | copy-start | bytes 393220
  34.3 3.5 %copy-start.12 = (bf16[3,512,128]{2,1,0:T(8,128)(2,1)}, bf16[3,512,128]{2,1,0:T(8,128)(2,1)S(1)}, u32[]{:S(2)}) copy-start(bf16[3,512,128]{2,1,0:T(8,128)(2,1)S(1)} %collective-permute-done.rest_1_) | copy-start | bytes 1179652
  34.3 2.0 collective-permute-start.2
  34.4 1.9 collective-permute-start.3
  36.3 1.6 copy-start.15
  36.3 2.3 copy-start.13
  36.3 31.0 %collective-permute-start.5 = (bf16[512,1024]{1,0:T(8,128)(2,1)}, bf16[512,1024]{1,0:T(8,128)(2,1)}, u32[]{:S(2)}, u32[]{:S(2)}) collective-permute-start(bf16[512,1024]{1,0:T(8,128)(2,1)} %bitcast.12.rest_0_), channel_id=1, source_target_pairs={{0,1},{1,0},{2,3},{3,2},{4,5},{5,4},{6,7},{7,6},{8,9},{9,8},{10,11... | collective-permute-start | bytes 3145736 | tf_op jit(solution)/shard_map/ppermute | solution.py:829
  38.6 28.7 %collective-permute-start.6 = (bf16[256,512]{1,0:T(8,128)(2,1)}, bf16[256,512]{1,0:T(8,128)(2,1)S(1)}, u32[]{:S(2)}, u32[]{:S(2)}) collective-permute-start(bf16[256,512]{1,0:T(8,128)(2,1)} %slice_bitcast_fusion.4), channel_id=1, source_target_pairs={{0,1},{1,0},{2,3},{3,2},{4,5},{5,4},{6,7},{7,6},{8,9},{9,8},{10,11... | collective-permute-start | bytes 786440 | tf_op jit(solution)/shard_map/ppermute | solution.py:829
  66.9 6.3 %copy-start = (bf16[16,2,64,512]{3,2,1,0:T(8,128)(2,1)}, bf16[16,2,64,512]{3,2,1,0:T(8,128)(2,1)S(1)}, u32[]{:S(2)}) copy-start(bf16[16,2,64,512]{3,2,1,0:T(8,128)(2,1)S(1)} %all-to-all-done.1.cot_ref) | copy-start | bytes 6291460
  67.3 5.8 %copy-start.8 = (bf16[256,512]{1,0:T(8,128)(2,1)}, bf16[256,512]{1,0:T(8,128)(2,1)S(1)}, u32[]{:S(2)}) copy-start(bf16[256,512]{1,0:T(8,128)(2,1)S(1)} %collective-permute-done.6.rest_3_) | copy-start | bytes 786436
  67.3 28.8 %all-to-all-start.2 = ((bf16[16,64,512]{2,1,0:T(8,128)(2,1)}), bf16[16,64,512]{2,1,0:T(8,128)(2,1)}, u32[]{:S(2)}, u32[]{:S(2)}) async-start(bf16[16,64,512]{2,1,0:T(8,128)(2,1)} %spread.3), calls=%async_computation.2 | async-start | bytes 2097152 | tf_op jit(solution)/shard_map/all_to_all | solution.py:837
  73.2 19.9 %collective-permute-start.4 = (bf16[768,512]{1,0:T(8,128)(2,1)S(1)}, bf16[768,512]{1,0:T(8,128)(2,1)S(1)}, u32[]{:S(2)}, u32[]{:S(2)}) collective-permute-start(bf16[768,512]{1,0:T(8,128)(2,1)S(1)} %slice_bitcast_fusion), channel_id=1, source_target_pairs={{0,1},{1,0},{2,3},{3,2},{4,5},{5,4},{6,7},{7,6},{8,9},{9,8},{10,11... | collective-permute-start | bytes 2359304 | tf_op jit(solution)/shard_map/ppermute | solution.py:829
  93.1 9.9 %copy-start.6 = (bf16[768,512]{1,0:T(8,128)(2,1)}, bf16[768,512]{1,0:T(8,128)(2,1)S(1)}, u32[]{:S(2)}) copy-start(bf16[768,512]{1,0:T(8,128)(2,1)S(1)} %collective-permute-done.4.rest_4_) | copy-start | bytes 2359300
  96.1 29.8 %all-to-all-start = ((bf16[16,64,512]{2,1,0:T(8,128)(2,1)}), bf16[16,64,512]{2,1,0:T(8,128)(2,1)S(1)}, u32[]{:S(2)}, u32[]{:S(2)}) async-start(bf16[16,64,512]{2,1,0:T(8,128)(2,1)} %spread.2), calls=%async_computation | async-start | bytes 2097152 | tf_op jit(solution)/shard_map/all_to_all | solution.py:837
  125.9 6.9 %copy-start.4 = (bf16[16,64,512]{2,1,0:T(8,128)(2,1)}, bf16[16,64,512]{2,1,0:T(8,128)(2,1)S(1)}, u32[]{:S(2)}) copy-start(bf16[16,64,512]{2,1,0:T(8,128)(2,1)S(1)} %all-to-all-done) | copy-start | bytes 3145732
  125.9 30.0 %all-to-all-start.4 = ((bf16[16,64,512]{2,1,0:T(8,128)(2,1)}), bf16[16,64,512]{2,1,0:T(8,128)(2,1)}, u32[]{:S(2)}, u32[]{:S(2)}) async-start(bf16[16,64,512]{2,1,0:T(8,128)(2,1)} %bitcast.55), calls=%async_computation.4 | async-start | bytes 2097152 | tf_op jit(solution)/shard_map/all_to_all | solution.py:837
  155.9 29.7 %all-to-all-start.3 = ((bf16[16,64,512]{2,1,0:T(8,128)(2,1)}), bf16[16,64,512]{2,1,0:T(8,128)(2,1)S(1)}, u32[]{:S(2)}, u32[]{:S(2)}) async-start(bf16[16,64,512]{2,1,0:T(8,128)(2,1)} %bitcast.54), calls=%async_computation.3 | async-start | bytes 2097152 | tf_op jit(solution)/shard_map/all_to_all | solution.py:837
  162.7 29.9 %collective-permute-start.9 = (bf16[512,1024]{1,0:T(8,128)(2,1)}, bf16[512,1024]{1,0:T(8,128)(2,1)S(1)}, u32[]{:S(2)}, u32[]{:S(2)}) collective-permute-start(bf16[512,1024]{1,0:T(8,128)(2,1)} %get-tuple-element.114), channel_id=1, source_target_pairs={{0,1},{1,0},{2,3},{3,2},{4,5},{5,4},{6,7},{7,6},{8,9},{9,8},{10,11... | collective-permute-start | bytes 3145736 | tf_op jit(solution)/shard_map/ppermute | solution.py:829
  165.2 27.4 %collective-permute-start.10 = (bf16[192,512]{1,0:T(8,128)(2,1)S(1)}, bf16[192,512]{1,0:T(8,128)(2,1)S(1)}, u32[]{:S(2)}, u32[]{:S(2)}) collective-permute-start(bf16[192,512]{1,0:T(8,128)(2,1)S(1)} %slice.59), channel_id=1, source_target_pairs={{0,1},{1,0},{2,3},{3,2},{4,5},{5,4},{6,7},{7,6},{8,9},{9,8},{10,11... | collective-permute-start | bytes 589832 | tf_op jit(solution)/shard_map/ppermute | solution.py:829
  185.7 1.0 copy-start.1
  192.6 49.9 %all-to-all-start.5 = ((bf16[16,2,64,512]{3,2,1,0:T(8,128)(2,1)}), bf16[16,2,64,512]{3,2,1,0:T(8,128)(2,1)S(1)}, u32[]{:S(2)}, u32[]{:S(2)}) async-start(bf16[16,2,64,512]{3,2,1,0:T(8,128)(2,1)} %get-tuple-element.128), calls=%async_computation.5 | async-start | bytes 4194304 | tf_op jit(solution)/shard_map/all_to_all | solution.py:837
  199.4 2.8 copy-start.17
  199.4 22.3 %collective-permute-start.7 = (bf16[4,200,512]{2,1,0:T(8,128)(2,1)}, bf16[4,200,512]{2,1,0:T(8,128)(2,1)S(1)}, u32[]{:S(2)}, u32[]{:S(2)}) collective-permute-start(bf16[4,200,512]{2,1,0:T(8,128)(2,1)} %get-tuple-element.111), channel_id=1, source_target_pairs={{0,1},{1,0},{2,3},{3,2},{4,5},{5,4},{6,7},{7,6},{8,9},{9,8},{10,11... | collective-permute-start | bytes 2457608 | tf_op jit(solution)/shard_map/ppermute | solution.py:829
  202.2 19.5 %collective-permute-start.8 = (f32[4,16,208]{2,1,0:T(8,128)S(1)}, f32[4,16,208]{2,1,0:T(8,128)S(1)}, u32[]{:S(2)}, u32[]{:S(2)}) collective-permute-start(f32[4,16,208]{2,1,0:T(8,128)S(1)} %copy-done.17), channel_id=1, source_target_pairs={{0,1},{1,0},{2,3},{3,2},{4,5},{5,4},{6,7},{7,6},{8,9},{9,8},{10,11... | collective-permute-start | bytes 159752 | tf_op jit(solution)/shard_map/ppermute | solution.py:829
  221.7 1.6 copy-start.16
  221.7 1.6 copy-start.10
  221.7 20.8 %collective-permute-start.11 = (bf16[832,512]{1,0:T(8,128)(2,1)S(1)}, bf16[832,512]{1,0:T(8,128)(2,1)}, u32[]{:S(2)}, u32[]{:S(2)}) collective-permute-start(bf16[832,512]{1,0:T(8,128)(2,1)S(1)} %slice.60), channel_id=1, source_target_pairs={{0,1},{1,0},{2,3},{3,2},{4,5},{5,4},{6,7},{7,6},{8,9},{9,8},{10,11... | collective-permute-start | bytes 2555912 | tf_op jit(solution)/shard_map/ppermute | solution.py:829
  242.5 3.2 collective-permute-start.12
  242.6 22.2 %collective-permute-start.14 = (bf16[4,200,512]{2,1,0:T(8,128)(2,1)}, bf16[4,200,512]{2,1,0:T(8,128)(2,1)}, u32[]{:S(2)}, u32[]{:S(2)}) collective-permute-start(bf16[4,200,512]{2,1,0:T(8,128)(2,1)} %get-tuple-element.133.refs_0_), channel_id=1, source_target_pairs={{0,1},{1,0},{2,3},{3,2},{4,5},{5,4},{6,7},{7,6},{8,9},{9,8},{10,11... | collective-permute-start | bytes 2457608 | tf_op jit(solution)/shard_map/ppermute | solution.py:829
  248.4 15.2 %collective-permute-start.13 = (bf16[2,544,256]{2,1,0:T(8,128)(2,1)}, bf16[2,544,256]{2,1,0:T(8,128)(2,1)}, u32[]{:S(2)}, u32[]{:S(2)}) collective-permute-start(bf16[2,544,256]{2,1,0:T(8,128)(2,1)} %constant_dynamic-slice_fusion.4), channel_id=1, source_target_pairs={{0,4},{2,6},{4,0},{6,2},{8,12},{10,14},{12,8},{14,10},{16,20},{18,... | collective-permute-start | bytes 1671176 | tf_op jit(solution)/shard_map/ppermute | solution.py:937
  264.8 12.4 %collective-permute-start.15 = (bf16[2,272,256]{2,1,0:T(8,128)(2,1)S(1)}, bf16[2,272,256]{2,1,0:T(8,128)(2,1)S(1)}, u32[]{:S(2)}, u32[]{:S(2)}) collective-permute-start(bf16[2,272,256]{2,1,0:T(8,128)(2,1)S(1)} %constant_dynamic-slice_fusion.2), channel_id=1, source_target_pairs={{0,8},{2,10},{4,12},{6,14},{8,0},{10,2},{12,4},{14,6},{16,24},{18,... | collective-permute-start | bytes 835592 | tf_op jit(solution)/shard_map/ppermute | solution.py:937
  270.6 19.9 %collective-permute-start.17 = (bf16[4,200,512]{2,1,0:T(8,128)(2,1)}, bf16[4,200,512]{2,1,0:T(8,128)(2,1)S(1)}, u32[]{:S(2)}, u32[]{:S(2)}) collective-permute-start(bf16[4,200,512]{2,1,0:T(8,128)(2,1)} %get-tuple-element.159), channel_id=1, source_target_pairs={{0,1},{1,0},{2,3},{3,2},{4,5},{5,4},{6,7},{7,6},{8,9},{9,8},{10,11... | collective-permute-start | bytes 2457608 | tf_op jit(solution)/shard_map/ppermute | solution.py:829
  277.3 9.9 %collective-permute-start.16 = (bf16[2,136,256]{2,1,0:T(8,128)(2,1)S(1)}, bf16[2,136,256]{2,1,0:T(8,128)(2,1)S(1)}, u32[]{:S(2)}, u32[]{:S(2)}) collective-permute-start(bf16[2,136,256]{2,1,0:T(8,128)(2,1)S(1)} %constant_dynamic-slice_fusion.1), channel_id=1, source_target_pairs={{0,16},{2,18},{4,20},{6,22},{8,24},{10,26},{12,28},{14,30},{16,0},... | collective-permute-start | bytes 417800 | tf_op jit(solution)/shard_map/ppermute | solution.py:937
  283.5 8.5 %copy-start.3 = (f32[4,208,512]{2,1,0:T(8,128)S(1)}, f32[4,208,512]{2,1,0:T(8,128)}, u32[]{:S(2)}) copy-start(f32[4,208,512]{2,1,0:T(8,128)} %get-tuple-element.117.rest_4_) | copy-start | bytes 5111812
  290.5 4.3 %collective-permute-start.18 = (bf16[136,256]{1,0:T(8,128)(2,1)S(1)}, bf16[136,256]{1,0:T(8,128)(2,1)S(1)}, u32[]{:S(2)}, u32[]{:S(2)}) collective-permute-start(bf16[136,256]{1,0:T(8,128)(2,1)S(1)} %slice_bitcast_fusion.5), channel_id=1, source_target_pairs={{0,1},{1,0},{2,3},{3,2},{4,5},{5,4},{6,7},{7,6},{8,9},{9,8},{10,11... | collective-permute-start | bytes 208904 | tf_op jit(solution)/shard_map/ppermute | solution.py:829
  292.3 21.2 %copy-start.5 = (bf16[4,200,512]{2,1,0:T(8,128)(2,1)}, bf16[4,200,512]{2,1,0:T(8,128)(2,1)S(1)}, u32[]{:S(2)}) copy-start(bf16[4,200,512]{2,1,0:T(8,128)(2,1)S(1)} %add_convert_fusion.1.refs_0_) | copy-start | bytes 2457604
  294.8 6.0 %collective-permute-start.19 = (bf16[136,256]{1,0:T(8,128)(2,1)S(1)}, bf16[136,256]{1,0:T(8,128)(2,1)S(1)}, u32[]{:S(2)}, u32[]{:S(2)}) collective-permute-start(bf16[136,256]{1,0:T(8,128)(2,1)S(1)} %fusion.1), channel_id=1, source_target_pairs={{0,16},{2,18},{4,20},{6,22},{8,24},{10,26},{12,28},{14,30},{16,0},... | collective-permute-start | bytes 208904 | tf_op jit(solution)/shard_map/ppermute | solution.py:937
  296.3 17.2 %collective-permute-start.22 = (bf16[4,200,512]{2,1,0:T(8,128)(2,1)S(1)}, bf16[4,200,512]{2,1,0:T(8,128)(2,1)S(1)}, u32[]{:S(2)}, u32[]{:S(2)}) collective-permute-start(bf16[4,200,512]{2,1,0:T(8,128)(2,1)S(1)} %add_convert_fusion.1.refs_0_), channel_id=1, source_target_pairs={{0,1},{1,0},{2,3},{3,2},{4,5},{5,4},{6,7},{7,6},{8,9},{9,8},{10,11... | collective-permute-start | bytes 2457608 | tf_op jit(solution)/shard_map/ppermute | solution.py:829
  300.8 5.1 %collective-permute-start.20 = (bf16[272,256]{1,0:T(8,128)(2,1)S(1)}, bf16[272,256]{1,0:T(8,128)(2,1)S(1)}, u32[]{:S(2)}, u32[]{:S(2)}) collective-permute-start(bf16[272,256]{1,0:T(8,128)(2,1)S(1)} %maximum_select_fusion.3), channel_id=1, source_target_pairs={{0,8},{2,10},{4,12},{6,14},{8,0},{10,2},{12,4},{14,6},{16,24},{18,... | collective-permute-start | bytes 417800 | tf_op jit(solution)/shard_map/ppermute | solution.py:937
  306.1 6.6 %collective-permute-start.21 = (bf16[544,256]{1,0:T(8,128)(2,1)S(1)}, bf16[544,256]{1,0:T(8,128)(2,1)S(1)}, u32[]{:S(2)}, u32[]{:S(2)}) collective-permute-start(bf16[544,256]{1,0:T(8,128)(2,1)S(1)} %maximum_select_fusion.2), channel_id=1, source_target_pairs={{0,4},{2,6},{4,0},{6,2},{8,12},{10,14},{12,8},{14,10},{16,20},{18,... | collective-permute-start | bytes 835592 | tf_op jit(solution)/shard_map/ppermute | solution.py:937
  313.5 0.9 copy-start.9
  313.5 4.0 %collective-permute-start.23 = (bf16[1088,256]{1,0:T(8,128)(2,1)S(1)}, bf16[1088,256]{1,0:T(8,128)(2,1)S(1)}, u32[]{:S(2)}, u32[]{:S(2)}) collective-permute-start(bf16[1088,256]{1,0:T(8,128)(2,1)S(1)} %maximum_select_fusion.1), channel_id=1, source_target_pairs={{0,2},{2,0},{4,6},{6,4},{8,10},{10,8},{12,14},{14,12},{16,18},{18,... | collective-permute-start | bytes 1671176 | tf_op jit(solution)/shard_map/ppermute | solution.py:937

commit v4 on v3

--- a/solution.py
+++ b/solution.py
@@ -548,7 +548,8 @@
     if probs:
         turned = grads.T
         value = turned[:experts] + turned[experts:]
-        rest[0][0] = value + old[1][0] if old else value
+        value = value + old[1][0] if old else value
+        rest[0][0] = value.astype(rest[0].dtype)
 
 
 def collect(first, code_col, parts, own, dtype, half, block, probs=False, numbers=None, before=(), rows=PAD):
@@ -556,7 +557,7 @@
     count, width = parts[0].shape
     outs = [jax.ShapeDtypeStruct((own, rows, width), dtype)]
     if probs:
-        outs.append(jax.ShapeDtypeStruct((own, count // block, PAD), F32))
+        outs.append(jax.ShapeDtypeStruct((own, count // block, PAD), dtype))
     return pl.pallas_call(
         functools.partial(
             collect_kernel, numbers=numbers, half=half, block=block, probs=probs, before=len(before)
@@ -623,7 +624,7 @@
         tail = jnp.zeros((PAD - more[0].shape[1], model), F32)
         both = [v for b in range(batch) for v in (more[0][b].astype(F32), tail)]
         grad_routed = grad_routed + jnp.concatenate(both, axis=0)
-        grad_probs = grad_probs + more[1][...]
+        grad_probs = grad_probs + more[1][...].astype(F32)
     grad_probs = jnp.concatenate([grad_probs[g] for g in range(batch)], axis=1)
     grad_logits = probs * (grad_probs - jnp.sum(probs * grad_probs, axis=0, keepdims=True))
     high = grad_logits.astype(BF16)
@@ -868,7 +869,7 @@
     cot_slots = exchange(cot_slots)
     w1 = shards_of(after(w_expert_in[0], wq[-1], wo[-1]), 1)
     if ways == 2:
-        cut = w_expert_out.shape[1] // 4
+        cut = 3 * w_expert_out.shape[1] // 16
         w2_first = other(after(w_expert_out[0, :cut], wq[-1], wo[-1]))
         w2_rest = other(after(w_expert_out[0, cut:], wq[-1], wo[-1]))
     place = jnp.stack([rank * own, core]).astype(jnp.int32)

time: 323 us -> 322 us (level)
  transfers between devices with their start and end apart: 30 -> 30, of which waited for: 18 -> 17; matrix products, arithmetic and copies ran while one was open for 6% -> 6% of each run, Pallas kernels for 42% -> 42%
where the time goes in v4:
time: 322 us; the launch traced here: 320 us
  Pallas kernels  146 us (45%)
  waiting for transfers between devices  74.4 us (23%)
  starting transfers between devices  73 us (23%)
  other arithmetic  14.8 us (5%)
  local copies, waits for them, and re-layouts  11.3 us (4%)
    pallas_call x2, Pallas kernels, experts_step(): pl.pallas_call(functools.partial(expert_kernel, parts=parts, half=half, b...  45 us
    all_to_all x6, starting transfers between devices, exchange(): lax.all_to_all(rows, 'expert', split_axis=0, concat_axis=0, tiled=True)  40.9 us
    ppermute x14, waiting for transfers between devices, other(): return lax.ppermute(v, 'tensor', swap)  38.1 us
    pallas_call x4, Pallas kernels, collect(): pl.pallas_call(functools.partial(collect_kernel, numbers=numbers, half=ha...  28.9 us
    pallas_call x1, Pallas kernels, attend(): pl.pallas_call(functools.partial(attend_kernel, pieces=pieces, own=own),...  22.2 us
    ppermute x8, waiting for transfers between devices, swap_bit(): return lax.ppermute(v, 'expert', [(i, i ^ bit) for i in range(groups)])  21.5 us
    pallas_call x1, Pallas kernels, back(): pl.pallas_call(functools.partial(back_kernel, steps=own // batch, receive...  19.2 us
    ppermute x14, starting transfers between devices, other(): return lax.ppermute(v, 'tensor', swap)  17.6 us
  transfers between devices with their start and end apart: 30, of which 17 were waited for; matrix products, arithmetic and copies ran while one was open for 6% of the time, Pallas kernels for 42%

profile of v4, /device:TPU:0, one launch (start us, length us, event | category | flops | bytes accessed | tf_op | source)
XLA Modules:
  0.0 320.4 jit_solution(2631953506426649834)
XLA Ops:
  2.8 9.6 %front.1 = (bf16[8,208,512]{2,1,0:T(8,128)(2,1)}, bf16[16,2,64,512]{3,2,1,0:T(8,128)(2,1)}, s32[208,16]{1,0:T(8,128)}, s32[2,1664]{1,0:T(2,128)}) custom-call(s32[1]{0:T(128)} %bitcast.2.rank_ref, bf16[1576,512]{1,0:T(8,128)(2,1)} %cot_ref.1, s32[16,208]{1,0:T(8,128)} %get-tuple-element.163.col_ref, s32[2,1664]{1,0:T(2,128)} %reshape.75.row_ref), custom_call_target="tpu_custom_call" | custom-call | bytes 36900000 | tf_op jit(solution)/shard_map/front/pallas_call | solution.py:151
  12.4 7.5 %all-to-all-start.1 = ((bf16[16,2,64,512]{3,2,1,0:T(8,128)(2,1)}), bf16[16,2,64,512]{3,2,1,0:T(8,128)(2,1)S(1)}, u32[]{:S(2)}, u32[]{:S(2)}) async-start(bf16[16,2,64,512]{3,2,1,0:T(8,128)(2,1)} %get-tuple-element.81), calls=%async_computation.1 | async-start | bytes 4194304 | tf_op jit(solution)/shard_map/all_to_all | solution.py:838
  20.0 1.6 collective-permute-start
  22.2 4.1 %pad.74.tok_ref.rest_6_ = bf16[8,208,512]{2,1,0:T(8,128)(2,1)} custom-call(bf16[1576,512]{1,0:T(8,128)(2,1)} %source), custom_call_target="tpu_custom_call" | custom-call | bytes 7380000 | tf_op jit(solution)/shard_map/pad/pallas_call | solution.py:67
  26.3 7.9 %collective-permute-done.1.rest_4_ = bf16[128,512]{1,0:T(8,128)(2,1)S(1)} collective-permute-done((bf16[128,512]{1,0:T(8,128)(2,1)S(1)}, bf16[128,512]{1,0:T(8,128)(2,1)S(1)}, u32[]{:S(2)}, u32[]{:S(2)}) %collective-permute-start.1) | collective-permute-done | bytes 131104 | tf_op jit(solution)/shard_map/ppermute | solution.py:830
  36.3 1.6 collective-permute-start.5
  39.1 22.2 %attend.1 = (bf16[8,208,512]{2,1,0:T(8,128)(2,1)}, f32[4,208,512]{2,1,0:T(8,128)}, bf16[4,208,1536]{2,1,0:T(8,128)(2,1)}, bf16[4,2,832,208]{3,2,1,0:T(8,128)(2,1...) custom-call(s32[2]{0:T(128)} %pad_add_fusion.place_ref, ...), custom_call_target="tpu_custom_call" | custom-call | bytes 92250000 | tf_op jit(solution)/shard_map/attend/pallas_call | solution.py:300
  61.3 4.9 %spread.3 = bf16[16,64,512]{2,1,0:T(8,128)(2,1)} custom-call(s32[2,1664]{1,0:T(2,128)} %get-tuple-element.80.code_ref, bf16[1664,512]{1,0:T(8,128)(2,1)} %bitcast.47), custom_call_target="tpu_custom_call" | custom-call | bytes 18450000 | tf_op jit(solution)/shard_map/spread/pallas_call | solution.py:178
  66.3 6.0 %all-to-all-start.2 = ((bf16[16,64,512]{2,1,0:T(8,128)(2,1)}), bf16[16,64,512]{2,1,0:T(8,128)(2,1)}, u32[]{:S(2)}, u32[]{:S(2)}) async-start(bf16[16,64,512]{2,1,0:T(8,128)(2,1)} %spread.3), calls=%async_computation.2 | async-start | bytes 2097152 | tf_op jit(solution)/shard_map/all_to_all | solution.py:838
  72.4 1.6 collective-permute-start.4
  73.9 4.8 %spread.2 = bf16[16,64,512]{2,1,0:T(8,128)(2,1)} custom-call(s32[2,1664]{1,0:T(2,128)} %get-tuple-element.80.code_ref, bf16[1664,512]{1,0:T(8,128)(2,1)} %bitcast.48), custom_call_target="tpu_custom_call" | custom-call | bytes 18450000 | tf_op jit(solution)/shard_map/spread/pallas_call | solution.py:178
  78.8 14.9 %collective-permute-done.4.rest_4_ = bf16[832,512]{1,0:T(8,128)(2,1)S(1)} collective-permute-done((bf16[832,512]{1,0:T(8,128)(2,1)S(1)}, bf16[832,512]{1,0:T(8,128)(2,1)S(1)}, u32[]{:S(2)}, u32[]{:S(2)}) %collective-permute-start.4) | collective-permute-done | bytes 852000 | tf_op jit(solution)/shard_map/ppermute | solution.py:830
  93.6 1.6 all-to-all-done.2
  95.3 6.9 %all-to-all-start = ((bf16[16,64,512]{2,1,0:T(8,128)(2,1)}), bf16[16,64,512]{2,1,0:T(8,128)(2,1)S(1)}, u32[]{:S(2)}, u32[]{:S(2)}) async-start(bf16[16,64,512]{2,1,0:T(8,128)(2,1)} %spread.2), calls=%async_computation | async-start | bytes 2097152 | tf_op jit(solution)/shard_map/all_to_all | solution.py:838
  102.2 22.0 %experts.2 = (bf16[1024,512]{1,0:T(8,128)(2,1)}, bf16[16,2,64,512]{3,2,1,0:T(8,128)(2,1)}, f32[512,1024]{1,0:T(8,128)}, f32[512,1024]{1,0:T(8,128)}, f32[1024,512]{1,0:T(8,128)}, /*index=5*/f32[1024,512]{1,0:T(8,128)}) custom-call(s32[1]{0:T(128)} %bitcast.5.expert_ref, bf16[1024,512]{1,0:T(8,128)(2,1)} %bitcast.15.x_ref, bf16[16,2,64,512]{3,2,1,0:T(8,128)(2,1)} %copy-done, ...), custom_call_target="tpu_custom_call" | custom-call | bytes 73800000 | tf_op jit(solution)/shard_map/experts/pallas_call | solution.py:464
  125.1 6.9 %all-to-all-start.4 = ((bf16[16,64,512]{2,1,0:T(8,128)(2,1)}), bf16[16,64,512]{2,1,0:T(8,128)(2,1)}, u32[]{:S(2)}, u32[]{:S(2)}) async-start(bf16[16,64,512]{2,1,0:T(8,128)(2,1)} %bitcast.55), calls=%async_computation.4 | async-start | bytes 2097152 | tf_op jit(solution)/shard_map/all_to_all | solution.py:838
  132.0 23.0 %experts.3 = (bf16[1024,512]{1,0:T(8,128)(2,1)}, bf16[16,2,64,512]{3,2,1,0:T(8,128)(2,1)}, f32[512,1024]{1,0:T(8,128)}, bf16[512,1024]{1,0:T(8,128)(2,1)}, f32[1...) custom-call(s32[1]{0:T(128)} %bitcast.5.expert_ref, bf16[1024,512]{1,0:T(8,128)(2,1)} %bitcast.49, ...), custom_call_target="tpu_custom_call", output_to_operand_aliasing={{1}: (13, {})} | custom-call | bytes 73800000 | tf_op jit(solution)/shard_map/experts/pallas_call | solution.py:464
  155.0 6.8 %all-to-all-start.3 = ((bf16[16,64,512]{2,1,0:T(8,128)(2,1)}), bf16[16,64,512]{2,1,0:T(8,128)(2,1)S(1)}, u32[]{:S(2)}, u32[]{:S(2)}) async-start(bf16[16,64,512]{2,1,0:T(8,128)(2,1)} %bitcast.54), calls=%async_computation.3 | async-start | bytes 2097152 | tf_op jit(solution)/shard_map/all_to_all | solution.py:838
  161.9 1.6 collective-permute-start.9
  165.0 8.9 %collect.4 = (f32[8,208,512]{2,1,0:T(8,128)}, f32[8,16,208]{2,1,0:T(8,128)}) custom-call(s32[1]{0:T(128)} %constant.99.clone.1.first_ref, s32[208,16]{1,0:T(8,128)} %get-tuple-element.79.code_ref, bf16[1024,512]{1,0:T(8,128)(2,1)} %bitcast.19.rest_0_), custom_call_target="tpu_custom_call" | custom-call | bytes 25830000 | tf_op jit(solution)/shard_map/collect/pallas_call | solution.py:561
  173.9 10.9 %all-to-all-done.3 = bf16[16,64,512]{2,1,0:T(8,128)(2,1)S(1)} async-done(((bf16[16,64,512]{2,1,0:T(8,128)(2,1)}), bf16[16,64,512]{2,1,0:T(8,128)(2,1)S(1)}, u32[]{:S(2)}, u32[]{:S(2)}) %all-to-all-start.3) | async-done | bytes 1048608 | tf_op jit(solution)/shard_map/all_to_all | solution.py:838
  185.8 5.9 %collect.6 = (bf16[4,200,512]{2,1,0:T(8,128)(2,1)}, bf16[4,16,208]{2,1,0:T(8,128)(2,1)}) custom-call(s32[1]{0:T(128)} %bitcast.20.first_ref, s32[208,16]{1,0:T(8,128)} %get-tuple-element.79.code_ref, bf16[1024,512]{1,0:T(8,128)(2,1)} %bitcast.43, f32[8,208,512]{2,1,0:T(8,128)} %get-tuple-element.107.rest_1_, f32[8,16,208]{2,1,0:T(8,128)} %get-tuple-element.108.rest_2_), custom_call_target="tpu_custom_call" | custom-call | bytes 25830000 | tf_op jit(solution)/shard_map/collect/pallas_call | solution.py:561
  191.8 6.8 %all-to-all-start.5 = ((bf16[16,2,64,512]{3,2,1,0:T(8,128)(2,1)}), bf16[16,2,64,512]{3,2,1,0:T(8,128)(2,1)S(1)}, u32[]{:S(2)}, u32[]{:S(2)}) async-start(bf16[16,2,64,512]{3,2,1,0:T(8,128)(2,1)} %get-tuple-element.128), calls=%async_computation.5 | async-start | bytes 4194304 | tf_op jit(solution)/shard_map/all_to_all | solution.py:838
  198.6 1.6 collective-permute-start.7
  202.0 3.4 %convert_add_fusion.1 = f32[512,1024]{1,0:T(8,128)} fusion(f32[512,1024]{1,0:T(8,128)} %get-tuple-element.113, bf16[512,1024]{1,0:T(8,128)(2,1)S(1)} %collective-permute-done.9), kind=kLoop, calls=%fused_computation.2 | loop fusion | flops 1048576 | bytes 5242880 | tf_op jit(solution)/shard_map/add | solution.py:914
  205.3 5.9 %collect.5 = (f32[4,208,512]{2,1,0:T(8,128)}, f32[4,16,208]{2,1,0:T(8,128)}) custom-call(s32[1]{0:T(128)} %bitcast.first_ref, s32[208,16]{1,0:T(8,128)} %get-tuple-element.79.code_ref, bf16[1024,512]{1,0:T(8,128)(2,1)} %bitcast.44, f32[8,208,512]{2,1,0:T(8,128)} %get-tuple-element.107.rest_1_, f32[8,16,208]{2,1,0:T(8,128)} %get-tuple-element.108.rest_2_), custom_call_target="tpu_custom_call" | custom-call | bytes 25830000 | tf_op jit(solution)/shard_map/collect/pallas_call | solution.py:561
  211.2 9.0 %collective-permute-done.8.rest_3_ = bf16[4,16,208]{2,1,0:T(8,128)(2,1)S(1)} collective-permute-done((bf16[4,16,208]{2,1,0:T(8,128)(2,1)S(1)}, bf16[4,16,208]{2,1,0:T(8,128)(2,1)S(1)}, u32[]{:S(2)}, u32[]{:S(2)}) %collective-permute-start.8) | collective-permute-done | bytes 26656 | tf_op jit(solution)/shard_map/ppermute | solution.py:830
  220.2 1.6 collective-permute-start.11
  221.7 19.2 %back.1 = (bf16[4,200,512]{2,1,0:T(8,128)(2,1)}, bf16[2,1088,256]{2,1,0:T(8,128)(2,1)}, bf16[2,1088,256]{2,1,0:T(8,128)(2,1)}) custom-call(s32[2]{0:T(128)} %pad_add_fusion.place_ref, f32[4,208,512]{2,1,0:T(8,128)} %get-tuple-element.109.rest_0_, f32[4,16,208]{2,1,0:T(8,128)} %get-tuple-element.110.rest_1_, bf16[4,200,512]{2,1,0:T(8,128)(2,1)} %copy-done.9, ...), custom_call_target="tpu_custom_call" | custom-call | bytes 59040000 | tf_op jit(solution)/shard_map/back/pallas_call | solution.py:731
  242.3 1.8 collective-permute-done.12
  244.1 1.9 add_convert_fusion
  246.9 2.4 collective-permute-start.13
  250.8 8.2 %collect.7 = bf16[8,200,512]{2,1,0:T(8,128)(2,1)} custom-call(s32[1]{0:T(128)} %constant.99.clone.1.first_ref, s32[208,16]{1,0:T(8,128)} %get-tuple-element.79.code_ref, bf16[1024,512]{1,0:T(8,128)(2,1)} %bitcast.51, bf16[1024,512]{1,0:T(8,128)(2,1)} %bitcast.50), custom_call_target="tpu_custom_call" | custom-call | bytes 25830000 | tf_op jit(solution)/shard_map/collect/pallas_call | solution.py:561
  259.0 2.4 constant_dynamic-slice_fusion
  264.0 5.8 %collective-permute-start.15 = (bf16[2,272,256]{2,1,0:T(8,128)(2,1)S(1)}, bf16[2,272,256]{2,1,0:T(8,128)(2,1)S(1)}, u32[]{:S(2)}, u32[]{:S(2)}) collective-permute-start(bf16[2,272,256]{2,1,0:T(8,128)(2,1)S(1)} %constant_dynamic-slice_fusion.2), channel_id=1, source_target_pairs={{0,8},{2,10},{4,12},{6,14},{8,0},{10,2},{12,4},{14,6},{16,24},{18,... | collective-permute-start | bytes 835592 | tf_op jit(solution)/shard_map/ppermute | solution.py:938
  269.8 1.5 collective-permute-start.17
  271.3 5.1 %collective-permute-done.15 = bf16[2,272,256]{2,1,0:T(8,128)(2,1)S(1)} collective-permute-done((bf16[2,272,256]{2,1,0:T(8,128)(2,1)S(1)}, bf16[2,272,256]{2,1,0:T(8,128)(2,1)S(1)}, u32[]{:S(2)}, u32[]{:S(2)}) %collective-permute-start.15) | collective-permute-done | bytes 278560 | tf_op jit(solution)/shard_map/ppermute | solution.py:938
  276.5 2.7 collective-permute-start.16
  279.2 3.4 %convert_add_fusion = f32[1024,512]{1,0:T(8,128)} fusion(f32[1024,512]{1,0:T(8,128)} %get-tuple-element.135, bf16[832,512]{1,0:T(8,128)(2,1)} %collective-permute-done.11, bf16[192,512]{1,0:T(8,128)(2,1)S(1)} %collective-permute-done.10), kind=kLoop, calls=%fused_computation.1 | loop fusion | flops 2621440 | bytes 5242880 | tf_op jit(solution)/shard_map/add | solution.py:966
  282.6 3.8 %unpad.2 = f32[1576,512]{1,0:T(8,128)} custom-call(s32[1]{0:T(128)} %bitcast.first_ref, bf16[4,200,512]{2,1,0:T(8,128)(2,1)} %get-tuple-element.133.refs_0_, bf16[4,200,512]{2,1,0:T(8,128)(2,1)} %collective-permute-done.14.refs_1_), custom_call_target="tpu_custom_call" | custom-call | bytes 7380000 | tf_op jit(solution)/shard_map/unpad/pallas_call | solution.py:802
  286.5 3.2 collective-permute-done.17
  289.7 1.5 collective-permute-start.18
  291.5 2.4 collective-permute-done.18
  295.5 1.5 collective-permute-start.22
  297.0 3.0 collective-permute-done.19
  300.1 5.0 %collective-permute-done.20 = bf16[272,256]{1,0:T(8,128)(2,1)S(1)} collective-permute-done((bf16[272,256]{1,0:T(8,128)(2,1)S(1)}, bf16[272,256]{1,0:T(8,128)(2,1)S(1)}, u32[]{:S(2)}, u32[]{:S(2)}) %collective-permute-start.20) | collective-permute-done | bytes 139296 | tf_op jit(solution)/shard_map/ppermute | solution.py:938
  306.7 5.2 %collective-permute-done.21 = bf16[544,256]{1,0:T(8,128)(2,1)S(1)} collective-permute-done((bf16[544,256]{1,0:T(8,128)(2,1)S(1)}, bf16[544,256]{1,0:T(8,128)(2,1)S(1)}, u32[]{:S(2)}, u32[]{:S(2)}) %collective-permute-start.21) | collective-permute-done | bytes 278560 | tf_op jit(solution)/shard_map/ppermute | solution.py:938
  313.6 3.1 unpad.3
  (97 shorter events, 26.7 us)
Async XLA Ops:
  12.4 7.5 %copy-start.7 = (bf16[3,512,256]{2,1,0:T(8,128)(2,1)S(1)}, bf16[3,512,256]{2,1,0:T(8,128)(2,1)}, u32[]{:S(2)}) copy-start(bf16[3,512,256]{2,1,0:T(8,128)(2,1)} %rest_0_.1) | copy-start | bytes 2359300
  12.4 9.2 %copy-start.11 = (bf16[256,512]{1,0:T(8,128)(2,1)S(1)}, bf16[256,512]{1,0:T(8,128)(2,1)}, u32[]{:S(2)}) copy-start(bf16[256,512]{1,0:T(8,128)(2,1)} %rest_3_.1) | copy-start | bytes 786436
  12.4 53.9 %all-to-all-start.1 = ((bf16[16,2,64,512]{3,2,1,0:T(8,128)(2,1)}), bf16[16,2,64,512]{3,2,1,0:T(8,128)(2,1)S(1)}, u32[]{:S(2)}, u32[]{:S(2)}) async-start(bf16[16,2,64,512]{3,2,1,0:T(8,128)(2,1)} %get-tuple-element.81), calls=%async_computation.1 | async-start | bytes 4194304 | tf_op jit(solution)/shard_map/all_to_all | solution.py:838
  20.0 14.3 %collective-permute-start = (bf16[3,512,128]{2,1,0:T(8,128)(2,1)S(1)}, bf16[3,512,128]{2,1,0:T(8,128)(2,1)S(1)}, u32[]{:S(2)}, u32[]{:S(2)}) collective-permute-start(bf16[3,512,128]{2,1,0:T(8,128)(2,1)S(1)} %constant_dynamic-slice_fusion.6), channel_id=1, source_target_pairs={{0,1},{1,0},{2,3},{3,2},{4,5},{5,4},{6,7},{7,6},{8,9},{9,8},{10,11... | collective-permute-start | bytes 1179656 | tf_op jit(solution)/shard_map/ppermute | solution.py:830
  21.6 16.2 %copy-start.2 = (bf16[1,1024,512]{2,1,0:T(8,128)(2,1)S(1)}, bf16[1,1024,512]{2,1,0:T(8,128)(2,1)}, u32[]{:S(2)}) copy-start(bf16[1,1024,512]{2,1,0:T(8,128)(2,1)} %param.18) | copy-start | bytes 3145732
  21.6 12.7 %collective-permute-start.1 = (bf16[128,512]{1,0:T(8,128)(2,1)S(1)}, bf16[128,512]{1,0:T(8,128)(2,1)S(1)}, u32[]{:S(2)}, u32[]{:S(2)}) collective-permute-start(bf16[128,512]{1,0:T(8,128)(2,1)S(1)} %constant_dynamic-slice_fusion.5), channel_id=1, source_target_pairs={{0,1},{1,0},{2,3},{3,2},{4,5},{5,4},{6,7},{7,6},{8,9},{9,8},{10,11... | collective-permute-start | bytes 393224 | tf_op jit(solution)/shard_map/ppermute | solution.py:830
  34.3 3.6 %copy-start.14 = (bf16[128,512]{1,0:T(8,128)(2,1)}, bf16[128,512]{1,0:T(8,128)(2,1)S(1)}, u32[]{:S(2)}) copy-start(bf16[128,512]{1,0:T(8,128)(2,1)S(1)} %collective-permute-done.1.rest_4_) | copy-start | bytes 393220
  34.3 3.5 %copy-start.12 = (bf16[3,512,128]{2,1,0:T(8,128)(2,1)}, bf16[3,512,128]{2,1,0:T(8,128)(2,1)S(1)}, u32[]{:S(2)}) copy-start(bf16[3,512,128]{2,1,0:T(8,128)(2,1)S(1)} %collective-permute-done.rest_1_) | copy-start | bytes 1179652
  34.3 2.0 collective-permute-start.2
  34.3 1.9 collective-permute-start.3
  36.2 1.6 copy-start.15
  36.2 1.6 copy-start.13
  36.3 30.0 %collective-permute-start.5 = (bf16[512,1024]{1,0:T(8,128)(2,1)}, bf16[512,1024]{1,0:T(8,128)(2,1)}, u32[]{:S(2)}, u32[]{:S(2)}) collective-permute-start(bf16[512,1024]{1,0:T(8,128)(2,1)} %bitcast.12.rest_0_), channel_id=1, source_target_pairs={{0,1},{1,0},{2,3},{3,2},{4,5},{5,4},{6,7},{7,6},{8,9},{9,8},{10,11... | collective-permute-start | bytes 3145736 | tf_op jit(solution)/shard_map/ppermute | solution.py:830
  37.9 28.4 %collective-permute-start.6 = (bf16[192,512]{1,0:T(8,128)(2,1)S(1)}, bf16[192,512]{1,0:T(8,128)(2,1)S(1)}, u32[]{:S(2)}, u32[]{:S(2)}) collective-permute-start(bf16[192,512]{1,0:T(8,128)(2,1)S(1)} %slice_bitcast_fusion.4), channel_id=1, source_target_pairs={{0,1},{1,0},{2,3},{3,2},{4,5},{5,4},{6,7},{7,6},{8,9},{9,8},{10,11... | collective-permute-start | bytes 589832 | tf_op jit(solution)/shard_map/ppermute | solution.py:830
  66.2 6.1 %copy-start = (bf16[16,2,64,512]{3,2,1,0:T(8,128)(2,1)}, bf16[16,2,64,512]{3,2,1,0:T(8,128)(2,1)S(1)}, u32[]{:S(2)}) copy-start(bf16[16,2,64,512]{3,2,1,0:T(8,128)(2,1)S(1)} %all-to-all-done.1.cot_ref) | copy-start | bytes 6291460
  66.2 6.0 %copy-start.10 = (bf16[192,512]{1,0:T(8,128)(2,1)}, bf16[192,512]{1,0:T(8,128)(2,1)S(1)}, u32[]{:S(2)}) copy-start(bf16[192,512]{1,0:T(8,128)(2,1)S(1)} %collective-permute-done.6.rest_3_) | copy-start | bytes 589828
  66.3 29.0 %all-to-all-start.2 = ((bf16[16,64,512]{2,1,0:T(8,128)(2,1)}), bf16[16,64,512]{2,1,0:T(8,128)(2,1)}, u32[]{:S(2)}, u32[]{:S(2)}) async-start(bf16[16,64,512]{2,1,0:T(8,128)(2,1)} %spread.3), calls=%async_computation.2 | async-start | bytes 2097152 | tf_op jit(solution)/shard_map/all_to_all | solution.py:838
  72.4 21.3 %collective-permute-start.4 = (bf16[832,512]{1,0:T(8,128)(2,1)S(1)}, bf16[832,512]{1,0:T(8,128)(2,1)S(1)}, u32[]{:S(2)}, u32[]{:S(2)}) collective-permute-start(bf16[832,512]{1,0:T(8,128)(2,1)S(1)} %slice_bitcast_fusion), channel_id=1, source_target_pairs={{0,1},{1,0},{2,3},{3,2},{4,5},{5,4},{6,7},{7,6},{8,9},{9,8},{10,11... | collective-permute-start | bytes 2555912 | tf_op jit(solution)/shard_map/ppermute | solution.py:830
  93.6 8.5 %copy-start.5 = (bf16[832,512]{1,0:T(8,128)(2,1)}, bf16[832,512]{1,0:T(8,128)(2,1)S(1)}, u32[]{:S(2)}) copy-start(bf16[832,512]{1,0:T(8,128)(2,1)S(1)} %collective-permute-done.4.rest_4_) | copy-start | bytes 2555908
  95.3 29.8 %all-to-all-start = ((bf16[16,64,512]{2,1,0:T(8,128)(2,1)}), bf16[16,64,512]{2,1,0:T(8,128)(2,1)S(1)}, u32[]{:S(2)}, u32[]{:S(2)}) async-start(bf16[16,64,512]{2,1,0:T(8,128)(2,1)} %spread.2), calls=%async_computation | async-start | bytes 2097152 | tf_op jit(solution)/shard_map/all_to_all | solution.py:838
  125.1 6.9 %copy-start.4 = (bf16[16,64,512]{2,1,0:T(8,128)(2,1)}, bf16[16,64,512]{2,1,0:T(8,128)(2,1)S(1)}, u32[]{:S(2)}) copy-start(bf16[16,64,512]{2,1,0:T(8,128)(2,1)S(1)} %all-to-all-done) | copy-start | bytes 3145732
  125.1 29.9 %all-to-all-start.4 = ((bf16[16,64,512]{2,1,0:T(8,128)(2,1)}), bf16[16,64,512]{2,1,0:T(8,128)(2,1)}, u32[]{:S(2)}, u32[]{:S(2)}) async-start(bf16[16,64,512]{2,1,0:T(8,128)(2,1)} %bitcast.55), calls=%async_computation.4 | async-start | bytes 2097152 | tf_op jit(solution)/shard_map/all_to_all | solution.py:838
  155.0 29.8 %all-to-all-start.3 = ((bf16[16,64,512]{2,1,0:T(8,128)(2,1)}), bf16[16,64,512]{2,1,0:T(8,128)(2,1)S(1)}, u32[]{:S(2)}, u32[]{:S(2)}) async-start(bf16[16,64,512]{2,1,0:T(8,128)(2,1)} %bitcast.54), calls=%async_computation.3 | async-start | bytes 2097152 | tf_op jit(solution)/shard_map/all_to_all | solution.py:838
  161.9 29.9 %collective-permute-start.9 = (bf16[512,1024]{1,0:T(8,128)(2,1)}, bf16[512,1024]{1,0:T(8,128)(2,1)S(1)}, u32[]{:S(2)}, u32[]{:S(2)}) collective-permute-start(bf16[512,1024]{1,0:T(8,128)(2,1)} %get-tuple-element.114), channel_id=1, source_target_pairs={{0,1},{1,0},{2,3},{3,2},{4,5},{5,4},{6,7},{7,6},{8,9},{9,8},{10,11... | collective-permute-start | bytes 3145736 | tf_op jit(solution)/shard_map/ppermute | solution.py:830
  164.4 27.4 %collective-permute-start.10 = (bf16[192,512]{1,0:T(8,128)(2,1)S(1)}, bf16[192,512]{1,0:T(8,128)(2,1)S(1)}, u32[]{:S(2)}, u32[]{:S(2)}) collective-permute-start(bf16[192,512]{1,0:T(8,128)(2,1)S(1)} %slice.59), channel_id=1, source_target_pairs={{0,1},{1,0},{2,3},{3,2},{4,5},{5,4},{6,7},{7,6},{8,9},{9,8},{10,11... | collective-permute-start | bytes 589832 | tf_op jit(solution)/shard_map/ppermute | solution.py:830
  184.8 1.0 copy-start.1
  191.8 49.2 %all-to-all-start.5 = ((bf16[16,2,64,512]{3,2,1,0:T(8,128)(2,1)}), bf16[16,2,64,512]{3,2,1,0:T(8,128)(2,1)S(1)}, u32[]{:S(2)}, u32[]{:S(2)}) async-start(bf16[16,2,64,512]{3,2,1,0:T(8,128)(2,1)} %get-tuple-element.128), calls=%async_computation.5 | async-start | bytes 4194304 | tf_op jit(solution)/shard_map/all_to_all | solution.py:838
  198.6 2.8 copy-start.17
  198.6 21.6 %collective-permute-start.7 = (bf16[4,200,512]{2,1,0:T(8,128)(2,1)}, bf16[4,200,512]{2,1,0:T(8,128)(2,1)S(1)}, u32[]{:S(2)}, u32[]{:S(2)}) collective-permute-start(bf16[4,200,512]{2,1,0:T(8,128)(2,1)} %get-tuple-element.111), channel_id=1, source_target_pairs={{0,1},{1,0},{2,3},{3,2},{4,5},{5,4},{6,7},{7,6},{8,9},{9,8},{10,11... | collective-permute-start | bytes 2457608 | tf_op jit(solution)/shard_map/ppermute | solution.py:830
  201.4 18.8 %collective-permute-start.8 = (bf16[4,16,208]{2,1,0:T(8,128)(2,1)S(1)}, bf16[4,16,208]{2,1,0:T(8,128)(2,1)S(1)}, u32[]{:S(2)}, u32[]{:S(2)}) collective-permute-start(bf16[4,16,208]{2,1,0:T(8,128)(2,1)S(1)} %copy-done.17), channel_id=1, source_target_pairs={{0,1},{1,0},{2,3},{3,2},{4,5},{5,4},{6,7},{7,6},{8,9},{9,8},{10,11... | collective-permute-start | bytes 79880 | tf_op jit(solution)/shard_map/ppermute | solution.py:830
  220.2 1.6 copy-start.16
  220.2 1.6 copy-start.9
  220.2 20.8 %collective-permute-start.11 = (bf16[832,512]{1,0:T(8,128)(2,1)S(1)}, bf16[832,512]{1,0:T(8,128)(2,1)}, u32[]{:S(2)}, u32[]{:S(2)}) collective-permute-start(bf16[832,512]{1,0:T(8,128)(2,1)S(1)} %slice.60), channel_id=1, source_target_pairs={{0,1},{1,0},{2,3},{3,2},{4,5},{5,4},{6,7},{7,6},{8,9},{9,8},{10,11... | collective-permute-start | bytes 2555912 | tf_op jit(solution)/shard_map/ppermute | solution.py:830
  241.0 3.2 collective-permute-start.12
  241.1 22.9 %collective-permute-start.14 = (bf16[4,200,512]{2,1,0:T(8,128)(2,1)}, bf16[4,200,512]{2,1,0:T(8,128)(2,1)}, u32[]{:S(2)}, u32[]{:S(2)}) collective-permute-start(bf16[4,200,512]{2,1,0:T(8,128)(2,1)} %get-tuple-element.133.refs_0_), channel_id=1, source_target_pairs={{0,1},{1,0},{2,3},{3,2},{4,5},{5,4},{6,7},{7,6},{8,9},{9,8},{10,11... | collective-permute-start | bytes 2457608 | tf_op jit(solution)/shard_map/ppermute | solution.py:830
  246.9 15.9 %collective-permute-start.13 = (bf16[2,544,256]{2,1,0:T(8,128)(2,1)}, bf16[2,544,256]{2,1,0:T(8,128)(2,1)}, u32[]{:S(2)}, u32[]{:S(2)}) collective-permute-start(bf16[2,544,256]{2,1,0:T(8,128)(2,1)} %constant_dynamic-slice_fusion.4), channel_id=1, source_target_pairs={{0,4},{2,6},{4,0},{6,2},{8,12},{10,14},{12,8},{14,10},{16,20},{18,... | collective-permute-start | bytes 1671176 | tf_op jit(solution)/shard_map/ppermute | solution.py:938
  264.0 12.4 %collective-permute-start.15 = (bf16[2,272,256]{2,1,0:T(8,128)(2,1)S(1)}, bf16[2,272,256]{2,1,0:T(8,128)(2,1)S(1)}, u32[]{:S(2)}, u32[]{:S(2)}) collective-permute-start(bf16[2,272,256]{2,1,0:T(8,128)(2,1)S(1)} %constant_dynamic-slice_fusion.2), channel_id=1, source_target_pairs={{0,8},{2,10},{4,12},{6,14},{8,0},{10,2},{12,4},{14,6},{16,24},{18,... | collective-permute-start | bytes 835592 | tf_op jit(solution)/shard_map/ppermute | solution.py:938
  269.8 19.9 %collective-permute-start.17 = (bf16[4,200,512]{2,1,0:T(8,128)(2,1)}, bf16[4,200,512]{2,1,0:T(8,128)(2,1)S(1)}, u32[]{:S(2)}, u32[]{:S(2)}) collective-permute-start(bf16[4,200,512]{2,1,0:T(8,128)(2,1)} %get-tuple-element.159), channel_id=1, source_target_pairs={{0,1},{1,0},{2,3},{3,2},{4,5},{5,4},{6,7},{7,6},{8,9},{9,8},{10,11... | collective-permute-start | bytes 2457608 | tf_op jit(solution)/shard_map/ppermute | solution.py:830
  276.5 9.9 %collective-permute-start.16 = (bf16[2,136,256]{2,1,0:T(8,128)(2,1)S(1)}, bf16[2,136,256]{2,1,0:T(8,128)(2,1)S(1)}, u32[]{:S(2)}, u32[]{:S(2)}) collective-permute-start(bf16[2,136,256]{2,1,0:T(8,128)(2,1)S(1)} %constant_dynamic-slice_fusion.1), channel_id=1, source_target_pairs={{0,16},{2,18},{4,20},{6,22},{8,24},{10,26},{12,28},{14,30},{16,0},... | collective-permute-start | bytes 417800 | tf_op jit(solution)/shard_map/ppermute | solution.py:938
  282.6 8.5 %copy-start.3 = (f32[4,208,512]{2,1,0:T(8,128)S(1)}, f32[4,208,512]{2,1,0:T(8,128)}, u32[]{:S(2)}) copy-start(f32[4,208,512]{2,1,0:T(8,128)} %get-tuple-element.117.rest_4_) | copy-start | bytes 5111812
  289.7 4.3 %collective-permute-start.18 = (bf16[136,256]{1,0:T(8,128)(2,1)S(1)}, bf16[136,256]{1,0:T(8,128)(2,1)S(1)}, u32[]{:S(2)}, u32[]{:S(2)}) collective-permute-start(bf16[136,256]{1,0:T(8,128)(2,1)S(1)} %slice_bitcast_fusion.5), channel_id=1, source_target_pairs={{0,1},{1,0},{2,3},{3,2},{4,5},{5,4},{6,7},{7,6},{8,9},{9,8},{10,11... | collective-permute-start | bytes 208904 | tf_op jit(solution)/shard_map/ppermute | solution.py:830
  291.5 21.2 %copy-start.6 = (bf16[4,200,512]{2,1,0:T(8,128)(2,1)}, bf16[4,200,512]{2,1,0:T(8,128)(2,1)S(1)}, u32[]{:S(2)}) copy-start(bf16[4,200,512]{2,1,0:T(8,128)(2,1)S(1)} %add_convert_fusion.1.refs_0_) | copy-start | bytes 2457604
  294.0 6.0 %collective-permute-start.19 = (bf16[136,256]{1,0:T(8,128)(2,1)S(1)}, bf16[136,256]{1,0:T(8,128)(2,1)S(1)}, u32[]{:S(2)}, u32[]{:S(2)}) collective-permute-start(bf16[136,256]{1,0:T(8,128)(2,1)S(1)} %fusion.1), channel_id=1, source_target_pairs={{0,16},{2,18},{4,20},{6,22},{8,24},{10,26},{12,28},{14,30},{16,0},... | collective-permute-start | bytes 208904 | tf_op jit(solution)/shard_map/ppermute | solution.py:938
  295.5 17.2 %collective-permute-start.22 = (bf16[4,200,512]{2,1,0:T(8,128)(2,1)S(1)}, bf16[4,200,512]{2,1,0:T(8,128)(2,1)S(1)}, u32[]{:S(2)}, u32[]{:S(2)}) collective-permute-start(bf16[4,200,512]{2,1,0:T(8,128)(2,1)S(1)} %add_convert_fusion.1.refs_0_), channel_id=1, source_target_pairs={{0,1},{1,0},{2,3},{3,2},{4,5},{5,4},{6,7},{7,6},{8,9},{9,8},{10,11... | collective-permute-start | bytes 2457608 | tf_op jit(solution)/shard_map/ppermute | solution.py:830
  300.0 5.1 %collective-permute-start.20 = (bf16[272,256]{1,0:T(8,128)(2,1)S(1)}, bf16[272,256]{1,0:T(8,128)(2,1)S(1)}, u32[]{:S(2)}, u32[]{:S(2)}) collective-permute-start(bf16[272,256]{1,0:T(8,128)(2,1)S(1)} %maximum_select_fusion.3), channel_id=1, source_target_pairs={{0,8},{2,10},{4,12},{6,14},{8,0},{10,2},{12,4},{14,6},{16,24},{18,... | collective-permute-start | bytes 417800 | tf_op jit(solution)/shard_map/ppermute | solution.py:938
  305.2 6.6 %collective-permute-start.21 = (bf16[544,256]{1,0:T(8,128)(2,1)S(1)}, bf16[544,256]{1,0:T(8,128)(2,1)S(1)}, u32[]{:S(2)}, u32[]{:S(2)}) collective-permute-start(bf16[544,256]{1,0:T(8,128)(2,1)S(1)} %maximum_select_fusion.2), channel_id=1, source_target_pairs={{0,4},{2,6},{4,0},{6,2},{8,12},{10,14},{12,8},{14,10},{16,20},{18,... | collective-permute-start | bytes 835592 | tf_op jit(solution)/shard_map/ppermute | solution.py:938
  312.7 0.9 copy-start.8
  312.7 4.0 %collective-permute-start.23 = (bf16[1088,256]{1,0:T(8,128)(2,1)S(1)}, bf16[1088,256]{1,0:T(8,128)(2,1)S(1)}, u32[]{:S(2)}, u32[]{:S(2)}) collective-permute-start(bf16[1088,256]{1,0:T(8,128)(2,1)S(1)} %maximum_select_fusion.1), channel_id=1, source_target_pairs={{0,2},{2,0},{4,6},{6,4},{8,10},{10,8},{12,14},{14,12},{16,18},{18,... | collective-permute-start | bytes 1671176 | tf_op jit(solution)/shard_map/ppermute | solution.py:938
